TPU v7x, 32 devices: a whole 2x2x4 slice. The times are simulated.
32 devices in a mesh: groups: 2 (over y), tiles: 4 (over z), split: 2 (over x), depth: 2 (over core).
Axes of the slice: x: 2, y: 2, z: 4, core: 2. Of those that a mesh axis runs over, the one named last changes fastest.
Arguments:
- tile_codes: bfloat16 [2048, 256, 256], P(('groups', 'tiles', 'split', 'depth')), parts along dimension 0, may hold values from -127 to 127, as said below
- tile_scale: float32 [2048], P(('groups', 'tiles', 'split', 'depth')), parts along dimension 0, may hold values from 9.375e-05 to 0.00078125
- tile_row: int32 [2048], P(('groups', 'tiles', 'split', 'depth')), parts along dimension 0, may hold values from 0 to 15
- tile_column: int32 [2048], P(('groups', 'tiles', 'split', 'depth')), parts along dimension 0, may hold values from 0 to 11, as said below
- send_index: int32 [32, 4, 2], P(('groups', 'tiles', 'split', 'depth')), parts along dimension 0, may hold values from 0 to 3
- model_start: float32 [128, 256], P(('groups', 'tiles', 'split', 'depth')), parts along dimension 0, may hold values from -6 to 6
- reg_weight: float32 [128, 256], P(('groups', 'tiles', 'split', 'depth')), parts along dimension 0, may hold values from 0.05 to 1
- observed: float32 [128, 256], P(('groups', 'tiles')), parts along dimension 0, may hold values from -6 to 6
- data_weight: float32 [128, 256], P(('groups', 'tiles')), parts along dimension 0, may hold values from 0.5 to 2
Outputs:
- model: float32 [128, 256], P(('groups', 'tiles', 'split', 'depth')), parts along dimension 0
- residual: float32 [128, 256], P(('groups', 'tiles', 'split', 'depth')), parts along dimension 0
There are 2 independent parts, one for each index of `groups`. A program takes and returns all parts, laid end to end along the dimension named above; each array names one. Nothing has to cross between parts.
Inputs may be any that keep to these rules, and one draw needn't show every extreme that they name: `tile_column`: below 4 a position names a block of the device itself; position c >= 4 names slot (c - 4) % 2 of what map tile (c - 4) // 2 sends from the device with the same split and depth index. Every position is named on every device. `send_index`: entry [d, t, j] is the block of device d's own 4 blocks placed in slot j of what d sends to map tile t. `tile_codes`: each value is an integer.
All inputs are finite; a program needn't handle non-finite values.
Results may differ from a plain program's by a relative error of at most 0.0088.
Values may be sent and summed in bfloat16 or wider, within the bound.
No kernel may reach another device: no remote copies, remote signals or barrier semaphores. Data moves between devices by JAX's collectives and lax.ppermute only.
A program may use at most 64 MiB of HBM per device.

v0:
```python
import functools

import jax
import jax.numpy as jnp
from jax import lax
from jax.experimental import pallas as pl
from jax.experimental.pallas import tpu as pltpu
from jax.sharding import PartitionSpec as P

HIGH = lax.Precision.HIGHEST
EXTRA = 8
LIMIT = 16 * 1024 * 1024
GROUP = 16
CHUNK = 16
F32 = jnp.float32
BF16 = jnp.bfloat16


def exchange(values, axes, size):
    parts = [values[0]] + [None] * (size - 1)
    for shift in range(size - 1, 0, -1):
        perm = [(i, i ^ shift) for i in range(size)]
        parts[shift] = lax.ppermute(values[shift], axes, perm)
    return parts


def by_shift(order, parts):
    return [part for _, part in sorted(zip(order, parts), key=lambda pair: pair[0])]


def total_rows(parts):
    total = parts[0][...]
    for part in parts[1:]:
        total = total + part[...]
    return total


def total_blocks(parts, blocks):
    count = len(parts)
    groups = []
    for group in range(count):
        total = None
        for shift in range(count):
            start = (group ^ shift) * blocks
            piece = parts[shift][start : start + blocks, :]
            total = piece if total is None else total + piece
        groups.append(total)
    return jnp.concatenate(groups, axis=0)


def extra_rows(parts, start):
    total = parts[0][start : start + EXTRA, :]
    for part in parts[1:]:
        total = total + part[start : start + EXTRA, :]
    return total


def whole(value):
    return jnp.sum(value, axis=(0, 1), keepdims=True)


def columns(value):
    return jnp.sum(value, axis=0, keepdims=True)


def pack_rows(rows, width):
    filled = list(rows)
    while len(filled) < EXTRA:
        filled.append(jnp.zeros((1, width), F32))
    return jnp.concatenate(filled, axis=0)


def products(tile_of, picked):
    tiles, width = picked.shape
    index = lax.broadcasted_iota(jnp.int32, (GROUP, width), 0)
    pieces = []
    for first in range(0, tiles, GROUP):
        rows = picked[first : first + GROUP, :]
        total = None
        for i in range(GROUP):
            tile, turn = tile_of(first + i)
            dims = (((1,), (1 if turn else 0,)), ((), ()))
            value = lax.dot_general(rows, tile, dims, preferred_element_type=F32)
            total = value if total is None else jnp.where(index == i, value, total)
        pieces.append(total)
    return jnp.concatenate(pieces, axis=0)


def kept_tiles(codes):
    return lambda k: (codes[k], False)


def turned_tiles(early, late, turn=False):
    count = early.shape[0]
    shift = 0 if turn else count
    return lambda k: (early[k], False) if k < count else (late[k - shift], turn)


def pick(table, values):
    return jnp.dot(table, values, preferred_element_type=F32).astype(BF16)


def gather(table, scale, terms):
    scaled = scale * terms
    upper = scaled.astype(BF16)
    lower = (scaled - upper.astype(F32)).astype(BF16)
    both = jnp.concatenate([upper, lower], axis=0)
    return jnp.dot(table, both, preferred_element_type=F32)


def tables(index, values, picks, pairs):
    tiles = index.shape[1]
    hits = lax.broadcasted_iota(jnp.int32, (values, tiles), 0) == index
    ones = jnp.where(hits, 1.0, 0.0)
    picks[...] = ones.T.astype(BF16)
    pairs[...] = jnp.concatenate([ones, ones], axis=1).astype(BF16)


def loading_kernel(far_codes, opening, far_scale, far_row, *refs):
    codes, early, rows_pick, rows_pair, wide_scale, scale, row, done, small = refs
    near = [
        pltpu.make_async_copy(far_scale, scale, small.at[0]),
        pltpu.make_async_copy(far_row, row, small.at[1]),
    ]
    for copy in near:
        copy.start()
    tiles, width = wide_scale.shape
    copies = []
    for chunk in range(tiles // CHUNK):
        span = pl.ds(chunk * CHUNK, CHUNK)
        copies.append(pltpu.make_async_copy(far_codes.at[span], codes.at[span], done.at[chunk]))
        copies[-1].start()
    for copy in near:
        copy.wait()
    tables(row[...], rows_pick.shape[1], rows_pick, rows_pair)
    square = (tiles, tiles)
    same = lax.broadcasted_iota(jnp.int32, square, 0) == lax.broadcasted_iota(jnp.int32, square, 1)
    wide_scale[...] = jnp.dot(
        jnp.where(same, scale[...], 0.0),
        jnp.ones((tiles, width), F32),
        precision=HIGH,
        preferred_element_type=F32,
    )
    for chunk, copy in enumerate(copies):
        copy.wait()
        for k in range(chunk * CHUNK, min((chunk + 1) * CHUNK, early.shape[0])):
            early[k] = codes[k].T


def turning_kernel(codes, part, late):
    first = codes.shape[0] - late.shape[0]
    for k in range(late.shape[0]):
        late[k] = codes[first + k].T


def opening_kernel(start, weight, named, out, sources, weights, names, done):
    copies = [
        pltpu.make_async_copy(start, sources, done.at[0]),
        pltpu.make_async_copy(weight, weights, done.at[1]),
        pltpu.make_async_copy(named, names, done.at[2]),
    ]
    for copy in copies:
        copy.start()
    blocks, width = sources.shape
    slots, count = names.shape
    rest = out.shape[0] - 2 * blocks
    out[2 * blocks :, :] = jnp.zeros((rest, width), F32)
    for copy in copies:
        copy.wait()
    out[:blocks, :] = sources[...]
    out[blocks : 2 * blocks, :] = weights[...]
    out[2 * blocks : 2 * blocks + slots, :count] = names[...].astype(F32)


def first_kernel(blocks, slots, order, *refs):
    codes, early, scale, rows_pair, column, place = refs[:6]
    count = len(order)
    parts = by_shift(order, refs[6 : 6 + count])
    out, source_pick, source_pair, start, weight = refs[6 + count :]
    width = out.shape[1]
    here = place[0]
    columns_of = column[...]
    source = jnp.where(columns_of < blocks, columns_of, 0)
    lane = lax.broadcasted_iota(jnp.int32, (1, width), 1)
    for shift in range(count):
        other = jnp.bitwise_xor(here, shift)
        for slot in range(slots):
            named = parts[shift][2 * blocks + slot : 2 * blocks + slot + 1, :]
            mine = jnp.where(lane == here, named, 0.0)
            block = jnp.sum(mine, axis=1, keepdims=True).astype(jnp.int32) + shift * blocks
            source = jnp.where(columns_of == blocks + other * slots + slot, block, source)
    tables(source, count * blocks, source_pick, source_pair)
    field = jnp.concatenate([part[:blocks, :] for part in parts], axis=0)
    start[...] = field
    weight[...] = jnp.concatenate([part[blocks : 2 * blocks, :] for part in parts], axis=0)

    terms = products(turned_tiles(early, codes, True), pick(source_pick[...], field.astype(BF16)))
    out[...] = gather(rows_pair[...], scale[...], terms)


def start_data_kernel(count, *refs):
    codes, rows_pick, source_pair, scale, observed, data_weight, late = refs[:7]
    parts = refs[7 : 7 + count]
    out = refs[7 + count]
    total = total_rows(parts)
    data = (data_weight[...] * (observed[...] - total)).astype(BF16)
    terms = products(kept_tiles(codes), pick(rows_pick[...], data))
    out[...] = gather(source_pair[...], scale[...], terms)


def start_residual_kernel(blocks, order, *refs):
    count = len(order)
    early, late, source_pick, rows_pair, scale, start, weight = refs[:7]
    parts = by_shift(order, refs[7 : 7 + count])
    out, residual = refs[7 + count :]
    weights = weight[...]
    value = total_blocks(parts, blocks) - weights * start[...]
    residual[...] = value
    terms = products(turned_tiles(early, late), pick(source_pick[...], value.astype(BF16)))
    data_rows = rows_pair.shape[0]
    out[:data_rows, :] = gather(rows_pair[...], scale[...], terms)
    out[data_rows:, :] = pack_rows(
        [columns(value * value), columns(value * weights * value)], value.shape[1]
    )


def image_data_kernel(count, *refs):
    codes, rows_pick, source_pair, scale, data_weight = refs[:5]
    parts = refs[5 : 5 + count]
    out, predicted, sums = refs[5 + count :]
    data_rows = data_weight.shape[0]
    whole_part = total_rows(parts)
    total = whole_part[:data_rows, :]
    predicted[...] = total
    sums[...] = whole_part[data_rows:, :]
    data = (data_weight[...] * (0.0 - total)).astype(BF16)
    terms = products(kept_tiles(codes), pick(rows_pick[...], data))
    cells = source_pair.shape[0]
    out[:cells, :] = gather(source_pair[...], scale[...], terms)
    out[cells:, :] = pack_rows([columns(total * data.astype(F32))], total.shape[1])


def residual_kernel(blocks, order, *refs):
    count = len(order)
    early, late, source_pick, rows_pair, scale, weight, direction, sums = refs[:8]
    parts = by_shift(order, refs[8 : 8 + count])
    out, residual, step = refs[8 + count :]
    cells = source_pick.shape[1]
    weights = weight[...]
    along = direction[...]
    image = weights * along - total_blocks(parts, blocks)
    curve = whole(sums[1:2, :]) - whole(extra_rows(parts, cells)[0:1, :])
    alpha = whole(sums[0:1, :]) / curve
    step[...] = jnp.broadcast_to(alpha, step.shape)
    value = residual_of(along, alpha, image)
    residual[...] = value
    terms = products(turned_tiles(early, late), pick(source_pick[...], value.astype(BF16)))
    data_rows = rows_pair.shape[0]
    out[:data_rows, :] = gather(rows_pair[...], scale[...], terms)
    weighted = value * weights
    out[data_rows:, :] = pack_rows(
        [columns(value * value), columns(weighted * value), columns(weighted * along)],
        value.shape[1],
    )


def residual_of(residual, alpha, image):
    return residual - alpha * image


def second_data_kernel(blocks, count, *refs):
    codes, rows_pick, source_pair, scale, data_weight, predicted, sums = refs[:7]
    parts = refs[7 : 7 + count]
    outs, scalars = refs[7 + count : -1], refs[-1]
    data_rows = data_weight.shape[0]
    whole_part = total_rows(parts)
    norm = whole(whole_part[data_rows : data_rows + 1, :])
    beta = norm / whole(sums[0:1, :])
    curve = whole(
        whole_part[data_rows + 1 : data_rows + 2, :]
        + 2.0 * beta * whole_part[data_rows + 2 : data_rows + 3, :]
        + beta * beta * sums[1:2, :]
    )
    total = whole_part[:data_rows, :] + beta * predicted[...]
    data = (data_weight[...] * (0.0 - total)).astype(BF16)
    terms = products(kept_tiles(codes), pick(rows_pick[...], data))
    cells = gather(source_pair[...], scale[...], terms)
    curved = columns(total * data.astype(F32))
    for group, out in enumerate(outs):
        out[:blocks, :] = cells[group * blocks : (group + 1) * blocks, :]
        out[blocks:, :] = jnp.broadcast_to(curved, (out.shape[0] - blocks, total.shape[1]))
    wide = (1, scalars.shape[1])
    scalars[...] = pack_rows(
        [jnp.broadcast_to(value, wide) for value in (norm, beta, curve)], scalars.shape[1]
    )


def last_kernel(blocks, count, *refs):
    weight, start, first, second, step, scalars = refs[:6]
    parts = refs[6 : 6 + count]
    model, residual = refs[6 + count :]
    norm = scalars[0:1, 0:1]
    beta = scalars[1:2, 0:1]
    curve = scalars[2:3, 0:1]
    along = first[:blocks, :]
    left = second[:blocks, :]
    direction = left + beta * along
    whole_part = total_rows(parts)
    image = weight[:blocks, :] * direction - whole_part[:blocks, :]
    alpha = norm / (curve - whole(whole_part[blocks : blocks + 1, :]))
    model[...] = start[:blocks, :] + step[0:1, 0:1] * along + alpha * direction
    residual[...] = left - alpha * image


def call(body, outs, *args, scratch=()):
    specs = []
    for arg in args:
        far = getattr(jax.typeof(arg), "memory_space", None) == pltpu.HBM
        space = pl.ANY if far else pltpu.SMEM if arg.ndim == 1 else pltpu.VMEM
        specs.append(pl.BlockSpec(memory_space=space))
    return pl.pallas_call(
        body,
        out_shape=[jax.ShapeDtypeStruct(shape, dtype) for shape, dtype in outs],
        in_specs=specs,
        out_specs=[pl.BlockSpec(memory_space=pltpu.VMEM)] * len(outs),
        scratch_shapes=list(scratch),
        compiler_params=pltpu.CompilerParams(vmem_limit_bytes=LIMIT),
    )(*args)


def shards(
    tile_codes,
    tile_scale,
    tile_row,
    tile_column,
    send_index,
    model_start,
    reg_weight,
    observed,
    data_weight,
):
    blocks, width = model_start.shape
    slots = send_index.shape[2]
    data_rows = observed.shape[0]
    tiles = tile_codes.shape[0]
    count = lax.axis_size("tiles")
    sharing = lax.axis_size(("split", "depth"))
    cells = count * blocks
    place = lax.axis_index("tiles").astype(jnp.int32).reshape(1)

    order = [0] + sorted(range(1, count), key=lambda shift: (shift != 1, -abs(2 * shift - count)))

    def across(values):
        parts = exchange(values, "tiles", count)
        return [parts[shift] for shift in order]

    def within(value):
        return exchange([value] * sharing, ("split", "depth"), sharing)

    named = jnp.transpose(send_index, (0, 2, 1)).reshape(slots, count)
    (opening,) = call(
        opening_kernel,
        [((2 * blocks + EXTRA, width), F32)],
        pltpu.with_memory_space_constraint(model_start, pltpu.HBM),
        pltpu.with_memory_space_constraint(reg_weight, pltpu.HBM),
        pltpu.with_memory_space_constraint(named, pltpu.HBM),
        scratch=[
            pltpu.VMEM((blocks, width), F32),
            pltpu.VMEM((blocks, width), F32),
            pltpu.VMEM((slots, count), jnp.int32),
            pltpu.SemaphoreType.DMA((3,)),
        ],
    )
    begin = across([opening] * count)
    codes, early, rows_pick, rows_pair, scale = call(
        loading_kernel,
        [
            (tile_codes.shape, BF16),
            ((tiles - CHUNK, width, width), BF16),
            ((tiles, data_rows), BF16),
            ((data_rows, 2 * tiles), BF16),
            ((tiles, width), F32),
        ],
        pltpu.with_memory_space_constraint(tile_codes, pltpu.HBM),
        opening,
        pltpu.with_memory_space_constraint(tile_scale.reshape(1, -1), pltpu.HBM),
        pltpu.with_memory_space_constraint(tile_row.reshape(1, -1), pltpu.HBM),
        scratch=[
            pltpu.VMEM((1, tiles), F32),
            pltpu.VMEM((1, tiles), jnp.int32),
            pltpu.SemaphoreType.DMA((tiles // CHUNK,)),
            pltpu.SemaphoreType.DMA((2,)),
        ],
    )
    part, source_pick, source_pair, start, weight = call(
        functools.partial(first_kernel, blocks, slots, order),
        [
            ((data_rows, width), F32),
            ((tiles, cells), BF16),
            ((cells, 2 * tiles), BF16),
            ((cells, width), F32),
            ((cells, width), F32),
        ],
        codes,
        early,
        scale,
        rows_pair,
        tile_column.reshape(1, -1),
        place,
        *begin,
    )
    parts = within(part)
    (late,) = call(turning_kernel, [((CHUNK, width, width), BF16)], codes, part)
    (part,) = call(
        functools.partial(start_data_kernel, sharing),
        [((cells, width), F32)],
        codes,
        rows_pick,
        source_pair,
        scale,
        observed,
        data_weight,
        late,
        *parts,
    )
    part, first = call(
        functools.partial(start_residual_kernel, blocks, order),
        [((data_rows + EXTRA, width), F32), ((cells, width), F32)],
        early,
        late,
        source_pick,
        rows_pair,
        scale,
        start,
        weight,
        *across([part] * count),
    )
    part, predicted, sums = call(
        functools.partial(image_data_kernel, sharing),
        [((cells + EXTRA, width), F32), ((data_rows, width), F32), ((EXTRA, width), F32)],
        codes,
        rows_pick,
        source_pair,
        scale,
        data_weight,
        *within(part),
    )
    part, second, step = call(
        functools.partial(residual_kernel, blocks, order),
        [((data_rows + EXTRA, width), F32), ((cells, width), F32), ((8, 128), F32)],
        early,
        late,
        source_pick,
        rows_pair,
        scale,
        weight,
        first,
        sums,
        *across([part] * count),
    )
    *part, scalars = call(
        functools.partial(second_data_kernel, blocks, sharing),
        [((blocks + 4, width), F32)] * count + [((EXTRA, width), F32)],
        codes,
        rows_pick,
        source_pair,
        scale,
        data_weight,
        predicted,
        sums,
        *within(part),
    )
    model, residual = call(
        functools.partial(last_kernel, blocks, count),
        [((blocks, width), F32), ((blocks, width), F32)],
        weight,
        start,
        first,
        second,
        step,
        scalars,
        *[part[0]] + across(part)[:0:-1],
    )
    return (model, residual)


def solution(mesh):
    both = P(("groups", "tiles", "split", "depth"))
    owned = P(("groups", "tiles", "split", "depth"), None)
    wide = P(("groups", "tiles", "split", "depth"), None, None)
    data = P(("groups", "tiles"), None)
    in_specs = (wide, both, both, both, wide, owned, owned, data, data)
    return jax.shard_map(
        shards, mesh=mesh, in_specs=in_specs, out_specs=(owned, owned), check_vma=False
    )
```

profile of v0, /device:TPU:0, one launch (start us, length us, event | category | flops | bytes accessed | tf_op | source)
XLA Modules:
  0.0 55.2 jit_solution(15645380540387465677)
XLA Ops:
  0.6 0.0 copy-start.2
  0.6 0.7 %shard_map.104.opening.refs_6_ = f32[16,256]{1,0:T(8,128)S(1)} custom-call(f32[4,256]{1,0:T(4,128)} %start.1, f32[4,256]{1,0:T(4,128)} %weight.1, s32[2,4]{1,0:T(2,128)} %bitcast.8), custom_call_target="tpu_custom_call" | custom-call | tf_op jit(solution)/shard_map/pallas_call | solution.py:321
  1.4 4.1 %collective-permute-start.2 = (f32[16,256]{1,0:T(8,128)S(1)}, f32[16,256]{1,0:T(8,128)S(1)}, u32[]{:S(2)}, u32[]{:S(2)}) collective-permute-start(f32[16,256]{1,0:T(8,128)S(1)} %shard_map.104.opening.refs_6_), channel_id=1, source_target_pairs={{0,8},{4,12},{8,0},{12,4},{1,9},{5,13},{9,1},{13,5},{2,10},{6,14},... | collective-permute-start | bytes 49160 | tf_op jit(solution)/shard_map/ppermute | solution.py:23
  5.5 1.3 %collective-permute-start.1 = (f32[16,256]{1,0:T(8,128)S(1)}, f32[16,256]{1,0:T(8,128)S(1)}, u32[]{:S(2)}, u32[]{:S(2)}) collective-permute-start(f32[16,256]{1,0:T(8,128)S(1)} %shard_map.104.opening.refs_6_), channel_id=1, source_target_pairs={{0,12},{4,8},{8,4},{12,0},{1,13},{5,9},{9,5},{13,1},{2,14},{6,10},... | collective-permute-start | bytes 49160 | tf_op jit(solution)/shard_map/ppermute | solution.py:23
  6.8 0.2 collective-permute-start
  7.1 4.6 %shard_map.105 = (bf16[64,256,256]{2,1,0:T(8,128)(2,1)S(1)}, bf16[48,256,256]{2,1,0:T(8,128)(2,1)S(1)}, bf16[64,16]{1,0:T(8,128)(2,1)S(1)}, bf16[16,128]{1,0:T(8,128)(2,1)S(1)}, f32[64,256]{1,0:T(8,128)S(1)}) custom-call(bf16[64,256,256]{2,1,0:T(8,128)(2,1)} %far_codes.1, f32[16,256]{1,0:T(8,128)S(1)} %shard_map.104.opening.refs_6_, f32[1,64]{1,0:T(1,128)} %bitcast.9, ...), custom_call_target="tpu_custom_call" | custom-call | tf_op jit(solution)/shard_map/pallas_call | solution.py:321
  11.6 0.0 collective-permute-done.2.refs_9_
  11.6 0.0 collective-permute-done.1.refs_8_
  11.7 0.0 collective-permute-done.refs_7_
  11.7 0.0 copy-done.2
  11.7 1.9 %shard_map.106 = (f32[16,256]{1,0:T(8,128)S(1)}, bf16[64,16]{1,0:T(8,128)(2,1)S(1)}, bf16[16,128]{1,0:T(8,128)(2,1)S(1)}, f32[16,256]{1,0:T(8,128)S(1)}, f32[16,256]{1,0:T(8,128)S(1)}) custom-call(bf16[64,256,256]{2,1,0:T(8,128)(2,1)S(1)} %get-tuple-element.25.refs_0_.codes, bf16[48,256,256]{2,1,0:T(8,128)(2,1)S(1)} %get-tuple-element.26.refs_1_.refs_0_, ...), custom_call_target="tpu_custom_call" | custom-call | tf_op jit(solution)/shard_map/pallas_call | solution.py:321
  13.5 0.0 copy-start
  13.5 0.0 copy-start.1
  13.5 0.4 collective-permute-start.5
  13.9 1.2 %collective-permute-start.4 = (f32[16,256]{1,0:T(8,128)S(1)}, f32[16,256]{1,0:T(8,128)S(1)}, u32[]{:S(2)}, u32[]{:S(2)}) collective-permute-start(f32[16,256]{1,0:T(8,128)S(1)} %get-tuple-element.31.part.refs_7_), channel_id=1, source_target_pairs={{0,2},{1,3},{2,0},{3,1},{4,6},{5,7},{6,4},{7,5},{8,10},{9,11},{10,... | collective-permute-start | bytes 49160 | tf_op jit(solution)/shard_map/ppermute | solution.py:23
  15.1 0.3 collective-permute-start.3
  15.4 0.6 %shard_map.107.refs_6_.refs_1_ = bf16[16,256,256]{2,1,0:T(8,128)(2,1)S(1)} custom-call(bf16[64,256,256]{2,1,0:T(8,128)(2,1)S(1)} %get-tuple-element.25.refs_0_.codes, f32[16,256]{1,0:T(8,128)S(1)} %get-tuple-element.31.part.refs_7_), custom_call_target="tpu_custom_call" | custom-call | tf_op jit(solution)/shard_map/pallas_call | solution.py:321
  16.0 0.8 %collective-permute-done.5.refs_10_ = f32[16,256]{1,0:T(8,128)S(1)} collective-permute-done((f32[16,256]{1,0:T(8,128)S(1)}, f32[16,256]{1,0:T(8,128)S(1)}, u32[]{:S(2)}, u32[]{:S(2)}) %collective-permute-start.5) | collective-permute-done | bytes 16416 | tf_op jit(solution)/shard_map/ppermute | solution.py:23
  16.9 0.8 %collective-permute-done.4.refs_9_ = f32[16,256]{1,0:T(8,128)S(1)} collective-permute-done((f32[16,256]{1,0:T(8,128)S(1)}, f32[16,256]{1,0:T(8,128)S(1)}, u32[]{:S(2)}, u32[]{:S(2)}) %collective-permute-start.4) | collective-permute-done | bytes 16416 | tf_op jit(solution)/shard_map/ppermute | solution.py:23
  17.7 0.0 collective-permute-done.3.refs_8_
  17.7 0.0 copy-done
  17.7 0.0 copy-done.1
  17.7 1.4 %shard_map.108.refs_7_ = f32[16,256]{1,0:T(8,128)S(1)} custom-call(bf16[64,256,256]{2,1,0:T(8,128)(2,1)S(1)} %get-tuple-element.25.refs_0_.codes, bf16[64,16]{1,0:T(8,128)(2,1)S(1)} %get-tuple-element.33.refs_1_, bf16[16,128]{1,0:T(8,128)(2,1)S(1)} %get-tuple-element.34.refs_2_, f32[64,256]{1,0:T(8,128)S(1)} %get-tuple-element.27.refs_2_.refs_3_.refs_4_, ...), custom_call_target="tpu_custom_call" | custom-call | tf_op jit(solution)/shard_map/pallas_call | solution.py:321
  19.1 2.6 %collective-permute-start.8 = (f32[16,256]{1,0:T(8,128)S(1)}, f32[16,256]{1,0:T(8,128)S(1)}, u32[]{:S(2)}, u32[]{:S(2)}) collective-permute-start(f32[16,256]{1,0:T(8,128)S(1)} %shard_map.108.refs_7_), channel_id=1, source_target_pairs={{0,8},{4,12},{8,0},{12,4},{1,9},{5,13},{9,1},{13,5},{2,10},{6,14},... | collective-permute-start | bytes 49160 | tf_op jit(solution)/shard_map/ppermute | solution.py:23
  21.7 1.4 %collective-permute-start.7 = (f32[16,256]{1,0:T(8,128)S(1)}, f32[16,256]{1,0:T(8,128)S(1)}, u32[]{:S(2)}, u32[]{:S(2)}) collective-permute-start(f32[16,256]{1,0:T(8,128)S(1)} %shard_map.108.refs_7_), channel_id=1, source_target_pairs={{0,12},{4,8},{8,4},{12,0},{1,13},{5,9},{9,5},{13,1},{2,14},{6,10},... | collective-permute-start | bytes 49160 | tf_op jit(solution)/shard_map/ppermute | solution.py:23
  23.0 0.0 collective-permute-start.6
  23.0 0.7 %collective-permute-done.8.refs_10_ = f32[16,256]{1,0:T(8,128)S(1)} collective-permute-done((f32[16,256]{1,0:T(8,128)S(1)}, f32[16,256]{1,0:T(8,128)S(1)}, u32[]{:S(2)}, u32[]{:S(2)}) %collective-permute-start.8) | collective-permute-done | bytes 16416 | tf_op jit(solution)/shard_map/ppermute | solution.py:23
  23.7 3.4 %collective-permute-done.7.refs_9_ = f32[16,256]{1,0:T(8,128)S(1)} collective-permute-done((f32[16,256]{1,0:T(8,128)S(1)}, f32[16,256]{1,0:T(8,128)S(1)}, u32[]{:S(2)}, u32[]{:S(2)}) %collective-permute-start.7) | collective-permute-done | bytes 16416 | tf_op jit(solution)/shard_map/ppermute | solution.py:23
  27.2 0.0 collective-permute-done.6.refs_8_
  27.2 1.4 %shard_map.109 = (f32[24,256]{1,0:T(8,128)S(1)}, f32[16,256]{1,0:T(8,128)S(1)}) custom-call(bf16[48,256,256]{2,1,0:T(8,128)(2,1)S(1)} %get-tuple-element.26.refs_1_.refs_0_, bf16[16,256,256]{2,1,0:T(8,128)(2,1)S(1)} %shard_map.107.refs_6_.refs_1_, bf16[64,16]{1,0:T(8,128)(2,1)S(1)} %get-tuple-element.32.refs_2_, ...), custom_call_target="tpu_custom_call" | custom-call | tf_op jit(solution)/shard_map/pallas_call | solution.py:321
  28.6 0.0 collective-permute-start.11
  28.6 1.5 %collective-permute-start.10 = (f32[24,256]{1,0:T(8,128)S(1)}, f32[24,256]{1,0:T(8,128)S(1)}, u32[]{:S(2)}, u32[]{:S(2)}) collective-permute-start(f32[24,256]{1,0:T(8,128)S(1)} %get-tuple-element.36.refs_5_), channel_id=1, source_target_pairs={{0,2},{1,3},{2,0},{3,1},{4,6},{5,7},{6,4},{7,5},{8,10},{9,11},{10,... | collective-permute-start | bytes 73736 | tf_op jit(solution)/shard_map/ppermute | solution.py:23
  30.1 0.4 collective-permute-start.9
  30.5 1.6 %collective-permute-done.11.refs_8_ = f32[24,256]{1,0:T(8,128)S(1)} collective-permute-done((f32[24,256]{1,0:T(8,128)S(1)}, f32[24,256]{1,0:T(8,128)S(1)}, u32[]{:S(2)}, u32[]{:S(2)}) %collective-permute-start.11) | collective-permute-done | bytes 24608 | tf_op jit(solution)/shard_map/ppermute | solution.py:23
  32.1 0.4 collective-permute-done.10.refs_7_
  32.5 0.0 collective-permute-done.9.refs_6_
  32.5 1.4 %shard_map.110 = (f32[24,256]{1,0:T(8,128)S(1)}, f32[16,256]{1,0:T(8,128)S(1)}, f32[8,256]{1,0:T(8,128)S(1)}) custom-call(bf16[64,256,256]{2,1,0:T(8,128)(2,1)S(1)} %get-tuple-element.25.refs_0_.codes, bf16[64,16]{1,0:T(8,128)(2,1)S(1)} %get-tuple-element.33.refs_1_, bf16[16,128]{1,0:T(8,128)(2,1)S(1)} %get-tuple-element.34.refs_2_, ...), custom_call_target="tpu_custom_call" | custom-call | tf_op jit(solution)/shard_map/pallas_call | solution.py:321
  33.9 0.8 %collective-permute-start.14 = (f32[24,256]{1,0:T(8,128)S(1)}, f32[24,256]{1,0:T(8,128)S(1)}, u32[]{:S(2)}, u32[]{:S(2)}) collective-permute-start(f32[24,256]{1,0:T(8,128)S(1)} %get-tuple-element.38.refs_8_), channel_id=1, source_target_pairs={{0,8},{4,12},{8,0},{12,4},{1,9},{5,13},{9,1},{13,5},{2,10},{6,14},... | collective-permute-start | bytes 73736 | tf_op jit(solution)/shard_map/ppermute | solution.py:23
  34.7 1.4 %collective-permute-start.13 = (f32[24,256]{1,0:T(8,128)S(1)}, f32[24,256]{1,0:T(8,128)S(1)}, u32[]{:S(2)}, u32[]{:S(2)}) collective-permute-start(f32[24,256]{1,0:T(8,128)S(1)} %get-tuple-element.38.refs_8_), channel_id=1, source_target_pairs={{0,12},{4,8},{8,4},{12,0},{1,13},{5,9},{9,5},{13,1},{2,14},{6,10},... | collective-permute-start | bytes 73736 | tf_op jit(solution)/shard_map/ppermute | solution.py:23
  36.0 1.4 %collective-permute-start.12 = (f32[24,256]{1,0:T(8,128)S(1)}, f32[24,256]{1,0:T(8,128)S(1)}, u32[]{:S(2)}, u32[]{:S(2)}) collective-permute-start(f32[24,256]{1,0:T(8,128)S(1)} %get-tuple-element.38.refs_8_), channel_id=1, source_target_pairs={{0,4},{4,0},{8,12},{12,8},{1,5},{5,1},{9,13},{13,9},{2,6},{6,2},{1... | collective-permute-start | bytes 73736 | tf_op jit(solution)/shard_map/ppermute | solution.py:23
  37.4 1.3 %collective-permute-done.14.refs_11_ = f32[24,256]{1,0:T(8,128)S(1)} collective-permute-done((f32[24,256]{1,0:T(8,128)S(1)}, f32[24,256]{1,0:T(8,128)S(1)}, u32[]{:S(2)}, u32[]{:S(2)}) %collective-permute-start.14) | collective-permute-done | bytes 24608 | tf_op jit(solution)/shard_map/ppermute | solution.py:23
  38.7 1.6 %collective-permute-done.13.refs_10_ = f32[24,256]{1,0:T(8,128)S(1)} collective-permute-done((f32[24,256]{1,0:T(8,128)S(1)}, f32[24,256]{1,0:T(8,128)S(1)}, u32[]{:S(2)}, u32[]{:S(2)}) %collective-permute-start.13) | collective-permute-done | bytes 24608 | tf_op jit(solution)/shard_map/ppermute | solution.py:23
  40.4 0.0 collective-permute-done.12.refs_9_
  40.4 1.5 %shard_map.111 = (f32[24,256]{1,0:T(8,128)S(1)}, f32[16,256]{1,0:T(8,128)S(1)}, f32[8,128]{1,0:T(8,128)S(1)}) custom-call(bf16[48,256,256]{2,1,0:T(8,128)(2,1)S(1)} %get-tuple-element.26.refs_1_.refs_0_, bf16[16,256,256]{2,1,0:T(8,128)(2,1)S(1)} %shard_map.107.refs_6_.refs_1_, bf16[64,16]{1,0:T(8,128)(2,1)S(1)} %get-tuple-element.32.refs_2_, ...), custom_call_target="tpu_custom_call" | custom-call | tf_op jit(solution)/shard_map/pallas_call | solution.py:321
  41.9 0.0 collective-permute-start.17
  41.9 1.5 %collective-permute-start.16 = (f32[24,256]{1,0:T(8,128)S(1)}, f32[24,256]{1,0:T(8,128)S(1)}, u32[]{:S(2)}, u32[]{:S(2)}) collective-permute-start(f32[24,256]{1,0:T(8,128)S(1)} %get-tuple-element.42.refs_7_), channel_id=1, source_target_pairs={{0,2},{1,3},{2,0},{3,1},{4,6},{5,7},{6,4},{7,5},{8,10},{9,11},{10,... | collective-permute-start | bytes 73736 | tf_op jit(solution)/shard_map/ppermute | solution.py:23
  43.4 0.4 collective-permute-start.15
  43.8 1.6 %collective-permute-done.17.refs_10_ = f32[24,256]{1,0:T(8,128)S(1)} collective-permute-done((f32[24,256]{1,0:T(8,128)S(1)}, f32[24,256]{1,0:T(8,128)S(1)}, u32[]{:S(2)}, u32[]{:S(2)}) %collective-permute-start.17) | collective-permute-done | bytes 24608 | tf_op jit(solution)/shard_map/ppermute | solution.py:23
  45.4 0.4 collective-permute-done.16.refs_9_
  45.8 0.0 collective-permute-done.15.refs_8_
  45.8 1.6 %shard_map.112 = (f32[8,256]{1,0:T(8,128)S(1)}, f32[8,256]{1,0:T(8,128)S(1)}, f32[8,256]{1,0:T(8,128)S(1)}, f32[8,256]{1,0:T(8,128)S(1)}, f32[8,256]{1,0:T(8,128)S(1)}) custom-call(bf16[64,256,256]{2,1,0:T(8,128)(2,1)S(1)} %get-tuple-element.25.refs_0_.codes, bf16[64,16]{1,0:T(8,128)(2,1)S(1)} %get-tuple-element.33.refs_1_, ...), custom_call_target="tpu_custom_call" | custom-call | tf_op jit(solution)/shard_map/pallas_call | solution.py:321
  47.3 1.5 %collective-permute-start.18 = (f32[8,256]{1,0:T(8,128)S(1)}, f32[8,256]{1,0:T(8,128)S(1)}, u32[]{:S(2)}, u32[]{:S(2)}) collective-permute-start(f32[8,256]{1,0:T(8,128)S(1)} %get-tuple-element.45), channel_id=1, source_target_pairs={{0,8},{4,12},{8,0},{12,4},{1,9},{5,13},{9,1},{13,5},{2,10},{6,14},... | collective-permute-start | bytes 24584 | tf_op jit(solution)/shard_map/ppermute | solution.py:23
  48.8 1.8 %collective-permute-start.19 = (f32[8,256]{1,0:T(8,128)S(1)}, f32[8,256]{1,0:T(8,128)S(1)}, u32[]{:S(2)}, u32[]{:S(2)}) collective-permute-start(f32[8,256]{1,0:T(8,128)S(1)} %get-tuple-element.46), channel_id=1, source_target_pairs={{0,12},{4,8},{8,4},{12,0},{1,13},{5,9},{9,5},{13,1},{2,14},{6,10},... | collective-permute-start | bytes 24584 | tf_op jit(solution)/shard_map/ppermute | solution.py:23
  50.6 0.2 collective-permute-start.20
  50.8 1.1 %collective-permute-done.18.refs_7_ = f32[8,256]{1,0:T(8,128)S(1)} collective-permute-done((f32[8,256]{1,0:T(8,128)S(1)}, f32[8,256]{1,0:T(8,128)S(1)}, u32[]{:S(2)}, u32[]{:S(2)}) %collective-permute-start.18) | collective-permute-done | bytes 8224 | tf_op jit(solution)/shard_map/ppermute | solution.py:23
  51.9 2.4 %collective-permute-done.19.refs_8_ = f32[8,256]{1,0:T(8,128)S(1)} collective-permute-done((f32[8,256]{1,0:T(8,128)S(1)}, f32[8,256]{1,0:T(8,128)S(1)}, u32[]{:S(2)}, u32[]{:S(2)}) %collective-permute-start.19) | collective-permute-done | bytes 8224 | tf_op jit(solution)/shard_map/ppermute | solution.py:23
  54.3 0.1 collective-permute-done.20.refs_9_
  54.4 0.8 %shard_map.113 = (f32[4,256]{1,0:T(4,128)}, f32[4,256]{1,0:T(4,128)}) custom-call(f32[16,256]{1,0:T(8,128)S(1)} %get-tuple-element.29.refs_6_.refs_5_.refs_0_, f32[16,256]{1,0:T(8,128)S(1)} %get-tuple-element.30.refs_5_.refs_1_, f32[16,256]{1,0:T(8,128)S(1)} %get-tuple-element.35.refs_6_.refs_2_, f32[16,256]{1,0:T(8,128)S(1)} %get-tuple-element.39.refs_3_, ...), custom_call_target="tpu_custom_call" | custom-call | tf_op jit(solution)/shard_map/pallas_call | solution.py:321
Async XLA Ops:
  0.6 11.0 %copy-start.2 = (s32[64]{0:T(128)S(1)}, s32[64]{0:T(128)}, u32[]{:S(2)}) copy-start(s32[64]{0:T(128)} %param.12) | copy-start | bytes 772
  1.4 10.2 %collective-permute-start.2 = (f32[16,256]{1,0:T(8,128)S(1)}, f32[16,256]{1,0:T(8,128)S(1)}, u32[]{:S(2)}, u32[]{:S(2)}) collective-permute-start(f32[16,256]{1,0:T(8,128)S(1)} %shard_map.104.opening.refs_6_), channel_id=1, source_target_pairs={{0,8},{4,12},{8,0},{12,4},{1,9},{5,13},{9,1},{13,5},{2,10},{6,14},... | collective-permute-start | bytes 49160 | tf_op jit(solution)/shard_map/ppermute | solution.py:23
  5.5 6.2 %collective-permute-start.1 = (f32[16,256]{1,0:T(8,128)S(1)}, f32[16,256]{1,0:T(8,128)S(1)}, u32[]{:S(2)}, u32[]{:S(2)}) collective-permute-start(f32[16,256]{1,0:T(8,128)S(1)} %shard_map.104.opening.refs_6_), channel_id=1, source_target_pairs={{0,12},{4,8},{8,4},{12,0},{1,13},{5,9},{9,5},{13,1},{2,14},{6,10},... | collective-permute-start | bytes 49160 | tf_op jit(solution)/shard_map/ppermute | solution.py:23
  6.8 4.8 %collective-permute-start = (f32[16,256]{1,0:T(8,128)S(1)}, f32[16,256]{1,0:T(8,128)S(1)}, u32[]{:S(2)}, u32[]{:S(2)}) collective-permute-start(f32[16,256]{1,0:T(8,128)S(1)} %shard_map.104.opening.refs_6_), channel_id=1, source_target_pairs={{0,4},{4,0},{8,12},{12,8},{1,5},{5,1},{9,13},{13,9},{2,6},{6,2},{1... | collective-permute-start | bytes 49160 | tf_op jit(solution)/shard_map/ppermute | solution.py:23
  13.5 4.1 %copy-start = (f32[16,256]{1,0:T(8,128)S(1)}, f32[16,256]{1,0:T(8,128)}, u32[]{:S(2)}) copy-start(f32[16,256]{1,0:T(8,128)} %refs_4_.5) | copy-start | bytes 49156
  13.5 4.1 %copy-start.1 = (f32[16,256]{1,0:T(8,128)S(1)}, f32[16,256]{1,0:T(8,128)}, u32[]{:S(2)}) copy-start(f32[16,256]{1,0:T(8,128)} %refs_4_.3) | copy-start | bytes 49156
  13.5 3.3 %collective-permute-start.5 = (f32[16,256]{1,0:T(8,128)S(1)}, f32[16,256]{1,0:T(8,128)S(1)}, u32[]{:S(2)}, u32[]{:S(2)}) collective-permute-start(f32[16,256]{1,0:T(8,128)S(1)} %get-tuple-element.31.part.refs_7_), channel_id=1, source_target_pairs={{0,3},{1,2},{2,1},{3,0},{4,7},{5,6},{6,5},{7,4},{8,11},{9,10},{10,... | collective-permute-start | bytes 49160 | tf_op jit(solution)/shard_map/ppermute | solution.py:23
  13.9 3.7 %collective-permute-start.4 = (f32[16,256]{1,0:T(8,128)S(1)}, f32[16,256]{1,0:T(8,128)S(1)}, u32[]{:S(2)}, u32[]{:S(2)}) collective-permute-start(f32[16,256]{1,0:T(8,128)S(1)} %get-tuple-element.31.part.refs_7_), channel_id=1, source_target_pairs={{0,2},{1,3},{2,0},{3,1},{4,6},{5,7},{6,4},{7,5},{8,10},{9,11},{10,... | collective-permute-start | bytes 49160 | tf_op jit(solution)/shard_map/ppermute | solution.py:23
  15.1 2.6 %collective-permute-start.3 = (f32[16,256]{1,0:T(8,128)S(1)}, f32[16,256]{1,0:T(8,128)S(1)}, u32[]{:S(2)}, u32[]{:S(2)}) collective-permute-start(f32[16,256]{1,0:T(8,128)S(1)} %get-tuple-element.31.part.refs_7_), channel_id=1, source_target_pairs={{0,1},{1,0},{2,3},{3,2},{4,5},{5,4},{6,7},{7,6},{8,9},{9,8},{10,11... | collective-permute-start | bytes 49160 | tf_op jit(solution)/shard_map/ppermute | solution.py:23
  19.1 4.6 %collective-permute-start.8 = (f32[16,256]{1,0:T(8,128)S(1)}, f32[16,256]{1,0:T(8,128)S(1)}, u32[]{:S(2)}, u32[]{:S(2)}) collective-permute-start(f32[16,256]{1,0:T(8,128)S(1)} %shard_map.108.refs_7_), channel_id=1, source_target_pairs={{0,8},{4,12},{8,0},{12,4},{1,9},{5,13},{9,1},{13,5},{2,10},{6,14},... | collective-permute-start | bytes 49160 | tf_op jit(solution)/shard_map/ppermute | solution.py:23
  21.7 5.5 %collective-permute-start.7 = (f32[16,256]{1,0:T(8,128)S(1)}, f32[16,256]{1,0:T(8,128)S(1)}, u32[]{:S(2)}, u32[]{:S(2)}) collective-permute-start(f32[16,256]{1,0:T(8,128)S(1)} %shard_map.108.refs_7_), channel_id=1, source_target_pairs={{0,12},{4,8},{8,4},{12,0},{1,13},{5,9},{9,5},{13,1},{2,14},{6,10},... | collective-permute-start | bytes 49160 | tf_op jit(solution)/shard_map/ppermute | solution.py:23
  23.0 4.2 %collective-permute-start.6 = (f32[16,256]{1,0:T(8,128)S(1)}, f32[16,256]{1,0:T(8,128)S(1)}, u32[]{:S(2)}, u32[]{:S(2)}) collective-permute-start(f32[16,256]{1,0:T(8,128)S(1)} %shard_map.108.refs_7_), channel_id=1, source_target_pairs={{0,4},{4,0},{8,12},{12,8},{1,5},{5,1},{9,13},{13,9},{2,6},{6,2},{1... | collective-permute-start | bytes 49160 | tf_op jit(solution)/shard_map/ppermute | solution.py:23
  28.6 3.5 %collective-permute-start.11 = (f32[24,256]{1,0:T(8,128)S(1)}, f32[24,256]{1,0:T(8,128)S(1)}, u32[]{:S(2)}, u32[]{:S(2)}) collective-permute-start(f32[24,256]{1,0:T(8,128)S(1)} %get-tuple-element.36.refs_5_), channel_id=1, source_target_pairs={{0,3},{1,2},{2,1},{3,0},{4,7},{5,6},{6,5},{7,4},{8,11},{9,10},{10,... | collective-permute-start | bytes 73736 | tf_op jit(solution)/shard_map/ppermute | solution.py:23
  28.6 3.9 %collective-permute-start.10 = (f32[24,256]{1,0:T(8,128)S(1)}, f32[24,256]{1,0:T(8,128)S(1)}, u32[]{:S(2)}, u32[]{:S(2)}) collective-permute-start(f32[24,256]{1,0:T(8,128)S(1)} %get-tuple-element.36.refs_5_), channel_id=1, source_target_pairs={{0,2},{1,3},{2,0},{3,1},{4,6},{5,7},{6,4},{7,5},{8,10},{9,11},{10,... | collective-permute-start | bytes 73736 | tf_op jit(solution)/shard_map/ppermute | solution.py:23
  30.1 2.4 %collective-permute-start.9 = (f32[24,256]{1,0:T(8,128)S(1)}, f32[24,256]{1,0:T(8,128)S(1)}, u32[]{:S(2)}, u32[]{:S(2)}) collective-permute-start(f32[24,256]{1,0:T(8,128)S(1)} %get-tuple-element.36.refs_5_), channel_id=1, source_target_pairs={{0,1},{1,0},{2,3},{3,2},{4,5},{5,4},{6,7},{7,6},{8,9},{9,8},{10,11... | collective-permute-start | bytes 73736 | tf_op jit(solution)/shard_map/ppermute | solution.py:23
  33.9 4.8 %collective-permute-start.14 = (f32[24,256]{1,0:T(8,128)S(1)}, f32[24,256]{1,0:T(8,128)S(1)}, u32[]{:S(2)}, u32[]{:S(2)}) collective-permute-start(f32[24,256]{1,0:T(8,128)S(1)} %get-tuple-element.38.refs_8_), channel_id=1, source_target_pairs={{0,8},{4,12},{8,0},{12,4},{1,9},{5,13},{9,1},{13,5},{2,10},{6,14},... | collective-permute-start | bytes 73736 | tf_op jit(solution)/shard_map/ppermute | solution.py:23
  34.7 5.7 %collective-permute-start.13 = (f32[24,256]{1,0:T(8,128)S(1)}, f32[24,256]{1,0:T(8,128)S(1)}, u32[]{:S(2)}, u32[]{:S(2)}) collective-permute-start(f32[24,256]{1,0:T(8,128)S(1)} %get-tuple-element.38.refs_8_), channel_id=1, source_target_pairs={{0,12},{4,8},{8,4},{12,0},{1,13},{5,9},{9,5},{13,1},{2,14},{6,10},... | collective-permute-start | bytes 73736 | tf_op jit(solution)/shard_map/ppermute | solution.py:23
  36.0 4.3 %collective-permute-start.12 = (f32[24,256]{1,0:T(8,128)S(1)}, f32[24,256]{1,0:T(8,128)S(1)}, u32[]{:S(2)}, u32[]{:S(2)}) collective-permute-start(f32[24,256]{1,0:T(8,128)S(1)} %get-tuple-element.38.refs_8_), channel_id=1, source_target_pairs={{0,4},{4,0},{8,12},{12,8},{1,5},{5,1},{9,13},{13,9},{2,6},{6,2},{1... | collective-permute-start | bytes 73736 | tf_op jit(solution)/shard_map/ppermute | solution.py:23
  41.9 3.5 %collective-permute-start.17 = (f32[24,256]{1,0:T(8,128)S(1)}, f32[24,256]{1,0:T(8,128)S(1)}, u32[]{:S(2)}, u32[]{:S(2)}) collective-permute-start(f32[24,256]{1,0:T(8,128)S(1)} %get-tuple-element.42.refs_7_), channel_id=1, source_target_pairs={{0,3},{1,2},{2,1},{3,0},{4,7},{5,6},{6,5},{7,4},{8,11},{9,10},{10,... | collective-permute-start | bytes 73736 | tf_op jit(solution)/shard_map/ppermute | solution.py:23
  41.9 3.9 %collective-permute-start.16 = (f32[24,256]{1,0:T(8,128)S(1)}, f32[24,256]{1,0:T(8,128)S(1)}, u32[]{:S(2)}, u32[]{:S(2)}) collective-permute-start(f32[24,256]{1,0:T(8,128)S(1)} %get-tuple-element.42.refs_7_), channel_id=1, source_target_pairs={{0,2},{1,3},{2,0},{3,1},{4,6},{5,7},{6,4},{7,5},{8,10},{9,11},{10,... | collective-permute-start | bytes 73736 | tf_op jit(solution)/shard_map/ppermute | solution.py:23
  43.4 2.4 %collective-permute-start.15 = (f32[24,256]{1,0:T(8,128)S(1)}, f32[24,256]{1,0:T(8,128)S(1)}, u32[]{:S(2)}, u32[]{:S(2)}) collective-permute-start(f32[24,256]{1,0:T(8,128)S(1)} %get-tuple-element.42.refs_7_), channel_id=1, source_target_pairs={{0,1},{1,0},{2,3},{3,2},{4,5},{5,4},{6,7},{7,6},{8,9},{9,8},{10,11... | collective-permute-start | bytes 73736 | tf_op jit(solution)/shard_map/ppermute | solution.py:23
  47.3 4.6 %collective-permute-start.18 = (f32[8,256]{1,0:T(8,128)S(1)}, f32[8,256]{1,0:T(8,128)S(1)}, u32[]{:S(2)}, u32[]{:S(2)}) collective-permute-start(f32[8,256]{1,0:T(8,128)S(1)} %get-tuple-element.45), channel_id=1, source_target_pairs={{0,8},{4,12},{8,0},{12,4},{1,9},{5,13},{9,1},{13,5},{2,10},{6,14},... | collective-permute-start | bytes 24584 | tf_op jit(solution)/shard_map/ppermute | solution.py:23
  48.8 5.5 %collective-permute-start.19 = (f32[8,256]{1,0:T(8,128)S(1)}, f32[8,256]{1,0:T(8,128)S(1)}, u32[]{:S(2)}, u32[]{:S(2)}) collective-permute-start(f32[8,256]{1,0:T(8,128)S(1)} %get-tuple-element.46), channel_id=1, source_target_pairs={{0,12},{4,8},{8,4},{12,0},{1,13},{5,9},{9,5},{13,1},{2,14},{6,10},... | collective-permute-start | bytes 24584 | tf_op jit(solution)/shard_map/ppermute | solution.py:23
  50.6 3.7 %collective-permute-start.20 = (f32[8,256]{1,0:T(8,128)S(1)}, f32[8,256]{1,0:T(8,128)S(1)}, u32[]{:S(2)}, u32[]{:S(2)}) collective-permute-start(f32[8,256]{1,0:T(8,128)S(1)} %get-tuple-element.47), channel_id=1, source_target_pairs={{0,4},{4,0},{8,12},{12,8},{1,5},{5,1},{9,13},{13,9},{2,6},{6,2},{1... | collective-permute-start | bytes 24584 | tf_op jit(solution)/shard_map/ppermute | solution.py:23
where the time goes:
time: 55.4 us; the launch traced here: 55.2 us
  starting transfers between devices  22.2 us (40%)
  waiting for transfers between devices  16.3 us (29%)
  Pallas kernels  15.9 us (29%)
  between operations  0.72 us (1%)
    ppermute x21, starting transfers between devices, exchange(): parts[shift] = lax.ppermute(values[shift], axes, perm)  22.2 us
    ppermute x21, waiting for transfers between devices, exchange(): parts[shift] = lax.ppermute(values[shift], axes, perm)  16.3 us
    pallas_call x10, Pallas kernels, call(): pl.pallas_call(body, out_shape=[jax.ShapeDtypeStruct(shape, dtype) for sh...  15.9 us
  transfers between devices with their start and end apart: 21, of which 13 were waited for; matrix products, arithmetic and copies ran while one was open for 0% of the time, Pallas kernels for 9%

commit v1 on v0

--- a/solution.py
+++ b/solution.py
@@ -12,6 +12,7 @@
 LIMIT = 16 * 1024 * 1024
 GROUP = 16
 CHUNK = 16
+FLIGHT = 2
 F32 = jnp.float32
 BF16 = jnp.bfloat16
 
@@ -129,7 +130,8 @@
     for chunk in range(tiles // CHUNK):
         span = pl.ds(chunk * CHUNK, CHUNK)
         copies.append(pltpu.make_async_copy(far_codes.at[span], codes.at[span], done.at[chunk]))
-        copies[-1].start()
+    for copy in copies[:FLIGHT]:
+        copy.start()
     for copy in near:
         copy.wait()
     tables(row[...], rows_pick.shape[1], rows_pick, rows_pair)
@@ -143,6 +145,8 @@
     )
     for chunk, copy in enumerate(copies):
         copy.wait()
+        if chunk + FLIGHT < len(copies):
+            copies[chunk + FLIGHT].start()
         for k in range(chunk * CHUNK, min((chunk + 1) * CHUNK, early.shape[0])):
             early[k] = codes[k].T
 
@@ -346,6 +350,7 @@
     count = lax.axis_size("tiles")
     sharing = lax.axis_size(("split", "depth"))
     cells = count * blocks
+    late_tiles = tiles // 2
     place = lax.axis_index("tiles").astype(jnp.int32).reshape(1)
 
     order = [0] + sorted(range(1, count), key=lambda shift: (shift != 1, -abs(2 * shift - count)))
@@ -376,7 +381,7 @@
         loading_kernel,
         [
             (tile_codes.shape, BF16),
-            ((tiles - CHUNK, width, width), BF16),
+            ((tiles - late_tiles, width, width), BF16),
             ((tiles, data_rows), BF16),
             ((data_rows, 2 * tiles), BF16),
             ((tiles, width), F32),
@@ -410,7 +415,7 @@
         *begin,
     )
     parts = within(part)
-    (late,) = call(turning_kernel, [((CHUNK, width, width), BF16)], codes, part)
+    (late,) = call(turning_kernel, [((late_tiles, width, width), BF16)], codes, part)
     (part,) = call(
         functools.partial(start_data_kernel, sharing),
         [((cells, width), F32)],

time: 55.4 us -> 55.1 us (level)
  no operation moved by 1% of the time
where the time goes in v1:
time: 55.1 us; the launch traced here: 54.9 us
  starting transfers between devices  22.2 us (40%)
  Pallas kernels  16.2 us (29%)
  waiting for transfers between devices  15.8 us (29%)
  between operations  0.72 us (1%)
    ppermute x21, starting transfers between devices, exchange(): parts[shift] = lax.ppermute(values[shift], axes, perm)  22.2 us
    pallas_call x10, Pallas kernels, call(): pl.pallas_call(body, out_shape=[jax.ShapeDtypeStruct(shape, dtype) for sh...  16.2 us
    ppermute x21, waiting for transfers between devices, exchange(): parts[shift] = lax.ppermute(values[shift], axes, perm)  15.8 us
  transfers between devices with their start and end apart: 21, of which 13 were waited for; matrix products, arithmetic and copies ran while one was open for 0% of the time, Pallas kernels for 9%

profile of v1, /device:TPU:0, one launch (start us, length us, event | category | flops | bytes accessed | tf_op | source)
XLA Modules:
  0.0 54.9 jit_solution(17610483246787258497)
XLA Ops:
  0.6 0.0 copy-start.2
  0.6 0.7 %shard_map.104.opening.refs_6_ = f32[16,256]{1,0:T(8,128)S(1)} custom-call(f32[4,256]{1,0:T(4,128)} %start.1, f32[4,256]{1,0:T(4,128)} %weight.1, s32[2,4]{1,0:T(2,128)} %bitcast.8), custom_call_target="tpu_custom_call" | custom-call | tf_op jit(solution)/shard_map/pallas_call | solution.py:325
  1.4 4.1 %collective-permute-start.2 = (f32[16,256]{1,0:T(8,128)S(1)}, f32[16,256]{1,0:T(8,128)S(1)}, u32[]{:S(2)}, u32[]{:S(2)}) collective-permute-start(f32[16,256]{1,0:T(8,128)S(1)} %shard_map.104.opening.refs_6_), channel_id=1, source_target_pairs={{0,8},{4,12},{8,0},{12,4},{1,9},{5,13},{9,1},{13,5},{2,10},{6,14},... | collective-permute-start | bytes 49160 | tf_op jit(solution)/shard_map/ppermute | solution.py:24
  5.5 1.3 %collective-permute-start.1 = (f32[16,256]{1,0:T(8,128)S(1)}, f32[16,256]{1,0:T(8,128)S(1)}, u32[]{:S(2)}, u32[]{:S(2)}) collective-permute-start(f32[16,256]{1,0:T(8,128)S(1)} %shard_map.104.opening.refs_6_), channel_id=1, source_target_pairs={{0,12},{4,8},{8,4},{12,0},{1,13},{5,9},{9,5},{13,1},{2,14},{6,10},... | collective-permute-start | bytes 49160 | tf_op jit(solution)/shard_map/ppermute | solution.py:24
  6.8 0.2 collective-permute-start
  7.1 4.0 %shard_map.105 = (bf16[64,256,256]{2,1,0:T(8,128)(2,1)S(1)}, bf16[32,256,256]{2,1,0:T(8,128)(2,1)S(1)}, bf16[64,16]{1,0:T(8,128)(2,1)S(1)}, bf16[16,128]{1,0:T(8,128)(2,1)S(1)}, f32[64,256]{1,0:T(8,128)S(1)}) custom-call(bf16[64,256,256]{2,1,0:T(8,128)(2,1)} %far_codes.1, f32[16,256]{1,0:T(8,128)S(1)} %shard_map.104.opening.refs_6_, f32[1,64]{1,0:T(1,128)} %bitcast.9, ...), custom_call_target="tpu_custom_call" | custom-call | tf_op jit(solution)/shard_map/pallas_call | solution.py:325
  11.1 0.0 collective-permute-done.2.refs_9_
  11.1 0.0 collective-permute-done.1.refs_8_
  11.1 0.0 collective-permute-done.refs_7_
  11.1 0.0 copy-done.2
  11.1 2.1 %shard_map.106 = (f32[16,256]{1,0:T(8,128)S(1)}, bf16[64,16]{1,0:T(8,128)(2,1)S(1)}, bf16[16,128]{1,0:T(8,128)(2,1)S(1)}, f32[16,256]{1,0:T(8,128)S(1)}, f32[16,256]{1,0:T(8,128)S(1)}) custom-call(bf16[64,256,256]{2,1,0:T(8,128)(2,1)S(1)} %get-tuple-element.25.refs_0_.codes, bf16[32,256,256]{2,1,0:T(8,128)(2,1)S(1)} %get-tuple-element.26.refs_1_.refs_0_, ...), custom_call_target="tpu_custom_call" | custom-call | tf_op jit(solution)/shard_map/pallas_call | solution.py:325
  13.3 0.0 copy-start
  13.3 0.0 copy-start.1
  13.3 0.4 collective-permute-start.5
  13.7 1.2 %collective-permute-start.4 = (f32[16,256]{1,0:T(8,128)S(1)}, f32[16,256]{1,0:T(8,128)S(1)}, u32[]{:S(2)}, u32[]{:S(2)}) collective-permute-start(f32[16,256]{1,0:T(8,128)S(1)} %get-tuple-element.31.part.refs_7_), channel_id=1, source_target_pairs={{0,2},{1,3},{2,0},{3,1},{4,6},{5,7},{6,4},{7,5},{8,10},{9,11},{10,... | collective-permute-start | bytes 49160 | tf_op jit(solution)/shard_map/ppermute | solution.py:24
  14.9 0.3 collective-permute-start.3
  15.2 1.1 %shard_map.107.refs_6_.refs_1_ = bf16[32,256,256]{2,1,0:T(8,128)(2,1)S(1)} custom-call(bf16[64,256,256]{2,1,0:T(8,128)(2,1)S(1)} %get-tuple-element.25.refs_0_.codes, f32[16,256]{1,0:T(8,128)S(1)} %get-tuple-element.31.part.refs_7_), custom_call_target="tpu_custom_call" | custom-call | tf_op jit(solution)/shard_map/pallas_call | solution.py:325
  16.3 0.3 collective-permute-done.5.refs_10_
  16.6 0.8 %collective-permute-done.4.refs_9_ = f32[16,256]{1,0:T(8,128)S(1)} collective-permute-done((f32[16,256]{1,0:T(8,128)S(1)}, f32[16,256]{1,0:T(8,128)S(1)}, u32[]{:S(2)}, u32[]{:S(2)}) %collective-permute-start.4) | collective-permute-done | bytes 16416 | tf_op jit(solution)/shard_map/ppermute | solution.py:24
  17.4 0.0 collective-permute-done.3.refs_8_
  17.4 0.0 copy-done
  17.4 0.0 copy-done.1
  17.4 1.4 %shard_map.108.refs_7_ = f32[16,256]{1,0:T(8,128)S(1)} custom-call(bf16[64,256,256]{2,1,0:T(8,128)(2,1)S(1)} %get-tuple-element.25.refs_0_.codes, bf16[64,16]{1,0:T(8,128)(2,1)S(1)} %get-tuple-element.33.refs_1_, bf16[16,128]{1,0:T(8,128)(2,1)S(1)} %get-tuple-element.34.refs_2_, f32[64,256]{1,0:T(8,128)S(1)} %get-tuple-element.27.refs_2_.refs_3_.refs_4_, ...), custom_call_target="tpu_custom_call" | custom-call | tf_op jit(solution)/shard_map/pallas_call | solution.py:325
  18.8 2.6 %collective-permute-start.8 = (f32[16,256]{1,0:T(8,128)S(1)}, f32[16,256]{1,0:T(8,128)S(1)}, u32[]{:S(2)}, u32[]{:S(2)}) collective-permute-start(f32[16,256]{1,0:T(8,128)S(1)} %shard_map.108.refs_7_), channel_id=1, source_target_pairs={{0,8},{4,12},{8,0},{12,4},{1,9},{5,13},{9,1},{13,5},{2,10},{6,14},... | collective-permute-start | bytes 49160 | tf_op jit(solution)/shard_map/ppermute | solution.py:24
  21.4 1.4 %collective-permute-start.7 = (f32[16,256]{1,0:T(8,128)S(1)}, f32[16,256]{1,0:T(8,128)S(1)}, u32[]{:S(2)}, u32[]{:S(2)}) collective-permute-start(f32[16,256]{1,0:T(8,128)S(1)} %shard_map.108.refs_7_), channel_id=1, source_target_pairs={{0,12},{4,8},{8,4},{12,0},{1,13},{5,9},{9,5},{13,1},{2,14},{6,10},... | collective-permute-start | bytes 49160 | tf_op jit(solution)/shard_map/ppermute | solution.py:24
  22.7 0.0 collective-permute-start.6
  22.7 0.7 %collective-permute-done.8.refs_10_ = f32[16,256]{1,0:T(8,128)S(1)} collective-permute-done((f32[16,256]{1,0:T(8,128)S(1)}, f32[16,256]{1,0:T(8,128)S(1)}, u32[]{:S(2)}, u32[]{:S(2)}) %collective-permute-start.8) | collective-permute-done | bytes 16416 | tf_op jit(solution)/shard_map/ppermute | solution.py:24
  23.5 3.4 %collective-permute-done.7.refs_9_ = f32[16,256]{1,0:T(8,128)S(1)} collective-permute-done((f32[16,256]{1,0:T(8,128)S(1)}, f32[16,256]{1,0:T(8,128)S(1)}, u32[]{:S(2)}, u32[]{:S(2)}) %collective-permute-start.7) | collective-permute-done | bytes 16416 | tf_op jit(solution)/shard_map/ppermute | solution.py:24
  26.9 0.0 collective-permute-done.6.refs_8_
  26.9 1.4 %shard_map.109 = (f32[24,256]{1,0:T(8,128)S(1)}, f32[16,256]{1,0:T(8,128)S(1)}) custom-call(bf16[32,256,256]{2,1,0:T(8,128)(2,1)S(1)} %get-tuple-element.26.refs_1_.refs_0_, bf16[32,256,256]{2,1,0:T(8,128)(2,1)S(1)} %shard_map.107.refs_6_.refs_1_, bf16[64,16]{1,0:T(8,128)(2,1)S(1)} %get-tuple-element.32.refs_2_, ...), custom_call_target="tpu_custom_call" | custom-call | tf_op jit(solution)/shard_map/pallas_call | solution.py:325
  28.4 0.0 collective-permute-start.11
  28.4 1.5 %collective-permute-start.10 = (f32[24,256]{1,0:T(8,128)S(1)}, f32[24,256]{1,0:T(8,128)S(1)}, u32[]{:S(2)}, u32[]{:S(2)}) collective-permute-start(f32[24,256]{1,0:T(8,128)S(1)} %get-tuple-element.36.refs_5_), channel_id=1, source_target_pairs={{0,2},{1,3},{2,0},{3,1},{4,6},{5,7},{6,4},{7,5},{8,10},{9,11},{10,... | collective-permute-start | bytes 73736 | tf_op jit(solution)/shard_map/ppermute | solution.py:24
  29.9 0.4 collective-permute-start.9
  30.2 1.6 %collective-permute-done.11.refs_8_ = f32[24,256]{1,0:T(8,128)S(1)} collective-permute-done((f32[24,256]{1,0:T(8,128)S(1)}, f32[24,256]{1,0:T(8,128)S(1)}, u32[]{:S(2)}, u32[]{:S(2)}) %collective-permute-start.11) | collective-permute-done | bytes 24608 | tf_op jit(solution)/shard_map/ppermute | solution.py:24
  31.9 0.4 collective-permute-done.10.refs_7_
  32.2 0.0 collective-permute-done.9.refs_6_
  32.2 1.4 %shard_map.110 = (f32[24,256]{1,0:T(8,128)S(1)}, f32[16,256]{1,0:T(8,128)S(1)}, f32[8,256]{1,0:T(8,128)S(1)}) custom-call(bf16[64,256,256]{2,1,0:T(8,128)(2,1)S(1)} %get-tuple-element.25.refs_0_.codes, bf16[64,16]{1,0:T(8,128)(2,1)S(1)} %get-tuple-element.33.refs_1_, bf16[16,128]{1,0:T(8,128)(2,1)S(1)} %get-tuple-element.34.refs_2_, ...), custom_call_target="tpu_custom_call" | custom-call | tf_op jit(solution)/shard_map/pallas_call | solution.py:325
  33.7 0.8 %collective-permute-start.14 = (f32[24,256]{1,0:T(8,128)S(1)}, f32[24,256]{1,0:T(8,128)S(1)}, u32[]{:S(2)}, u32[]{:S(2)}) collective-permute-start(f32[24,256]{1,0:T(8,128)S(1)} %get-tuple-element.38.refs_8_), channel_id=1, source_target_pairs={{0,8},{4,12},{8,0},{12,4},{1,9},{5,13},{9,1},{13,5},{2,10},{6,14},... | collective-permute-start | bytes 73736 | tf_op jit(solution)/shard_map/ppermute | solution.py:24
  34.4 1.4 %collective-permute-start.13 = (f32[24,256]{1,0:T(8,128)S(1)}, f32[24,256]{1,0:T(8,128)S(1)}, u32[]{:S(2)}, u32[]{:S(2)}) collective-permute-start(f32[24,256]{1,0:T(8,128)S(1)} %get-tuple-element.38.refs_8_), channel_id=1, source_target_pairs={{0,12},{4,8},{8,4},{12,0},{1,13},{5,9},{9,5},{13,1},{2,14},{6,10},... | collective-permute-start | bytes 73736 | tf_op jit(solution)/shard_map/ppermute | solution.py:24
  35.8 1.4 %collective-permute-start.12 = (f32[24,256]{1,0:T(8,128)S(1)}, f32[24,256]{1,0:T(8,128)S(1)}, u32[]{:S(2)}, u32[]{:S(2)}) collective-permute-start(f32[24,256]{1,0:T(8,128)S(1)} %get-tuple-element.38.refs_8_), channel_id=1, source_target_pairs={{0,4},{4,0},{8,12},{12,8},{1,5},{5,1},{9,13},{13,9},{2,6},{6,2},{1... | collective-permute-start | bytes 73736 | tf_op jit(solution)/shard_map/ppermute | solution.py:24
  37.2 1.3 %collective-permute-done.14.refs_11_ = f32[24,256]{1,0:T(8,128)S(1)} collective-permute-done((f32[24,256]{1,0:T(8,128)S(1)}, f32[24,256]{1,0:T(8,128)S(1)}, u32[]{:S(2)}, u32[]{:S(2)}) %collective-permute-start.14) | collective-permute-done | bytes 24608 | tf_op jit(solution)/shard_map/ppermute | solution.py:24
  38.5 1.6 %collective-permute-done.13.refs_10_ = f32[24,256]{1,0:T(8,128)S(1)} collective-permute-done((f32[24,256]{1,0:T(8,128)S(1)}, f32[24,256]{1,0:T(8,128)S(1)}, u32[]{:S(2)}, u32[]{:S(2)}) %collective-permute-start.13) | collective-permute-done | bytes 24608 | tf_op jit(solution)/shard_map/ppermute | solution.py:24
  40.1 0.0 collective-permute-done.12.refs_9_
  40.1 1.5 %shard_map.111 = (f32[24,256]{1,0:T(8,128)S(1)}, f32[16,256]{1,0:T(8,128)S(1)}, f32[8,128]{1,0:T(8,128)S(1)}) custom-call(bf16[32,256,256]{2,1,0:T(8,128)(2,1)S(1)} %get-tuple-element.26.refs_1_.refs_0_, bf16[32,256,256]{2,1,0:T(8,128)(2,1)S(1)} %shard_map.107.refs_6_.refs_1_, bf16[64,16]{1,0:T(8,128)(2,1)S(1)} %get-tuple-element.32.refs_2_, ...), custom_call_target="tpu_custom_call" | custom-call | tf_op jit(solution)/shard_map/pallas_call | solution.py:325
  41.6 0.0 collective-permute-start.17
  41.6 1.5 %collective-permute-start.16 = (f32[24,256]{1,0:T(8,128)S(1)}, f32[24,256]{1,0:T(8,128)S(1)}, u32[]{:S(2)}, u32[]{:S(2)}) collective-permute-start(f32[24,256]{1,0:T(8,128)S(1)} %get-tuple-element.42.refs_7_), channel_id=1, source_target_pairs={{0,2},{1,3},{2,0},{3,1},{4,6},{5,7},{6,4},{7,5},{8,10},{9,11},{10,... | collective-permute-start | bytes 73736 | tf_op jit(solution)/shard_map/ppermute | solution.py:24
  43.1 0.4 collective-permute-start.15
  43.5 1.6 %collective-permute-done.17.refs_10_ = f32[24,256]{1,0:T(8,128)S(1)} collective-permute-done((f32[24,256]{1,0:T(8,128)S(1)}, f32[24,256]{1,0:T(8,128)S(1)}, u32[]{:S(2)}, u32[]{:S(2)}) %collective-permute-start.17) | collective-permute-done | bytes 24608 | tf_op jit(solution)/shard_map/ppermute | solution.py:24
  45.1 0.4 collective-permute-done.16.refs_9_
  45.5 0.0 collective-permute-done.15.refs_8_
  45.5 1.6 %shard_map.112 = (f32[8,256]{1,0:T(8,128)S(1)}, f32[8,256]{1,0:T(8,128)S(1)}, f32[8,256]{1,0:T(8,128)S(1)}, f32[8,256]{1,0:T(8,128)S(1)}, f32[8,256]{1,0:T(8,128)S(1)}) custom-call(bf16[64,256,256]{2,1,0:T(8,128)(2,1)S(1)} %get-tuple-element.25.refs_0_.codes, bf16[64,16]{1,0:T(8,128)(2,1)S(1)} %get-tuple-element.33.refs_1_, ...), custom_call_target="tpu_custom_call" | custom-call | tf_op jit(solution)/shard_map/pallas_call | solution.py:325
  47.1 1.5 %collective-permute-start.18 = (f32[8,256]{1,0:T(8,128)S(1)}, f32[8,256]{1,0:T(8,128)S(1)}, u32[]{:S(2)}, u32[]{:S(2)}) collective-permute-start(f32[8,256]{1,0:T(8,128)S(1)} %get-tuple-element.45), channel_id=1, source_target_pairs={{0,8},{4,12},{8,0},{12,4},{1,9},{5,13},{9,1},{13,5},{2,10},{6,14},... | collective-permute-start | bytes 24584 | tf_op jit(solution)/shard_map/ppermute | solution.py:24
  48.6 1.8 %collective-permute-start.19 = (f32[8,256]{1,0:T(8,128)S(1)}, f32[8,256]{1,0:T(8,128)S(1)}, u32[]{:S(2)}, u32[]{:S(2)}) collective-permute-start(f32[8,256]{1,0:T(8,128)S(1)} %get-tuple-element.46), channel_id=1, source_target_pairs={{0,12},{4,8},{8,4},{12,0},{1,13},{5,9},{9,5},{13,1},{2,14},{6,10},... | collective-permute-start | bytes 24584 | tf_op jit(solution)/shard_map/ppermute | solution.py:24
  50.4 0.2 collective-permute-start.20
  50.6 1.1 %collective-permute-done.18.refs_7_ = f32[8,256]{1,0:T(8,128)S(1)} collective-permute-done((f32[8,256]{1,0:T(8,128)S(1)}, f32[8,256]{1,0:T(8,128)S(1)}, u32[]{:S(2)}, u32[]{:S(2)}) %collective-permute-start.18) | collective-permute-done | bytes 8224 | tf_op jit(solution)/shard_map/ppermute | solution.py:24
  51.6 2.4 %collective-permute-done.19.refs_8_ = f32[8,256]{1,0:T(8,128)S(1)} collective-permute-done((f32[8,256]{1,0:T(8,128)S(1)}, f32[8,256]{1,0:T(8,128)S(1)}, u32[]{:S(2)}, u32[]{:S(2)}) %collective-permute-start.19) | collective-permute-done | bytes 8224 | tf_op jit(solution)/shard_map/ppermute | solution.py:24
  54.0 0.1 collective-permute-done.20.refs_9_
  54.1 0.8 %shard_map.113 = (f32[4,256]{1,0:T(4,128)}, f32[4,256]{1,0:T(4,128)}) custom-call(f32[16,256]{1,0:T(8,128)S(1)} %get-tuple-element.29.refs_6_.refs_5_.refs_0_, f32[16,256]{1,0:T(8,128)S(1)} %get-tuple-element.30.refs_5_.refs_1_, f32[16,256]{1,0:T(8,128)S(1)} %get-tuple-element.35.refs_6_.refs_2_, f32[16,256]{1,0:T(8,128)S(1)} %get-tuple-element.39.refs_3_, ...), custom_call_target="tpu_custom_call" | custom-call | tf_op jit(solution)/shard_map/pallas_call | solution.py:325
Async XLA Ops:
  0.6 10.5 %copy-start.2 = (s32[64]{0:T(128)S(1)}, s32[64]{0:T(128)}, u32[]{:S(2)}) copy-start(s32[64]{0:T(128)} %param.12) | copy-start | bytes 772
  1.4 9.7 %collective-permute-start.2 = (f32[16,256]{1,0:T(8,128)S(1)}, f32[16,256]{1,0:T(8,128)S(1)}, u32[]{:S(2)}, u32[]{:S(2)}) collective-permute-start(f32[16,256]{1,0:T(8,128)S(1)} %shard_map.104.opening.refs_6_), channel_id=1, source_target_pairs={{0,8},{4,12},{8,0},{12,4},{1,9},{5,13},{9,1},{13,5},{2,10},{6,14},... | collective-permute-start | bytes 49160 | tf_op jit(solution)/shard_map/ppermute | solution.py:24
  5.5 5.6 %collective-permute-start.1 = (f32[16,256]{1,0:T(8,128)S(1)}, f32[16,256]{1,0:T(8,128)S(1)}, u32[]{:S(2)}, u32[]{:S(2)}) collective-permute-start(f32[16,256]{1,0:T(8,128)S(1)} %shard_map.104.opening.refs_6_), channel_id=1, source_target_pairs={{0,12},{4,8},{8,4},{12,0},{1,13},{5,9},{9,5},{13,1},{2,14},{6,10},... | collective-permute-start | bytes 49160 | tf_op jit(solution)/shard_map/ppermute | solution.py:24
  6.8 4.3 %collective-permute-start = (f32[16,256]{1,0:T(8,128)S(1)}, f32[16,256]{1,0:T(8,128)S(1)}, u32[]{:S(2)}, u32[]{:S(2)}) collective-permute-start(f32[16,256]{1,0:T(8,128)S(1)} %shard_map.104.opening.refs_6_), channel_id=1, source_target_pairs={{0,4},{4,0},{8,12},{12,8},{1,5},{5,1},{9,13},{13,9},{2,6},{6,2},{1... | collective-permute-start | bytes 49160 | tf_op jit(solution)/shard_map/ppermute | solution.py:24
  13.3 4.1 %copy-start = (f32[16,256]{1,0:T(8,128)S(1)}, f32[16,256]{1,0:T(8,128)}, u32[]{:S(2)}) copy-start(f32[16,256]{1,0:T(8,128)} %refs_4_.5) | copy-start | bytes 49156
  13.3 4.1 %copy-start.1 = (f32[16,256]{1,0:T(8,128)S(1)}, f32[16,256]{1,0:T(8,128)}, u32[]{:S(2)}) copy-start(f32[16,256]{1,0:T(8,128)} %refs_4_.3) | copy-start | bytes 49156
  13.3 3.3 %collective-permute-start.5 = (f32[16,256]{1,0:T(8,128)S(1)}, f32[16,256]{1,0:T(8,128)S(1)}, u32[]{:S(2)}, u32[]{:S(2)}) collective-permute-start(f32[16,256]{1,0:T(8,128)S(1)} %get-tuple-element.31.part.refs_7_), channel_id=1, source_target_pairs={{0,3},{1,2},{2,1},{3,0},{4,7},{5,6},{6,5},{7,4},{8,11},{9,10},{10,... | collective-permute-start | bytes 49160 | tf_op jit(solution)/shard_map/ppermute | solution.py:24
  13.7 3.7 %collective-permute-start.4 = (f32[16,256]{1,0:T(8,128)S(1)}, f32[16,256]{1,0:T(8,128)S(1)}, u32[]{:S(2)}, u32[]{:S(2)}) collective-permute-start(f32[16,256]{1,0:T(8,128)S(1)} %get-tuple-element.31.part.refs_7_), channel_id=1, source_target_pairs={{0,2},{1,3},{2,0},{3,1},{4,6},{5,7},{6,4},{7,5},{8,10},{9,11},{10,... | collective-permute-start | bytes 49160 | tf_op jit(solution)/shard_map/ppermute | solution.py:24
  14.9 2.6 %collective-permute-start.3 = (f32[16,256]{1,0:T(8,128)S(1)}, f32[16,256]{1,0:T(8,128)S(1)}, u32[]{:S(2)}, u32[]{:S(2)}) collective-permute-start(f32[16,256]{1,0:T(8,128)S(1)} %get-tuple-element.31.part.refs_7_), channel_id=1, source_target_pairs={{0,1},{1,0},{2,3},{3,2},{4,5},{5,4},{6,7},{7,6},{8,9},{9,8},{10,11... | collective-permute-start | bytes 49160 | tf_op jit(solution)/shard_map/ppermute | solution.py:24
  18.8 4.6 %collective-permute-start.8 = (f32[16,256]{1,0:T(8,128)S(1)}, f32[16,256]{1,0:T(8,128)S(1)}, u32[]{:S(2)}, u32[]{:S(2)}) collective-permute-start(f32[16,256]{1,0:T(8,128)S(1)} %shard_map.108.refs_7_), channel_id=1, source_target_pairs={{0,8},{4,12},{8,0},{12,4},{1,9},{5,13},{9,1},{13,5},{2,10},{6,14},... | collective-permute-start | bytes 49160 | tf_op jit(solution)/shard_map/ppermute | solution.py:24
  21.4 5.5 %collective-permute-start.7 = (f32[16,256]{1,0:T(8,128)S(1)}, f32[16,256]{1,0:T(8,128)S(1)}, u32[]{:S(2)}, u32[]{:S(2)}) collective-permute-start(f32[16,256]{1,0:T(8,128)S(1)} %shard_map.108.refs_7_), channel_id=1, source_target_pairs={{0,12},{4,8},{8,4},{12,0},{1,13},{5,9},{9,5},{13,1},{2,14},{6,10},... | collective-permute-start | bytes 49160 | tf_op jit(solution)/shard_map/ppermute | solution.py:24
  22.7 4.2 %collective-permute-start.6 = (f32[16,256]{1,0:T(8,128)S(1)}, f32[16,256]{1,0:T(8,128)S(1)}, u32[]{:S(2)}, u32[]{:S(2)}) collective-permute-start(f32[16,256]{1,0:T(8,128)S(1)} %shard_map.108.refs_7_), channel_id=1, source_target_pairs={{0,4},{4,0},{8,12},{12,8},{1,5},{5,1},{9,13},{13,9},{2,6},{6,2},{1... | collective-permute-start | bytes 49160 | tf_op jit(solution)/shard_map/ppermute | solution.py:24
  28.4 3.5 %collective-permute-start.11 = (f32[24,256]{1,0:T(8,128)S(1)}, f32[24,256]{1,0:T(8,128)S(1)}, u32[]{:S(2)}, u32[]{:S(2)}) collective-permute-start(f32[24,256]{1,0:T(8,128)S(1)} %get-tuple-element.36.refs_5_), channel_id=1, source_target_pairs={{0,3},{1,2},{2,1},{3,0},{4,7},{5,6},{6,5},{7,4},{8,11},{9,10},{10,... | collective-permute-start | bytes 73736 | tf_op jit(solution)/shard_map/ppermute | solution.py:24
  28.4 3.9 %collective-permute-start.10 = (f32[24,256]{1,0:T(8,128)S(1)}, f32[24,256]{1,0:T(8,128)S(1)}, u32[]{:S(2)}, u32[]{:S(2)}) collective-permute-start(f32[24,256]{1,0:T(8,128)S(1)} %get-tuple-element.36.refs_5_), channel_id=1, source_target_pairs={{0,2},{1,3},{2,0},{3,1},{4,6},{5,7},{6,4},{7,5},{8,10},{9,11},{10,... | collective-permute-start | bytes 73736 | tf_op jit(solution)/shard_map/ppermute | solution.py:24
  29.9 2.4 %collective-permute-start.9 = (f32[24,256]{1,0:T(8,128)S(1)}, f32[24,256]{1,0:T(8,128)S(1)}, u32[]{:S(2)}, u32[]{:S(2)}) collective-permute-start(f32[24,256]{1,0:T(8,128)S(1)} %get-tuple-element.36.refs_5_), channel_id=1, source_target_pairs={{0,1},{1,0},{2,3},{3,2},{4,5},{5,4},{6,7},{7,6},{8,9},{9,8},{10,11... | collective-permute-start | bytes 73736 | tf_op jit(solution)/shard_map/ppermute | solution.py:24
  33.7 4.8 %collective-permute-start.14 = (f32[24,256]{1,0:T(8,128)S(1)}, f32[24,256]{1,0:T(8,128)S(1)}, u32[]{:S(2)}, u32[]{:S(2)}) collective-permute-start(f32[24,256]{1,0:T(8,128)S(1)} %get-tuple-element.38.refs_8_), channel_id=1, source_target_pairs={{0,8},{4,12},{8,0},{12,4},{1,9},{5,13},{9,1},{13,5},{2,10},{6,14},... | collective-permute-start | bytes 73736 | tf_op jit(solution)/shard_map/ppermute | solution.py:24
  34.4 5.7 %collective-permute-start.13 = (f32[24,256]{1,0:T(8,128)S(1)}, f32[24,256]{1,0:T(8,128)S(1)}, u32[]{:S(2)}, u32[]{:S(2)}) collective-permute-start(f32[24,256]{1,0:T(8,128)S(1)} %get-tuple-element.38.refs_8_), channel_id=1, source_target_pairs={{0,12},{4,8},{8,4},{12,0},{1,13},{5,9},{9,5},{13,1},{2,14},{6,10},... | collective-permute-start | bytes 73736 | tf_op jit(solution)/shard_map/ppermute | solution.py:24
  35.8 4.3 %collective-permute-start.12 = (f32[24,256]{1,0:T(8,128)S(1)}, f32[24,256]{1,0:T(8,128)S(1)}, u32[]{:S(2)}, u32[]{:S(2)}) collective-permute-start(f32[24,256]{1,0:T(8,128)S(1)} %get-tuple-element.38.refs_8_), channel_id=1, source_target_pairs={{0,4},{4,0},{8,12},{12,8},{1,5},{5,1},{9,13},{13,9},{2,6},{6,2},{1... | collective-permute-start | bytes 73736 | tf_op jit(solution)/shard_map/ppermute | solution.py:24
  41.6 3.5 %collective-permute-start.17 = (f32[24,256]{1,0:T(8,128)S(1)}, f32[24,256]{1,0:T(8,128)S(1)}, u32[]{:S(2)}, u32[]{:S(2)}) collective-permute-start(f32[24,256]{1,0:T(8,128)S(1)} %get-tuple-element.42.refs_7_), channel_id=1, source_target_pairs={{0,3},{1,2},{2,1},{3,0},{4,7},{5,6},{6,5},{7,4},{8,11},{9,10},{10,... | collective-permute-start | bytes 73736 | tf_op jit(solution)/shard_map/ppermute | solution.py:24
  41.6 3.9 %collective-permute-start.16 = (f32[24,256]{1,0:T(8,128)S(1)}, f32[24,256]{1,0:T(8,128)S(1)}, u32[]{:S(2)}, u32[]{:S(2)}) collective-permute-start(f32[24,256]{1,0:T(8,128)S(1)} %get-tuple-element.42.refs_7_), channel_id=1, source_target_pairs={{0,2},{1,3},{2,0},{3,1},{4,6},{5,7},{6,4},{7,5},{8,10},{9,11},{10,... | collective-permute-start | bytes 73736 | tf_op jit(solution)/shard_map/ppermute | solution.py:24
  43.1 2.4 %collective-permute-start.15 = (f32[24,256]{1,0:T(8,128)S(1)}, f32[24,256]{1,0:T(8,128)S(1)}, u32[]{:S(2)}, u32[]{:S(2)}) collective-permute-start(f32[24,256]{1,0:T(8,128)S(1)} %get-tuple-element.42.refs_7_), channel_id=1, source_target_pairs={{0,1},{1,0},{2,3},{3,2},{4,5},{5,4},{6,7},{7,6},{8,9},{9,8},{10,11... | collective-permute-start | bytes 73736 | tf_op jit(solution)/shard_map/ppermute | solution.py:24
  47.1 4.6 %collective-permute-start.18 = (f32[8,256]{1,0:T(8,128)S(1)}, f32[8,256]{1,0:T(8,128)S(1)}, u32[]{:S(2)}, u32[]{:S(2)}) collective-permute-start(f32[8,256]{1,0:T(8,128)S(1)} %get-tuple-element.45), channel_id=1, source_target_pairs={{0,8},{4,12},{8,0},{12,4},{1,9},{5,13},{9,1},{13,5},{2,10},{6,14},... | collective-permute-start | bytes 24584 | tf_op jit(solution)/shard_map/ppermute | solution.py:24
  48.6 5.5 %collective-permute-start.19 = (f32[8,256]{1,0:T(8,128)S(1)}, f32[8,256]{1,0:T(8,128)S(1)}, u32[]{:S(2)}, u32[]{:S(2)}) collective-permute-start(f32[8,256]{1,0:T(8,128)S(1)} %get-tuple-element.46), channel_id=1, source_target_pairs={{0,12},{4,8},{8,4},{12,0},{1,13},{5,9},{9,5},{13,1},{2,14},{6,10},... | collective-permute-start | bytes 24584 | tf_op jit(solution)/shard_map/ppermute | solution.py:24
  50.4 3.7 %collective-permute-start.20 = (f32[8,256]{1,0:T(8,128)S(1)}, f32[8,256]{1,0:T(8,128)S(1)}, u32[]{:S(2)}, u32[]{:S(2)}) collective-permute-start(f32[8,256]{1,0:T(8,128)S(1)} %get-tuple-element.47), channel_id=1, source_target_pairs={{0,4},{4,0},{8,12},{12,8},{1,5},{5,1},{9,13},{13,9},{2,6},{6,2},{1... | collective-permute-start | bytes 24584 | tf_op jit(solution)/shard_map/ppermute | solution.py:24

commit v2 on v0

--- a/solution.py
+++ b/solution.py
@@ -11,7 +11,6 @@
 EXTRA = 8
 LIMIT = 16 * 1024 * 1024
 GROUP = 16
-CHUNK = 16
 F32 = jnp.float32
 BF16 = jnp.bfloat16
 
@@ -125,11 +124,13 @@
     for copy in near:
         copy.start()
     tiles, width = wide_scale.shape
-    copies = []
-    for chunk in range(tiles // CHUNK):
-        span = pl.ds(chunk * CHUNK, CHUNK)
-        copies.append(pltpu.make_async_copy(far_codes.at[span], codes.at[span], done.at[chunk]))
-        copies[-1].start()
+    first = early.shape[0]
+    spans = [pl.ds(0, first), pl.ds(first, tiles - first)]
+    copies = [
+        pltpu.make_async_copy(far_codes.at[span], codes.at[span], done.at[i])
+        for i, span in enumerate(spans)
+    ]
+    copies[0].start()
     for copy in near:
         copy.wait()
     tables(row[...], rows_pick.shape[1], rows_pick, rows_pair)
@@ -141,10 +142,11 @@
         precision=HIGH,
         preferred_element_type=F32,
     )
-    for chunk, copy in enumerate(copies):
-        copy.wait()
-        for k in range(chunk * CHUNK, min((chunk + 1) * CHUNK, early.shape[0])):
-            early[k] = codes[k].T
+    copies[0].wait()
+    copies[1].start()
+    for k in range(first):
+        early[k] = codes[k].T
+    copies[1].wait()
 
 
 def turning_kernel(codes, part, late):
@@ -346,6 +348,7 @@
     count = lax.axis_size("tiles")
     sharing = lax.axis_size(("split", "depth"))
     cells = count * blocks
+    late_tiles = tiles * 3 // 8
     place = lax.axis_index("tiles").astype(jnp.int32).reshape(1)
 
     order = [0] + sorted(range(1, count), key=lambda shift: (shift != 1, -abs(2 * shift - count)))
@@ -376,7 +379,7 @@
         loading_kernel,
         [
             (tile_codes.shape, BF16),
-            ((tiles - CHUNK, width, width), BF16),
+            ((tiles - late_tiles, width, width), BF16),
             ((tiles, data_rows), BF16),
             ((data_rows, 2 * tiles), BF16),
             ((tiles, width), F32),
@@ -388,7 +391,7 @@
         scratch=[
             pltpu.VMEM((1, tiles), F32),
             pltpu.VMEM((1, tiles), jnp.int32),
-            pltpu.SemaphoreType.DMA((tiles // CHUNK,)),
+            pltpu.SemaphoreType.DMA((2,)),
             pltpu.SemaphoreType.DMA((2,)),
         ],
     )
@@ -410,7 +413,7 @@
         *begin,
     )
     parts = within(part)
-    (late,) = call(turning_kernel, [((CHUNK, width, width), BF16)], codes, part)
+    (late,) = call(turning_kernel, [((late_tiles, width, width), BF16)], codes, part)
     (part,) = call(
         functools.partial(start_data_kernel, sharing),
         [((cells, width), F32)],

time: 55.4 us -> 55.4 us (level)
  transfers between devices with their start and end apart: 21 -> 21, of which waited for: 13 -> 13; matrix products, arithmetic and copies ran while one was open for 0% -> 0% of each run, Pallas kernels for 9% -> 10%
where the time goes in v2:
time: 55.4 us; the launch traced here: 55.2 us
  starting transfers between devices  22.2 us (40%)
  Pallas kernels  16.2 us (29%)
  waiting for transfers between devices  16 us (29%)
  between operations  0.72 us (1%)
    ppermute x21, starting transfers between devices, exchange(): parts[shift] = lax.ppermute(values[shift], axes, perm)  22.2 us
    pallas_call x10, Pallas kernels, call(): pl.pallas_call(body, out_shape=[jax.ShapeDtypeStruct(shape, dtype) for sh...  16.2 us
    ppermute x21, waiting for transfers between devices, exchange(): parts[shift] = lax.ppermute(values[shift], axes, perm)  16 us
  transfers between devices with their start and end apart: 21, of which 13 were waited for; matrix products, arithmetic and copies ran while one was open for 0% of the time, Pallas kernels for 10%

profile of v2, /device:TPU:0, one launch (start us, length us, event | category | flops | bytes accessed | tf_op | source)
XLA Modules:
  0.0 55.2 jit_solution(665822275844542317)
XLA Ops:
  0.6 0.0 copy-start.2
  0.6 0.7 %shard_map.104.opening.refs_6_ = f32[16,256]{1,0:T(8,128)S(1)} custom-call(f32[4,256]{1,0:T(4,128)} %start.1, f32[4,256]{1,0:T(4,128)} %weight.1, s32[2,4]{1,0:T(2,128)} %bitcast.8), custom_call_target="tpu_custom_call" | custom-call | tf_op jit(solution)/shard_map/pallas_call | solution.py:323
  1.4 4.1 %collective-permute-start.2 = (f32[16,256]{1,0:T(8,128)S(1)}, f32[16,256]{1,0:T(8,128)S(1)}, u32[]{:S(2)}, u32[]{:S(2)}) collective-permute-start(f32[16,256]{1,0:T(8,128)S(1)} %shard_map.104.opening.refs_6_), channel_id=1, source_target_pairs={{0,8},{4,12},{8,0},{12,4},{1,9},{5,13},{9,1},{13,5},{2,10},{6,14},... | collective-permute-start | bytes 49160 | tf_op jit(solution)/shard_map/ppermute | solution.py:22
  5.5 1.3 %collective-permute-start.1 = (f32[16,256]{1,0:T(8,128)S(1)}, f32[16,256]{1,0:T(8,128)S(1)}, u32[]{:S(2)}, u32[]{:S(2)}) collective-permute-start(f32[16,256]{1,0:T(8,128)S(1)} %shard_map.104.opening.refs_6_), channel_id=1, source_target_pairs={{0,12},{4,8},{8,4},{12,0},{1,13},{5,9},{9,5},{13,1},{2,14},{6,10},... | collective-permute-start | bytes 49160 | tf_op jit(solution)/shard_map/ppermute | solution.py:22
  6.8 0.2 collective-permute-start
  7.1 4.4 %shard_map.105 = (bf16[64,256,256]{2,1,0:T(8,128)(2,1)S(1)}, bf16[40,256,256]{2,1,0:T(8,128)(2,1)S(1)}, bf16[64,16]{1,0:T(8,128)(2,1)S(1)}, bf16[16,128]{1,0:T(8,128)(2,1)S(1)}, f32[64,256]{1,0:T(8,128)S(1)}) custom-call(bf16[64,256,256]{2,1,0:T(8,128)(2,1)} %far_codes.1, f32[16,256]{1,0:T(8,128)S(1)} %shard_map.104.opening.refs_6_, f32[1,64]{1,0:T(1,128)} %bitcast.9, ...), custom_call_target="tpu_custom_call" | custom-call | tf_op jit(solution)/shard_map/pallas_call | solution.py:323
  11.5 0.0 collective-permute-done.2.refs_9_
  11.5 0.0 collective-permute-done.1.refs_8_
  11.5 0.0 collective-permute-done.refs_7_
  11.6 0.0 copy-done.2
  11.6 2.0 %shard_map.106 = (f32[16,256]{1,0:T(8,128)S(1)}, bf16[64,16]{1,0:T(8,128)(2,1)S(1)}, bf16[16,128]{1,0:T(8,128)(2,1)S(1)}, f32[16,256]{1,0:T(8,128)S(1)}, f32[16,256]{1,0:T(8,128)S(1)}) custom-call(bf16[64,256,256]{2,1,0:T(8,128)(2,1)S(1)} %get-tuple-element.25.refs_0_.codes, bf16[40,256,256]{2,1,0:T(8,128)(2,1)S(1)} %get-tuple-element.26.refs_1_.refs_0_, ...), custom_call_target="tpu_custom_call" | custom-call | tf_op jit(solution)/shard_map/pallas_call | solution.py:323
  13.6 0.0 copy-start
  13.6 0.0 copy-start.1
  13.6 0.4 collective-permute-start.5
  13.9 1.2 %collective-permute-start.4 = (f32[16,256]{1,0:T(8,128)S(1)}, f32[16,256]{1,0:T(8,128)S(1)}, u32[]{:S(2)}, u32[]{:S(2)}) collective-permute-start(f32[16,256]{1,0:T(8,128)S(1)} %get-tuple-element.31.part.refs_7_), channel_id=1, source_target_pairs={{0,2},{1,3},{2,0},{3,1},{4,6},{5,7},{6,4},{7,5},{8,10},{9,11},{10,... | collective-permute-start | bytes 49160 | tf_op jit(solution)/shard_map/ppermute | solution.py:22
  15.1 0.3 collective-permute-start.3
  15.4 0.9 %shard_map.107.refs_6_.refs_1_ = bf16[24,256,256]{2,1,0:T(8,128)(2,1)S(1)} custom-call(bf16[64,256,256]{2,1,0:T(8,128)(2,1)S(1)} %get-tuple-element.25.refs_0_.codes, f32[16,256]{1,0:T(8,128)S(1)} %get-tuple-element.31.part.refs_7_), custom_call_target="tpu_custom_call" | custom-call | tf_op jit(solution)/shard_map/pallas_call | solution.py:323
  16.3 0.6 %collective-permute-done.5.refs_10_ = f32[16,256]{1,0:T(8,128)S(1)} collective-permute-done((f32[16,256]{1,0:T(8,128)S(1)}, f32[16,256]{1,0:T(8,128)S(1)}, u32[]{:S(2)}, u32[]{:S(2)}) %collective-permute-start.5) | collective-permute-done | bytes 16416 | tf_op jit(solution)/shard_map/ppermute | solution.py:22
  16.9 0.8 %collective-permute-done.4.refs_9_ = f32[16,256]{1,0:T(8,128)S(1)} collective-permute-done((f32[16,256]{1,0:T(8,128)S(1)}, f32[16,256]{1,0:T(8,128)S(1)}, u32[]{:S(2)}, u32[]{:S(2)}) %collective-permute-start.4) | collective-permute-done | bytes 16416 | tf_op jit(solution)/shard_map/ppermute | solution.py:22
  17.7 0.0 collective-permute-done.3.refs_8_
  17.7 0.0 copy-done
  17.7 0.0 copy-done.1
  17.7 1.4 %shard_map.108.refs_7_ = f32[16,256]{1,0:T(8,128)S(1)} custom-call(bf16[64,256,256]{2,1,0:T(8,128)(2,1)S(1)} %get-tuple-element.25.refs_0_.codes, bf16[64,16]{1,0:T(8,128)(2,1)S(1)} %get-tuple-element.33.refs_1_, bf16[16,128]{1,0:T(8,128)(2,1)S(1)} %get-tuple-element.34.refs_2_, f32[64,256]{1,0:T(8,128)S(1)} %get-tuple-element.27.refs_2_.refs_3_.refs_4_, ...), custom_call_target="tpu_custom_call" | custom-call | tf_op jit(solution)/shard_map/pallas_call | solution.py:323
  19.1 2.6 %collective-permute-start.8 = (f32[16,256]{1,0:T(8,128)S(1)}, f32[16,256]{1,0:T(8,128)S(1)}, u32[]{:S(2)}, u32[]{:S(2)}) collective-permute-start(f32[16,256]{1,0:T(8,128)S(1)} %shard_map.108.refs_7_), channel_id=1, source_target_pairs={{0,8},{4,12},{8,0},{12,4},{1,9},{5,13},{9,1},{13,5},{2,10},{6,14},... | collective-permute-start | bytes 49160 | tf_op jit(solution)/shard_map/ppermute | solution.py:22
  21.7 1.4 %collective-permute-start.7 = (f32[16,256]{1,0:T(8,128)S(1)}, f32[16,256]{1,0:T(8,128)S(1)}, u32[]{:S(2)}, u32[]{:S(2)}) collective-permute-start(f32[16,256]{1,0:T(8,128)S(1)} %shard_map.108.refs_7_), channel_id=1, source_target_pairs={{0,12},{4,8},{8,4},{12,0},{1,13},{5,9},{9,5},{13,1},{2,14},{6,10},... | collective-permute-start | bytes 49160 | tf_op jit(solution)/shard_map/ppermute | solution.py:22
  23.0 0.0 collective-permute-start.6
  23.0 0.7 %collective-permute-done.8.refs_10_ = f32[16,256]{1,0:T(8,128)S(1)} collective-permute-done((f32[16,256]{1,0:T(8,128)S(1)}, f32[16,256]{1,0:T(8,128)S(1)}, u32[]{:S(2)}, u32[]{:S(2)}) %collective-permute-start.8) | collective-permute-done | bytes 16416 | tf_op jit(solution)/shard_map/ppermute | solution.py:22
  23.8 3.4 %collective-permute-done.7.refs_9_ = f32[16,256]{1,0:T(8,128)S(1)} collective-permute-done((f32[16,256]{1,0:T(8,128)S(1)}, f32[16,256]{1,0:T(8,128)S(1)}, u32[]{:S(2)}, u32[]{:S(2)}) %collective-permute-start.7) | collective-permute-done | bytes 16416 | tf_op jit(solution)/shard_map/ppermute | solution.py:22
  27.2 0.0 collective-permute-done.6.refs_8_
  27.2 1.4 %shard_map.109 = (f32[24,256]{1,0:T(8,128)S(1)}, f32[16,256]{1,0:T(8,128)S(1)}) custom-call(bf16[40,256,256]{2,1,0:T(8,128)(2,1)S(1)} %get-tuple-element.26.refs_1_.refs_0_, bf16[24,256,256]{2,1,0:T(8,128)(2,1)S(1)} %shard_map.107.refs_6_.refs_1_, bf16[64,16]{1,0:T(8,128)(2,1)S(1)} %get-tuple-element.32.refs_2_, ...), custom_call_target="tpu_custom_call" | custom-call | tf_op jit(solution)/shard_map/pallas_call | solution.py:323
  28.6 0.0 collective-permute-start.11
  28.6 1.5 %collective-permute-start.10 = (f32[24,256]{1,0:T(8,128)S(1)}, f32[24,256]{1,0:T(8,128)S(1)}, u32[]{:S(2)}, u32[]{:S(2)}) collective-permute-start(f32[24,256]{1,0:T(8,128)S(1)} %get-tuple-element.36.refs_5_), channel_id=1, source_target_pairs={{0,2},{1,3},{2,0},{3,1},{4,6},{5,7},{6,4},{7,5},{8,10},{9,11},{10,... | collective-permute-start | bytes 73736 | tf_op jit(solution)/shard_map/ppermute | solution.py:22
  30.2 0.4 collective-permute-start.9
  30.5 1.6 %collective-permute-done.11.refs_8_ = f32[24,256]{1,0:T(8,128)S(1)} collective-permute-done((f32[24,256]{1,0:T(8,128)S(1)}, f32[24,256]{1,0:T(8,128)S(1)}, u32[]{:S(2)}, u32[]{:S(2)}) %collective-permute-start.11) | collective-permute-done | bytes 24608 | tf_op jit(solution)/shard_map/ppermute | solution.py:22
  32.2 0.4 collective-permute-done.10.refs_7_
  32.5 0.0 collective-permute-done.9.refs_6_
  32.5 1.4 %shard_map.110 = (f32[24,256]{1,0:T(8,128)S(1)}, f32[16,256]{1,0:T(8,128)S(1)}, f32[8,256]{1,0:T(8,128)S(1)}) custom-call(bf16[64,256,256]{2,1,0:T(8,128)(2,1)S(1)} %get-tuple-element.25.refs_0_.codes, bf16[64,16]{1,0:T(8,128)(2,1)S(1)} %get-tuple-element.33.refs_1_, bf16[16,128]{1,0:T(8,128)(2,1)S(1)} %get-tuple-element.34.refs_2_, ...), custom_call_target="tpu_custom_call" | custom-call | tf_op jit(solution)/shard_map/pallas_call | solution.py:323
  34.0 0.8 %collective-permute-start.14 = (f32[24,256]{1,0:T(8,128)S(1)}, f32[24,256]{1,0:T(8,128)S(1)}, u32[]{:S(2)}, u32[]{:S(2)}) collective-permute-start(f32[24,256]{1,0:T(8,128)S(1)} %get-tuple-element.38.refs_8_), channel_id=1, source_target_pairs={{0,8},{4,12},{8,0},{12,4},{1,9},{5,13},{9,1},{13,5},{2,10},{6,14},... | collective-permute-start | bytes 73736 | tf_op jit(solution)/shard_map/ppermute | solution.py:22
  34.7 1.4 %collective-permute-start.13 = (f32[24,256]{1,0:T(8,128)S(1)}, f32[24,256]{1,0:T(8,128)S(1)}, u32[]{:S(2)}, u32[]{:S(2)}) collective-permute-start(f32[24,256]{1,0:T(8,128)S(1)} %get-tuple-element.38.refs_8_), channel_id=1, source_target_pairs={{0,12},{4,8},{8,4},{12,0},{1,13},{5,9},{9,5},{13,1},{2,14},{6,10},... | collective-permute-start | bytes 73736 | tf_op jit(solution)/shard_map/ppermute | solution.py:22
  36.1 1.4 %collective-permute-start.12 = (f32[24,256]{1,0:T(8,128)S(1)}, f32[24,256]{1,0:T(8,128)S(1)}, u32[]{:S(2)}, u32[]{:S(2)}) collective-permute-start(f32[24,256]{1,0:T(8,128)S(1)} %get-tuple-element.38.refs_8_), channel_id=1, source_target_pairs={{0,4},{4,0},{8,12},{12,8},{1,5},{5,1},{9,13},{13,9},{2,6},{6,2},{1... | collective-permute-start | bytes 73736 | tf_op jit(solution)/shard_map/ppermute | solution.py:22
  37.5 1.3 %collective-permute-done.14.refs_11_ = f32[24,256]{1,0:T(8,128)S(1)} collective-permute-done((f32[24,256]{1,0:T(8,128)S(1)}, f32[24,256]{1,0:T(8,128)S(1)}, u32[]{:S(2)}, u32[]{:S(2)}) %collective-permute-start.14) | collective-permute-done | bytes 24608 | tf_op jit(solution)/shard_map/ppermute | solution.py:22
  38.7 1.6 %collective-permute-done.13.refs_10_ = f32[24,256]{1,0:T(8,128)S(1)} collective-permute-done((f32[24,256]{1,0:T(8,128)S(1)}, f32[24,256]{1,0:T(8,128)S(1)}, u32[]{:S(2)}, u32[]{:S(2)}) %collective-permute-start.13) | collective-permute-done | bytes 24608 | tf_op jit(solution)/shard_map/ppermute | solution.py:22
  40.4 0.0 collective-permute-done.12.refs_9_
  40.4 1.5 %shard_map.111 = (f32[24,256]{1,0:T(8,128)S(1)}, f32[16,256]{1,0:T(8,128)S(1)}, f32[8,128]{1,0:T(8,128)S(1)}) custom-call(bf16[40,256,256]{2,1,0:T(8,128)(2,1)S(1)} %get-tuple-element.26.refs_1_.refs_0_, bf16[24,256,256]{2,1,0:T(8,128)(2,1)S(1)} %shard_map.107.refs_6_.refs_1_, bf16[64,16]{1,0:T(8,128)(2,1)S(1)} %get-tuple-element.32.refs_2_, ...), custom_call_target="tpu_custom_call" | custom-call | tf_op jit(solution)/shard_map/pallas_call | solution.py:323
  41.9 0.0 collective-permute-start.17
  41.9 1.5 %collective-permute-start.16 = (f32[24,256]{1,0:T(8,128)S(1)}, f32[24,256]{1,0:T(8,128)S(1)}, u32[]{:S(2)}, u32[]{:S(2)}) collective-permute-start(f32[24,256]{1,0:T(8,128)S(1)} %get-tuple-element.42.refs_7_), channel_id=1, source_target_pairs={{0,2},{1,3},{2,0},{3,1},{4,6},{5,7},{6,4},{7,5},{8,10},{9,11},{10,... | collective-permute-start | bytes 73736 | tf_op jit(solution)/shard_map/ppermute | solution.py:22
  43.4 0.4 collective-permute-start.15
  43.8 1.6 %collective-permute-done.17.refs_10_ = f32[24,256]{1,0:T(8,128)S(1)} collective-permute-done((f32[24,256]{1,0:T(8,128)S(1)}, f32[24,256]{1,0:T(8,128)S(1)}, u32[]{:S(2)}, u32[]{:S(2)}) %collective-permute-start.17) | collective-permute-done | bytes 24608 | tf_op jit(solution)/shard_map/ppermute | solution.py:22
  45.4 0.4 collective-permute-done.16.refs_9_
  45.8 0.0 collective-permute-done.15.refs_8_
  45.8 1.6 %shard_map.112 = (f32[8,256]{1,0:T(8,128)S(1)}, f32[8,256]{1,0:T(8,128)S(1)}, f32[8,256]{1,0:T(8,128)S(1)}, f32[8,256]{1,0:T(8,128)S(1)}, f32[8,256]{1,0:T(8,128)S(1)}) custom-call(bf16[64,256,256]{2,1,0:T(8,128)(2,1)S(1)} %get-tuple-element.25.refs_0_.codes, bf16[64,16]{1,0:T(8,128)(2,1)S(1)} %get-tuple-element.33.refs_1_, ...), custom_call_target="tpu_custom_call" | custom-call | tf_op jit(solution)/shard_map/pallas_call | solution.py:323
  47.4 1.5 %collective-permute-start.18 = (f32[8,256]{1,0:T(8,128)S(1)}, f32[8,256]{1,0:T(8,128)S(1)}, u32[]{:S(2)}, u32[]{:S(2)}) collective-permute-start(f32[8,256]{1,0:T(8,128)S(1)} %get-tuple-element.45), channel_id=1, source_target_pairs={{0,8},{4,12},{8,0},{12,4},{1,9},{5,13},{9,1},{13,5},{2,10},{6,14},... | collective-permute-start | bytes 24584 | tf_op jit(solution)/shard_map/ppermute | solution.py:22
  48.9 1.8 %collective-permute-start.19 = (f32[8,256]{1,0:T(8,128)S(1)}, f32[8,256]{1,0:T(8,128)S(1)}, u32[]{:S(2)}, u32[]{:S(2)}) collective-permute-start(f32[8,256]{1,0:T(8,128)S(1)} %get-tuple-element.46), channel_id=1, source_target_pairs={{0,12},{4,8},{8,4},{12,0},{1,13},{5,9},{9,5},{13,1},{2,14},{6,10},... | collective-permute-start | bytes 24584 | tf_op jit(solution)/shard_map/ppermute | solution.py:22
  50.7 0.2 collective-permute-start.20
  50.9 1.1 %collective-permute-done.18.refs_7_ = f32[8,256]{1,0:T(8,128)S(1)} collective-permute-done((f32[8,256]{1,0:T(8,128)S(1)}, f32[8,256]{1,0:T(8,128)S(1)}, u32[]{:S(2)}, u32[]{:S(2)}) %collective-permute-start.18) | collective-permute-done | bytes 8224 | tf_op jit(solution)/shard_map/ppermute | solution.py:22
  51.9 2.4 %collective-permute-done.19.refs_8_ = f32[8,256]{1,0:T(8,128)S(1)} collective-permute-done((f32[8,256]{1,0:T(8,128)S(1)}, f32[8,256]{1,0:T(8,128)S(1)}, u32[]{:S(2)}, u32[]{:S(2)}) %collective-permute-start.19) | collective-permute-done | bytes 8224 | tf_op jit(solution)/shard_map/ppermute | solution.py:22
  54.3 0.1 collective-permute-done.20.refs_9_
  54.4 0.8 %shard_map.113 = (f32[4,256]{1,0:T(4,128)}, f32[4,256]{1,0:T(4,128)}) custom-call(f32[16,256]{1,0:T(8,128)S(1)} %get-tuple-element.29.refs_6_.refs_5_.refs_0_, f32[16,256]{1,0:T(8,128)S(1)} %get-tuple-element.30.refs_5_.refs_1_, f32[16,256]{1,0:T(8,128)S(1)} %get-tuple-element.35.refs_6_.refs_2_, f32[16,256]{1,0:T(8,128)S(1)} %get-tuple-element.39.refs_3_, ...), custom_call_target="tpu_custom_call" | custom-call | tf_op jit(solution)/shard_map/pallas_call | solution.py:323
Async XLA Ops:
  0.6 10.9 %copy-start.2 = (s32[64]{0:T(128)S(1)}, s32[64]{0:T(128)}, u32[]{:S(2)}) copy-start(s32[64]{0:T(128)} %param.12) | copy-start | bytes 772
  1.4 10.1 %collective-permute-start.2 = (f32[16,256]{1,0:T(8,128)S(1)}, f32[16,256]{1,0:T(8,128)S(1)}, u32[]{:S(2)}, u32[]{:S(2)}) collective-permute-start(f32[16,256]{1,0:T(8,128)S(1)} %shard_map.104.opening.refs_6_), channel_id=1, source_target_pairs={{0,8},{4,12},{8,0},{12,4},{1,9},{5,13},{9,1},{13,5},{2,10},{6,14},... | collective-permute-start | bytes 49160 | tf_op jit(solution)/shard_map/ppermute | solution.py:22
  5.5 6.0 %collective-permute-start.1 = (f32[16,256]{1,0:T(8,128)S(1)}, f32[16,256]{1,0:T(8,128)S(1)}, u32[]{:S(2)}, u32[]{:S(2)}) collective-permute-start(f32[16,256]{1,0:T(8,128)S(1)} %shard_map.104.opening.refs_6_), channel_id=1, source_target_pairs={{0,12},{4,8},{8,4},{12,0},{1,13},{5,9},{9,5},{13,1},{2,14},{6,10},... | collective-permute-start | bytes 49160 | tf_op jit(solution)/shard_map/ppermute | solution.py:22
  6.8 4.7 %collective-permute-start = (f32[16,256]{1,0:T(8,128)S(1)}, f32[16,256]{1,0:T(8,128)S(1)}, u32[]{:S(2)}, u32[]{:S(2)}) collective-permute-start(f32[16,256]{1,0:T(8,128)S(1)} %shard_map.104.opening.refs_6_), channel_id=1, source_target_pairs={{0,4},{4,0},{8,12},{12,8},{1,5},{5,1},{9,13},{13,9},{2,6},{6,2},{1... | collective-permute-start | bytes 49160 | tf_op jit(solution)/shard_map/ppermute | solution.py:22
  13.6 4.1 %copy-start = (f32[16,256]{1,0:T(8,128)S(1)}, f32[16,256]{1,0:T(8,128)}, u32[]{:S(2)}) copy-start(f32[16,256]{1,0:T(8,128)} %refs_4_.5) | copy-start | bytes 49156
  13.6 4.1 %copy-start.1 = (f32[16,256]{1,0:T(8,128)S(1)}, f32[16,256]{1,0:T(8,128)}, u32[]{:S(2)}) copy-start(f32[16,256]{1,0:T(8,128)} %refs_4_.3) | copy-start | bytes 49156
  13.6 3.3 %collective-permute-start.5 = (f32[16,256]{1,0:T(8,128)S(1)}, f32[16,256]{1,0:T(8,128)S(1)}, u32[]{:S(2)}, u32[]{:S(2)}) collective-permute-start(f32[16,256]{1,0:T(8,128)S(1)} %get-tuple-element.31.part.refs_7_), channel_id=1, source_target_pairs={{0,3},{1,2},{2,1},{3,0},{4,7},{5,6},{6,5},{7,4},{8,11},{9,10},{10,... | collective-permute-start | bytes 49160 | tf_op jit(solution)/shard_map/ppermute | solution.py:22
  13.9 3.7 %collective-permute-start.4 = (f32[16,256]{1,0:T(8,128)S(1)}, f32[16,256]{1,0:T(8,128)S(1)}, u32[]{:S(2)}, u32[]{:S(2)}) collective-permute-start(f32[16,256]{1,0:T(8,128)S(1)} %get-tuple-element.31.part.refs_7_), channel_id=1, source_target_pairs={{0,2},{1,3},{2,0},{3,1},{4,6},{5,7},{6,4},{7,5},{8,10},{9,11},{10,... | collective-permute-start | bytes 49160 | tf_op jit(solution)/shard_map/ppermute | solution.py:22
  15.1 2.6 %collective-permute-start.3 = (f32[16,256]{1,0:T(8,128)S(1)}, f32[16,256]{1,0:T(8,128)S(1)}, u32[]{:S(2)}, u32[]{:S(2)}) collective-permute-start(f32[16,256]{1,0:T(8,128)S(1)} %get-tuple-element.31.part.refs_7_), channel_id=1, source_target_pairs={{0,1},{1,0},{2,3},{3,2},{4,5},{5,4},{6,7},{7,6},{8,9},{9,8},{10,11... | collective-permute-start | bytes 49160 | tf_op jit(solution)/shard_map/ppermute | solution.py:22
  19.1 4.6 %collective-permute-start.8 = (f32[16,256]{1,0:T(8,128)S(1)}, f32[16,256]{1,0:T(8,128)S(1)}, u32[]{:S(2)}, u32[]{:S(2)}) collective-permute-start(f32[16,256]{1,0:T(8,128)S(1)} %shard_map.108.refs_7_), channel_id=1, source_target_pairs={{0,8},{4,12},{8,0},{12,4},{1,9},{5,13},{9,1},{13,5},{2,10},{6,14},... | collective-permute-start | bytes 49160 | tf_op jit(solution)/shard_map/ppermute | solution.py:22
  21.7 5.5 %collective-permute-start.7 = (f32[16,256]{1,0:T(8,128)S(1)}, f32[16,256]{1,0:T(8,128)S(1)}, u32[]{:S(2)}, u32[]{:S(2)}) collective-permute-start(f32[16,256]{1,0:T(8,128)S(1)} %shard_map.108.refs_7_), channel_id=1, source_target_pairs={{0,12},{4,8},{8,4},{12,0},{1,13},{5,9},{9,5},{13,1},{2,14},{6,10},... | collective-permute-start | bytes 49160 | tf_op jit(solution)/shard_map/ppermute | solution.py:22
  23.0 4.2 %collective-permute-start.6 = (f32[16,256]{1,0:T(8,128)S(1)}, f32[16,256]{1,0:T(8,128)S(1)}, u32[]{:S(2)}, u32[]{:S(2)}) collective-permute-start(f32[16,256]{1,0:T(8,128)S(1)} %shard_map.108.refs_7_), channel_id=1, source_target_pairs={{0,4},{4,0},{8,12},{12,8},{1,5},{5,1},{9,13},{13,9},{2,6},{6,2},{1... | collective-permute-start | bytes 49160 | tf_op jit(solution)/shard_map/ppermute | solution.py:22
  28.6 3.5 %collective-permute-start.11 = (f32[24,256]{1,0:T(8,128)S(1)}, f32[24,256]{1,0:T(8,128)S(1)}, u32[]{:S(2)}, u32[]{:S(2)}) collective-permute-start(f32[24,256]{1,0:T(8,128)S(1)} %get-tuple-element.36.refs_5_), channel_id=1, source_target_pairs={{0,3},{1,2},{2,1},{3,0},{4,7},{5,6},{6,5},{7,4},{8,11},{9,10},{10,... | collective-permute-start | bytes 73736 | tf_op jit(solution)/shard_map/ppermute | solution.py:22
  28.6 3.9 %collective-permute-start.10 = (f32[24,256]{1,0:T(8,128)S(1)}, f32[24,256]{1,0:T(8,128)S(1)}, u32[]{:S(2)}, u32[]{:S(2)}) collective-permute-start(f32[24,256]{1,0:T(8,128)S(1)} %get-tuple-element.36.refs_5_), channel_id=1, source_target_pairs={{0,2},{1,3},{2,0},{3,1},{4,6},{5,7},{6,4},{7,5},{8,10},{9,11},{10,... | collective-permute-start | bytes 73736 | tf_op jit(solution)/shard_map/ppermute | solution.py:22
  30.2 2.4 %collective-permute-start.9 = (f32[24,256]{1,0:T(8,128)S(1)}, f32[24,256]{1,0:T(8,128)S(1)}, u32[]{:S(2)}, u32[]{:S(2)}) collective-permute-start(f32[24,256]{1,0:T(8,128)S(1)} %get-tuple-element.36.refs_5_), channel_id=1, source_target_pairs={{0,1},{1,0},{2,3},{3,2},{4,5},{5,4},{6,7},{7,6},{8,9},{9,8},{10,11... | collective-permute-start | bytes 73736 | tf_op jit(solution)/shard_map/ppermute | solution.py:22
  34.0 4.8 %collective-permute-start.14 = (f32[24,256]{1,0:T(8,128)S(1)}, f32[24,256]{1,0:T(8,128)S(1)}, u32[]{:S(2)}, u32[]{:S(2)}) collective-permute-start(f32[24,256]{1,0:T(8,128)S(1)} %get-tuple-element.38.refs_8_), channel_id=1, source_target_pairs={{0,8},{4,12},{8,0},{12,4},{1,9},{5,13},{9,1},{13,5},{2,10},{6,14},... | collective-permute-start | bytes 73736 | tf_op jit(solution)/shard_map/ppermute | solution.py:22
  34.7 5.7 %collective-permute-start.13 = (f32[24,256]{1,0:T(8,128)S(1)}, f32[24,256]{1,0:T(8,128)S(1)}, u32[]{:S(2)}, u32[]{:S(2)}) collective-permute-start(f32[24,256]{1,0:T(8,128)S(1)} %get-tuple-element.38.refs_8_), channel_id=1, source_target_pairs={{0,12},{4,8},{8,4},{12,0},{1,13},{5,9},{9,5},{13,1},{2,14},{6,10},... | collective-permute-start | bytes 73736 | tf_op jit(solution)/shard_map/ppermute | solution.py:22
  36.1 4.3 %collective-permute-start.12 = (f32[24,256]{1,0:T(8,128)S(1)}, f32[24,256]{1,0:T(8,128)S(1)}, u32[]{:S(2)}, u32[]{:S(2)}) collective-permute-start(f32[24,256]{1,0:T(8,128)S(1)} %get-tuple-element.38.refs_8_), channel_id=1, source_target_pairs={{0,4},{4,0},{8,12},{12,8},{1,5},{5,1},{9,13},{13,9},{2,6},{6,2},{1... | collective-permute-start | bytes 73736 | tf_op jit(solution)/shard_map/ppermute | solution.py:22
  41.9 3.5 %collective-permute-start.17 = (f32[24,256]{1,0:T(8,128)S(1)}, f32[24,256]{1,0:T(8,128)S(1)}, u32[]{:S(2)}, u32[]{:S(2)}) collective-permute-start(f32[24,256]{1,0:T(8,128)S(1)} %get-tuple-element.42.refs_7_), channel_id=1, source_target_pairs={{0,3},{1,2},{2,1},{3,0},{4,7},{5,6},{6,5},{7,4},{8,11},{9,10},{10,... | collective-permute-start | bytes 73736 | tf_op jit(solution)/shard_map/ppermute | solution.py:22
  41.9 3.9 %collective-permute-start.16 = (f32[24,256]{1,0:T(8,128)S(1)}, f32[24,256]{1,0:T(8,128)S(1)}, u32[]{:S(2)}, u32[]{:S(2)}) collective-permute-start(f32[24,256]{1,0:T(8,128)S(1)} %get-tuple-element.42.refs_7_), channel_id=1, source_target_pairs={{0,2},{1,3},{2,0},{3,1},{4,6},{5,7},{6,4},{7,5},{8,10},{9,11},{10,... | collective-permute-start | bytes 73736 | tf_op jit(solution)/shard_map/ppermute | solution.py:22
  43.4 2.4 %collective-permute-start.15 = (f32[24,256]{1,0:T(8,128)S(1)}, f32[24,256]{1,0:T(8,128)S(1)}, u32[]{:S(2)}, u32[]{:S(2)}) collective-permute-start(f32[24,256]{1,0:T(8,128)S(1)} %get-tuple-element.42.refs_7_), channel_id=1, source_target_pairs={{0,1},{1,0},{2,3},{3,2},{4,5},{5,4},{6,7},{7,6},{8,9},{9,8},{10,11... | collective-permute-start | bytes 73736 | tf_op jit(solution)/shard_map/ppermute | solution.py:22
  47.4 4.6 %collective-permute-start.18 = (f32[8,256]{1,0:T(8,128)S(1)}, f32[8,256]{1,0:T(8,128)S(1)}, u32[]{:S(2)}, u32[]{:S(2)}) collective-permute-start(f32[8,256]{1,0:T(8,128)S(1)} %get-tuple-element.45), channel_id=1, source_target_pairs={{0,8},{4,12},{8,0},{12,4},{1,9},{5,13},{9,1},{13,5},{2,10},{6,14},... | collective-permute-start | bytes 24584 | tf_op jit(solution)/shard_map/ppermute | solution.py:22
  48.9 5.5 %collective-permute-start.19 = (f32[8,256]{1,0:T(8,128)S(1)}, f32[8,256]{1,0:T(8,128)S(1)}, u32[]{:S(2)}, u32[]{:S(2)}) collective-permute-start(f32[8,256]{1,0:T(8,128)S(1)} %get-tuple-element.46), channel_id=1, source_target_pairs={{0,12},{4,8},{8,4},{12,0},{1,13},{5,9},{9,5},{13,1},{2,14},{6,10},... | collective-permute-start | bytes 24584 | tf_op jit(solution)/shard_map/ppermute | solution.py:22
  50.7 3.7 %collective-permute-start.20 = (f32[8,256]{1,0:T(8,128)S(1)}, f32[8,256]{1,0:T(8,128)S(1)}, u32[]{:S(2)}, u32[]{:S(2)}) collective-permute-start(f32[8,256]{1,0:T(8,128)S(1)} %get-tuple-element.47), channel_id=1, source_target_pairs={{0,4},{4,0},{8,12},{12,8},{1,5},{5,1},{9,13},{13,9},{2,6},{6,2},{1... | collective-permute-start | bytes 24584 | tf_op jit(solution)/shard_map/ppermute | solution.py:22

commit v3 on v0

--- a/solution.py
+++ b/solution.py
@@ -11,7 +11,7 @@
 EXTRA = 8
 LIMIT = 16 * 1024 * 1024
 GROUP = 16
-CHUNK = 16
+CHUNK = 8
 F32 = jnp.float32
 BF16 = jnp.bfloat16
 
@@ -86,14 +86,9 @@
     return jnp.concatenate(pieces, axis=0)
 
 
-def kept_tiles(codes):
-    return lambda k: (codes[k], False)
-
-
-def turned_tiles(early, late, turn=False):
-    count = early.shape[0]
-    shift = 0 if turn else count
-    return lambda k: (early[k], False) if k < count else (late[k - shift], turn)
+def kept_tiles(low, high):
+    count = low.shape[0]
+    return lambda k: (low[k], False) if k < count else (high[k - count], False)
 
 
 def pick(table, values):
@@ -116,8 +111,18 @@
     pairs[...] = jnp.concatenate([ones, ones], axis=1).astype(BF16)
 
 
+def chunk_copies(codes, first, kept, done):
+    copies = []
+    for chunk in range(kept.shape[0] // CHUNK):
+        source = codes.at[pl.ds(first + chunk * CHUNK, CHUNK)]
+        target = kept.at[pl.ds(chunk * CHUNK, CHUNK)]
+        copies.append(pltpu.make_async_copy(source, target, done.at[chunk]))
+        copies[-1].start()
+    return copies
+
+
 def loading_kernel(far_codes, opening, far_scale, far_row, *refs):
-    codes, early, rows_pick, rows_pair, wide_scale, scale, row, done, small = refs
+    low, early, rows_pick, rows_pair, wide_scale, scale, row, done, small = refs
     near = [
         pltpu.make_async_copy(far_scale, scale, small.at[0]),
         pltpu.make_async_copy(far_row, row, small.at[1]),
@@ -125,11 +130,7 @@
     for copy in near:
         copy.start()
     tiles, width = wide_scale.shape
-    copies = []
-    for chunk in range(tiles // CHUNK):
-        span = pl.ds(chunk * CHUNK, CHUNK)
-        copies.append(pltpu.make_async_copy(far_codes.at[span], codes.at[span], done.at[chunk]))
-        copies[-1].start()
+    copies = chunk_copies(far_codes, 0, low, done)
     for copy in near:
         copy.wait()
     tables(row[...], rows_pick.shape[1], rows_pick, rows_pair)
@@ -144,13 +145,15 @@
     for chunk, copy in enumerate(copies):
         copy.wait()
         for k in range(chunk * CHUNK, min((chunk + 1) * CHUNK, early.shape[0])):
-            early[k] = codes[k].T
-
-
-def turning_kernel(codes, part, late):
-    first = codes.shape[0] - late.shape[0]
+            early[k] = low[k].T
+
+
+def turning_kernel(low, high, part, late):
+    first = low.shape[0] + high.shape[0] - late.shape[0]
+    tile_of = kept_tiles(low, high)
     for k in range(late.shape[0]):
-        late[k] = codes[first + k].T
+        tile, _ = tile_of(first + k)
+        late[k] = tile.T
 
 
 def opening_kernel(start, weight, named, out, sources, weights, names, done):
@@ -173,10 +176,12 @@
 
 
 def first_kernel(blocks, slots, order, *refs):
-    codes, early, scale, rows_pair, column, place = refs[:6]
+    far_codes, low, early, scale, rows_pair, column, place = refs[:7]
     count = len(order)
-    parts = by_shift(order, refs[6 : 6 + count])
-    out, source_pick, source_pair, start, weight = refs[6 + count :]
+    parts = by_shift(order, refs[7 : 7 + count])
+    out, high, source_pick, source_pair, start, weight, done = refs[7 + count :]
+    loaded = low.shape[0]
+    copies = chunk_copies(far_codes, loaded, high, done)
     width = out.shape[1]
     here = place[0]
     columns_of = column[...]
@@ -194,17 +199,27 @@
     start[...] = field
     weight[...] = jnp.concatenate([part[blocks : 2 * blocks, :] for part in parts], axis=0)
 
-    terms = products(turned_tiles(early, codes, True), pick(source_pick[...], field.astype(BF16)))
+
+    def tile_of(k):
+        if k < early.shape[0]:
+            return early[k], False
+        if k < loaded:
+            return low[k], True
+        if (k - loaded) % CHUNK == 0:
+            copies[(k - loaded) // CHUNK].wait()
+        return high[k - loaded], True
+
+    terms = products(tile_of, pick(source_pick[...], field.astype(BF16)))
     out[...] = gather(rows_pair[...], scale[...], terms)
 
 
 def start_data_kernel(count, *refs):
-    codes, rows_pick, source_pair, scale, observed, data_weight, late = refs[:7]
-    parts = refs[7 : 7 + count]
-    out = refs[7 + count]
+    low, high, rows_pick, source_pair, scale, observed, data_weight, late = refs[:8]
+    parts = refs[8 : 8 + count]
+    out = refs[8 + count]
     total = total_rows(parts)
     data = (data_weight[...] * (observed[...] - total)).astype(BF16)
-    terms = products(kept_tiles(codes), pick(rows_pick[...], data))
+    terms = products(kept_tiles(low, high), pick(rows_pick[...], data))
     out[...] = gather(source_pair[...], scale[...], terms)
 
 
@@ -216,7 +231,7 @@
     weights = weight[...]
     value = total_blocks(parts, blocks) - weights * start[...]
     residual[...] = value
-    terms = products(turned_tiles(early, late), pick(source_pick[...], value.astype(BF16)))
+    terms = products(kept_tiles(early, late), pick(source_pick[...], value.astype(BF16)))
     data_rows = rows_pair.shape[0]
     out[:data_rows, :] = gather(rows_pair[...], scale[...], terms)
     out[data_rows:, :] = pack_rows(
@@ -225,16 +240,16 @@
 
 
 def image_data_kernel(count, *refs):
-    codes, rows_pick, source_pair, scale, data_weight = refs[:5]
-    parts = refs[5 : 5 + count]
-    out, predicted, sums = refs[5 + count :]
+    low, high, rows_pick, source_pair, scale, data_weight = refs[:6]
+    parts = refs[6 : 6 + count]
+    out, predicted, sums = refs[6 + count :]
     data_rows = data_weight.shape[0]
     whole_part = total_rows(parts)
     total = whole_part[:data_rows, :]
     predicted[...] = total
     sums[...] = whole_part[data_rows:, :]
     data = (data_weight[...] * (0.0 - total)).astype(BF16)
-    terms = products(kept_tiles(codes), pick(rows_pick[...], data))
+    terms = products(kept_tiles(low, high), pick(rows_pick[...], data))
     cells = source_pair.shape[0]
     out[:cells, :] = gather(source_pair[...], scale[...], terms)
     out[cells:, :] = pack_rows([columns(total * data.astype(F32))], total.shape[1])
@@ -254,7 +269,7 @@
     step[...] = jnp.broadcast_to(alpha, step.shape)
     value = residual_of(along, alpha, image)
     residual[...] = value
-    terms = products(turned_tiles(early, late), pick(source_pick[...], value.astype(BF16)))
+    terms = products(kept_tiles(early, late), pick(source_pick[...], value.astype(BF16)))
     data_rows = rows_pair.shape[0]
     out[:data_rows, :] = gather(rows_pair[...], scale[...], terms)
     weighted = value * weights
@@ -269,9 +284,9 @@
 
 
 def second_data_kernel(blocks, count, *refs):
-    codes, rows_pick, source_pair, scale, data_weight, predicted, sums = refs[:7]
-    parts = refs[7 : 7 + count]
-    outs, scalars = refs[7 + count : -1], refs[-1]
+    low, high, rows_pick, source_pair, scale, data_weight, predicted, sums = refs[:8]
+    parts = refs[8 : 8 + count]
+    outs, scalars = refs[8 + count : -1], refs[-1]
     data_rows = data_weight.shape[0]
     whole_part = total_rows(parts)
     norm = whole(whole_part[data_rows : data_rows + 1, :])
@@ -283,7 +298,7 @@
     )
     total = whole_part[:data_rows, :] + beta * predicted[...]
     data = (data_weight[...] * (0.0 - total)).astype(BF16)
-    terms = products(kept_tiles(codes), pick(rows_pick[...], data))
+    terms = products(kept_tiles(low, high), pick(rows_pick[...], data))
     cells = gather(source_pair[...], scale[...], terms)
     curved = columns(total * data.astype(F32))
     for group, out in enumerate(outs):
@@ -346,6 +361,9 @@
     count = lax.axis_size("tiles")
     sharing = lax.axis_size(("split", "depth"))
     cells = count * blocks
+    late_tiles = tiles // 2
+    loaded = tiles * 5 // 8
+    codes = pltpu.with_memory_space_constraint(tile_codes, pltpu.HBM)
     place = lax.axis_index("tiles").astype(jnp.int32).reshape(1)
 
     order = [0] + sorted(range(1, count), key=lambda shift: (shift != 1, -abs(2 * shift - count)))
@@ -372,49 +390,53 @@
         ],
     )
     begin = across([opening] * count)
-    codes, early, rows_pick, rows_pair, scale = call(
+    low, early, rows_pick, rows_pair, scale = call(
         loading_kernel,
         [
-            (tile_codes.shape, BF16),
-            ((tiles - CHUNK, width, width), BF16),
+            ((loaded, width, width), BF16),
+            ((tiles - late_tiles, width, width), BF16),
             ((tiles, data_rows), BF16),
             ((data_rows, 2 * tiles), BF16),
             ((tiles, width), F32),
         ],
-        pltpu.with_memory_space_constraint(tile_codes, pltpu.HBM),
+        codes,
         opening,
         pltpu.with_memory_space_constraint(tile_scale.reshape(1, -1), pltpu.HBM),
         pltpu.with_memory_space_constraint(tile_row.reshape(1, -1), pltpu.HBM),
         scratch=[
             pltpu.VMEM((1, tiles), F32),
             pltpu.VMEM((1, tiles), jnp.int32),
-            pltpu.SemaphoreType.DMA((tiles // CHUNK,)),
+            pltpu.SemaphoreType.DMA((loaded // CHUNK,)),
             pltpu.SemaphoreType.DMA((2,)),
         ],
     )
-    part, source_pick, source_pair, start, weight = call(
+    part, high, source_pick, source_pair, start, weight = call(
         functools.partial(first_kernel, blocks, slots, order),
         [
             ((data_rows, width), F32),
+            ((tiles - loaded, width, width), BF16),
             ((tiles, cells), BF16),
             ((cells, 2 * tiles), BF16),
             ((cells, width), F32),
             ((cells, width), F32),
         ],
         codes,
+        low,
         early,
         scale,
         rows_pair,
         tile_column.reshape(1, -1),
         place,
         *begin,
+        scratch=[pltpu.SemaphoreType.DMA(((tiles - loaded) // CHUNK,))],
     )
     parts = within(part)
-    (late,) = call(turning_kernel, [((CHUNK, width, width), BF16)], codes, part)
+    (late,) = call(turning_kernel, [((late_tiles, width, width), BF16)], low, high, part)
     (part,) = call(
         functools.partial(start_data_kernel, sharing),
         [((cells, width), F32)],
-        codes,
+        low,
+        high,
         rows_pick,
         source_pair,
         scale,
@@ -438,7 +460,8 @@
     part, predicted, sums = call(
         functools.partial(image_data_kernel, sharing),
         [((cells + EXTRA, width), F32), ((data_rows, width), F32), ((EXTRA, width), F32)],
-        codes,
+        low,
+        high,
         rows_pick,
         source_pair,
         scale,
@@ -461,7 +484,8 @@
     *part, scalars = call(
         functools.partial(second_data_kernel, blocks, sharing),
         [((blocks + 4, width), F32)] * count + [((EXTRA, width), F32)],
-        codes,
+        low,
+        high,
         rows_pick,
         source_pair,
         scale,

time: 55.4 us -> 55.8 us (level)
  Pallas kernels: 15.9 us -> 16.8 us
    pallas_call x10, Pallas kernels: 15.9 us -> 16.8 us  [call(): pl.pallas_call(body, out_shape=[jax.ShapeDtypeStruct(shape, dtype) for sh...]
  transfers between devices with their start and end apart: 21 -> 21, of which waited for: 13 -> 14; matrix products, arithmetic and copies ran while one was open for 0% -> 0% of each run, Pallas kernels for 9% -> 8%
where the time goes in v3:
time: 55.8 us; the launch traced here: 55.6 us
  starting transfers between devices  22.1 us (40%)
  Pallas kernels  16.8 us (30%)
  waiting for transfers between devices  15.9 us (28%)
  between operations  0.71 us (1%)
    ppermute x21, starting transfers between devices, exchange(): parts[shift] = lax.ppermute(values[shift], axes, perm)  22.1 us
    pallas_call x10, Pallas kernels, call(): pl.pallas_call(body, out_shape=[jax.ShapeDtypeStruct(shape, dtype) for sh...  16.8 us
    ppermute x21, waiting for transfers between devices, exchange(): parts[shift] = lax.ppermute(values[shift], axes, perm)  15.9 us
  transfers between devices with their start and end apart: 21, of which 14 were waited for; matrix products, arithmetic and copies ran while one was open for 0% of the time, Pallas kernels for 8%

profile of v3, /device:TPU:0, one launch (start us, length us, event | category | flops | bytes accessed | tf_op | source)
XLA Modules:
  0.0 55.6 jit_solution(10477340720634230032)
XLA Ops:
  0.6 0.7 %shard_map.104.opening.refs_7_ = f32[16,256]{1,0:T(8,128)S(1)} custom-call(f32[4,256]{1,0:T(4,128)} %start.1, f32[4,256]{1,0:T(4,128)} %weight.1, s32[2,4]{1,0:T(2,128)} %bitcast.8), custom_call_target="tpu_custom_call" | custom-call | tf_op jit(solution)/shard_map/pallas_call | solution.py:336
  1.4 4.1 %collective-permute-start.2 = (f32[16,256]{1,0:T(8,128)S(1)}, f32[16,256]{1,0:T(8,128)S(1)}, u32[]{:S(2)}, u32[]{:S(2)}) collective-permute-start(f32[16,256]{1,0:T(8,128)S(1)} %shard_map.104.opening.refs_7_), channel_id=1, source_target_pairs={{0,8},{4,12},{8,0},{12,4},{1,9},{5,13},{9,1},{13,5},{2,10},{6,14},... | collective-permute-start | bytes 49160 | tf_op jit(solution)/shard_map/ppermute | solution.py:23
  5.5 1.3 %collective-permute-start.1 = (f32[16,256]{1,0:T(8,128)S(1)}, f32[16,256]{1,0:T(8,128)S(1)}, u32[]{:S(2)}, u32[]{:S(2)}) collective-permute-start(f32[16,256]{1,0:T(8,128)S(1)} %shard_map.104.opening.refs_7_), channel_id=1, source_target_pairs={{0,12},{4,8},{8,4},{12,0},{1,13},{5,9},{9,5},{13,1},{2,14},{6,10},... | collective-permute-start | bytes 49160 | tf_op jit(solution)/shard_map/ppermute | solution.py:23
  6.8 0.2 collective-permute-start
  7.1 0.0 copy-start.2
  7.1 3.5 %shard_map.105 = (bf16[40,256,256]{2,1,0:T(8,128)(2,1)S(1)}, bf16[32,256,256]{2,1,0:T(8,128)(2,1)S(1)}, bf16[64,16]{1,0:T(8,128)(2,1)S(1)}, bf16[16,128]{1,0:T(8,128)(2,1)S(1)}, f32[64,256]{1,0:T(8,128)S(1)}) custom-call(bf16[64,256,256]{2,1,0:T(8,128)(2,1)} %refs_0_.1, f32[16,256]{1,0:T(8,128)S(1)} %shard_map.104.opening.refs_7_, f32[1,64]{1,0:T(1,128)} %bitcast.9, ...), custom_call_target="tpu_custom_call" | custom-call | tf_op jit(solution)/shard_map/pallas_call | solution.py:336
  10.6 0.0 collective-permute-done.2.refs_10_
  10.6 0.4 collective-permute-done.1.refs_9_
  11.0 0.0 collective-permute-done.refs_8_
  11.0 0.0 copy-done.2
  11.0 3.3 %shard_map.106 = (f32[16,256]{1,0:T(8,128)S(1)}, bf16[24,256,256]{2,1,0:T(8,128)(2,1)S(1)}, bf16[64,16]{1,0:T(8,128)(2,1)S(1)}, bf16[16,128]{1,0:T(8,128)(2,1)S(...) custom-call(bf16[64,256,256]{2,1,0:T(8,128)(2,1)} %refs_0_.1, ...), custom_call_target="tpu_custom_call" | custom-call | tf_op jit(solution)/shard_map/pallas_call | solution.py:336
  14.3 0.1 collective-permute-start.5
  14.4 1.6 %collective-permute-start.4 = (f32[16,256]{1,0:T(8,128)S(1)}, f32[16,256]{1,0:T(8,128)S(1)}, u32[]{:S(2)}, u32[]{:S(2)}) collective-permute-start(f32[16,256]{1,0:T(8,128)S(1)} %get-tuple-element.33.part.refs_8_), channel_id=1, source_target_pairs={{0,2},{1,3},{2,0},{3,1},{4,6},{5,7},{6,4},{7,5},{8,10},{9,11},{10,... | collective-permute-start | bytes 49160 | tf_op jit(solution)/shard_map/ppermute | solution.py:23
  16.0 0.3 collective-permute-start.3
  16.2 0.0 copy-start
  16.2 0.0 copy-start.1
  16.3 1.1 %shard_map.107.refs_7_.refs_1_ = bf16[32,256,256]{2,1,0:T(8,128)(2,1)S(1)} custom-call(bf16[40,256,256]{2,1,0:T(8,128)(2,1)S(1)} %get-tuple-element.26.refs_1_.low.refs_0_, bf16[24,256,256]{2,1,0:T(8,128)(2,1)S(1)} %get-tuple-element.32.high.refs_1_, f32[16,256]{1,0:T(8,128)S(1)} %get-tuple-element.33.part.refs_8_), custom_call_target="tpu_custom_call" | custom-call | tf_op jit(solution)/shard_map/pallas_call | solution.py:336
  17.4 0.3 collective-permute-done.5.refs_11_
  17.7 0.5 collective-permute-done.4.refs_10_
  18.2 0.0 collective-permute-done.3.refs_9_
  18.2 0.0 copy-done
  18.2 0.0 copy-done.1
  18.2 1.4 %shard_map.108.refs_7_ = f32[16,256]{1,0:T(8,128)S(1)} custom-call(bf16[40,256,256]{2,1,0:T(8,128)(2,1)S(1)} %get-tuple-element.26.refs_1_.low.refs_0_, bf16[24,256,256]{2,1,0:T(8,128)(2,1)S(1)} %get-tuple-element.32.high.refs_1_, bf16[64,16]{1,0:T(8,128)(2,1)S(1)} %get-tuple-element.35.refs_2_, bf16[16,128]{1,0:T(8,128)(2,1)S(1)} %get-tuple-element.36.refs_3_, ...), custom_call_target="tpu_custom_call" | custom-call | tf_op jit(solution)/shard_map/pallas_call | solution.py:336
  19.6 2.4 %collective-permute-start.8 = (f32[16,256]{1,0:T(8,128)S(1)}, f32[16,256]{1,0:T(8,128)S(1)}, u32[]{:S(2)}, u32[]{:S(2)}) collective-permute-start(f32[16,256]{1,0:T(8,128)S(1)} %shard_map.108.refs_7_), channel_id=1, source_target_pairs={{0,8},{4,12},{8,0},{12,4},{1,9},{5,13},{9,1},{13,5},{2,10},{6,14},... | collective-permute-start | bytes 49160 | tf_op jit(solution)/shard_map/ppermute | solution.py:23
  22.1 1.4 %collective-permute-start.7 = (f32[16,256]{1,0:T(8,128)S(1)}, f32[16,256]{1,0:T(8,128)S(1)}, u32[]{:S(2)}, u32[]{:S(2)}) collective-permute-start(f32[16,256]{1,0:T(8,128)S(1)} %shard_map.108.refs_7_), channel_id=1, source_target_pairs={{0,12},{4,8},{8,4},{12,0},{1,13},{5,9},{9,5},{13,1},{2,14},{6,10},... | collective-permute-start | bytes 49160 | tf_op jit(solution)/shard_map/ppermute | solution.py:23
  23.4 0.0 collective-permute-start.6
  23.4 0.9 %collective-permute-done.8.refs_10_ = f32[16,256]{1,0:T(8,128)S(1)} collective-permute-done((f32[16,256]{1,0:T(8,128)S(1)}, f32[16,256]{1,0:T(8,128)S(1)}, u32[]{:S(2)}, u32[]{:S(2)}) %collective-permute-start.8) | collective-permute-done | bytes 16416 | tf_op jit(solution)/shard_map/ppermute | solution.py:23
  24.3 3.3 %collective-permute-done.7.refs_9_ = f32[16,256]{1,0:T(8,128)S(1)} collective-permute-done((f32[16,256]{1,0:T(8,128)S(1)}, f32[16,256]{1,0:T(8,128)S(1)}, u32[]{:S(2)}, u32[]{:S(2)}) %collective-permute-start.7) | collective-permute-done | bytes 16416 | tf_op jit(solution)/shard_map/ppermute | solution.py:23
  27.6 0.0 collective-permute-done.6.refs_8_
  27.6 1.4 %shard_map.109 = (f32[24,256]{1,0:T(8,128)S(1)}, f32[16,256]{1,0:T(8,128)S(1)}) custom-call(bf16[32,256,256]{2,1,0:T(8,128)(2,1)S(1)} %get-tuple-element.27.refs_2_.refs_0_, bf16[32,256,256]{2,1,0:T(8,128)(2,1)S(1)} %shard_map.107.refs_7_.refs_1_, bf16[64,16]{1,0:T(8,128)(2,1)S(1)} %get-tuple-element.34.refs_2_, ...), custom_call_target="tpu_custom_call" | custom-call | tf_op jit(solution)/shard_map/pallas_call | solution.py:336
  29.0 0.0 collective-permute-start.11
  29.0 1.5 %collective-permute-start.10 = (f32[24,256]{1,0:T(8,128)S(1)}, f32[24,256]{1,0:T(8,128)S(1)}, u32[]{:S(2)}, u32[]{:S(2)}) collective-permute-start(f32[24,256]{1,0:T(8,128)S(1)} %get-tuple-element.38.refs_6_), channel_id=1, source_target_pairs={{0,2},{1,3},{2,0},{3,1},{4,6},{5,7},{6,4},{7,5},{8,10},{9,11},{10,... | collective-permute-start | bytes 73736 | tf_op jit(solution)/shard_map/ppermute | solution.py:23
  30.6 0.3 collective-permute-start.9
  30.9 1.6 %collective-permute-done.11.refs_9_ = f32[24,256]{1,0:T(8,128)S(1)} collective-permute-done((f32[24,256]{1,0:T(8,128)S(1)}, f32[24,256]{1,0:T(8,128)S(1)}, u32[]{:S(2)}, u32[]{:S(2)}) %collective-permute-start.11) | collective-permute-done | bytes 24608 | tf_op jit(solution)/shard_map/ppermute | solution.py:23
  32.5 0.4 collective-permute-done.10.refs_8_
  32.9 0.0 collective-permute-done.9.refs_7_
  32.9 1.4 %shard_map.110 = (f32[24,256]{1,0:T(8,128)S(1)}, f32[16,256]{1,0:T(8,128)S(1)}, f32[8,256]{1,0:T(8,128)S(1)}) custom-call(bf16[40,256,256]{2,1,0:T(8,128)(2,1)S(1)} %get-tuple-element.26.refs_1_.low.refs_0_, bf16[24,256,256]{2,1,0:T(8,128)(2,1)S(1)} %get-tuple-element.32.high.refs_1_, bf16[64,16]{1,0:T(8,128)(2,1)S(1)} %get-tuple-element.35.refs_2_, ...), custom_call_target="tpu_custom_call" | custom-call | tf_op jit(solution)/shard_map/pallas_call | solution.py:336
  34.4 0.8 %collective-permute-start.14 = (f32[24,256]{1,0:T(8,128)S(1)}, f32[24,256]{1,0:T(8,128)S(1)}, u32[]{:S(2)}, u32[]{:S(2)}) collective-permute-start(f32[24,256]{1,0:T(8,128)S(1)} %get-tuple-element.40.refs_8_), channel_id=1, source_target_pairs={{0,8},{4,12},{8,0},{12,4},{1,9},{5,13},{9,1},{13,5},{2,10},{6,14},... | collective-permute-start | bytes 73736 | tf_op jit(solution)/shard_map/ppermute | solution.py:23
  35.1 1.4 %collective-permute-start.13 = (f32[24,256]{1,0:T(8,128)S(1)}, f32[24,256]{1,0:T(8,128)S(1)}, u32[]{:S(2)}, u32[]{:S(2)}) collective-permute-start(f32[24,256]{1,0:T(8,128)S(1)} %get-tuple-element.40.refs_8_), channel_id=1, source_target_pairs={{0,12},{4,8},{8,4},{12,0},{1,13},{5,9},{9,5},{13,1},{2,14},{6,10},... | collective-permute-start | bytes 73736 | tf_op jit(solution)/shard_map/ppermute | solution.py:23
  36.5 1.4 %collective-permute-start.12 = (f32[24,256]{1,0:T(8,128)S(1)}, f32[24,256]{1,0:T(8,128)S(1)}, u32[]{:S(2)}, u32[]{:S(2)}) collective-permute-start(f32[24,256]{1,0:T(8,128)S(1)} %get-tuple-element.40.refs_8_), channel_id=1, source_target_pairs={{0,4},{4,0},{8,12},{12,8},{1,5},{5,1},{9,13},{13,9},{2,6},{6,2},{1... | collective-permute-start | bytes 73736 | tf_op jit(solution)/shard_map/ppermute | solution.py:23
  37.9 1.3 %collective-permute-done.14.refs_11_ = f32[24,256]{1,0:T(8,128)S(1)} collective-permute-done((f32[24,256]{1,0:T(8,128)S(1)}, f32[24,256]{1,0:T(8,128)S(1)}, u32[]{:S(2)}, u32[]{:S(2)}) %collective-permute-start.14) | collective-permute-done | bytes 24608 | tf_op jit(solution)/shard_map/ppermute | solution.py:23
  39.1 1.7 %collective-permute-done.13.refs_10_ = f32[24,256]{1,0:T(8,128)S(1)} collective-permute-done((f32[24,256]{1,0:T(8,128)S(1)}, f32[24,256]{1,0:T(8,128)S(1)}, u32[]{:S(2)}, u32[]{:S(2)}) %collective-permute-start.13) | collective-permute-done | bytes 24608 | tf_op jit(solution)/shard_map/ppermute | solution.py:23
  40.8 0.0 collective-permute-done.12.refs_9_
  40.8 1.5 %shard_map.111 = (f32[24,256]{1,0:T(8,128)S(1)}, f32[16,256]{1,0:T(8,128)S(1)}, f32[8,128]{1,0:T(8,128)S(1)}) custom-call(bf16[32,256,256]{2,1,0:T(8,128)(2,1)S(1)} %get-tuple-element.27.refs_2_.refs_0_, bf16[32,256,256]{2,1,0:T(8,128)(2,1)S(1)} %shard_map.107.refs_7_.refs_1_, bf16[64,16]{1,0:T(8,128)(2,1)S(1)} %get-tuple-element.34.refs_2_, ...), custom_call_target="tpu_custom_call" | custom-call | tf_op jit(solution)/shard_map/pallas_call | solution.py:336
  42.3 0.0 collective-permute-start.17
  42.3 1.5 %collective-permute-start.16 = (f32[24,256]{1,0:T(8,128)S(1)}, f32[24,256]{1,0:T(8,128)S(1)}, u32[]{:S(2)}, u32[]{:S(2)}) collective-permute-start(f32[24,256]{1,0:T(8,128)S(1)} %get-tuple-element.44.refs_8_), channel_id=1, source_target_pairs={{0,2},{1,3},{2,0},{3,1},{4,6},{5,7},{6,4},{7,5},{8,10},{9,11},{10,... | collective-permute-start | bytes 73736 | tf_op jit(solution)/shard_map/ppermute | solution.py:23
  43.8 0.4 collective-permute-start.15
  44.2 1.6 %collective-permute-done.17.refs_11_ = f32[24,256]{1,0:T(8,128)S(1)} collective-permute-done((f32[24,256]{1,0:T(8,128)S(1)}, f32[24,256]{1,0:T(8,128)S(1)}, u32[]{:S(2)}, u32[]{:S(2)}) %collective-permute-start.17) | collective-permute-done | bytes 24608 | tf_op jit(solution)/shard_map/ppermute | solution.py:23
  45.8 0.4 collective-permute-done.16.refs_10_
  46.2 0.0 collective-permute-done.15.refs_9_
  46.2 1.6 %shard_map.112 = (f32[8,256]{1,0:T(8,128)S(1)}, f32[8,256]{1,0:T(8,128)S(1)}, f32[8,256]{1,0:T(8,128)S(1)}, f32[8,256]{1,0:T(8,128)S(1)}, f32[8,256]{1,0:T(8,128)S(1)}) custom-call(bf16[40,256,256]{2,1,0:T(8,128)(2,1)S(1)} %get-tuple-element.26.refs_1_.low.refs_0_, bf16[24,256,256]{2,1,0:T(8,128)(2,1)S(1)} %get-tuple-element.32.high.refs_1_, ...), custom_call_target="tpu_custom_call" | custom-call | tf_op jit(solution)/shard_map/pallas_call | solution.py:336
  47.8 1.5 %collective-permute-start.18 = (f32[8,256]{1,0:T(8,128)S(1)}, f32[8,256]{1,0:T(8,128)S(1)}, u32[]{:S(2)}, u32[]{:S(2)}) collective-permute-start(f32[8,256]{1,0:T(8,128)S(1)} %get-tuple-element.47), channel_id=1, source_target_pairs={{0,8},{4,12},{8,0},{12,4},{1,9},{5,13},{9,1},{13,5},{2,10},{6,14},... | collective-permute-start | bytes 24584 | tf_op jit(solution)/shard_map/ppermute | solution.py:23
  49.3 1.8 %collective-permute-start.19 = (f32[8,256]{1,0:T(8,128)S(1)}, f32[8,256]{1,0:T(8,128)S(1)}, u32[]{:S(2)}, u32[]{:S(2)}) collective-permute-start(f32[8,256]{1,0:T(8,128)S(1)} %get-tuple-element.48), channel_id=1, source_target_pairs={{0,12},{4,8},{8,4},{12,0},{1,13},{5,9},{9,5},{13,1},{2,14},{6,10},... | collective-permute-start | bytes 24584 | tf_op jit(solution)/shard_map/ppermute | solution.py:23
  51.1 0.2 collective-permute-start.20
  51.3 1.1 %collective-permute-done.18.refs_7_ = f32[8,256]{1,0:T(8,128)S(1)} collective-permute-done((f32[8,256]{1,0:T(8,128)S(1)}, f32[8,256]{1,0:T(8,128)S(1)}, u32[]{:S(2)}, u32[]{:S(2)}) %collective-permute-start.18) | collective-permute-done | bytes 8224 | tf_op jit(solution)/shard_map/ppermute | solution.py:23
  52.3 2.4 %collective-permute-done.19.refs_8_ = f32[8,256]{1,0:T(8,128)S(1)} collective-permute-done((f32[8,256]{1,0:T(8,128)S(1)}, f32[8,256]{1,0:T(8,128)S(1)}, u32[]{:S(2)}, u32[]{:S(2)}) %collective-permute-start.19) | collective-permute-done | bytes 8224 | tf_op jit(solution)/shard_map/ppermute | solution.py:23
  54.7 0.1 collective-permute-done.20.refs_9_
  54.8 0.8 %shard_map.113 = (f32[4,256]{1,0:T(4,128)}, f32[4,256]{1,0:T(4,128)}) custom-call(f32[16,256]{1,0:T(8,128)S(1)} %get-tuple-element.30.refs_6_.refs_5_.refs_0_, f32[16,256]{1,0:T(8,128)S(1)} %get-tuple-element.31.refs_5_.refs_1_, f32[16,256]{1,0:T(8,128)S(1)} %get-tuple-element.37.refs_6_.refs_2_, f32[16,256]{1,0:T(8,128)S(1)} %get-tuple-element.41.refs_3_, ...), custom_call_target="tpu_custom_call" | custom-call | tf_op jit(solution)/shard_map/pallas_call | solution.py:336
Async XLA Ops:
  1.4 9.2 %collective-permute-start.2 = (f32[16,256]{1,0:T(8,128)S(1)}, f32[16,256]{1,0:T(8,128)S(1)}, u32[]{:S(2)}, u32[]{:S(2)}) collective-permute-start(f32[16,256]{1,0:T(8,128)S(1)} %shard_map.104.opening.refs_7_), channel_id=1, source_target_pairs={{0,8},{4,12},{8,0},{12,4},{1,9},{5,13},{9,1},{13,5},{2,10},{6,14},... | collective-permute-start | bytes 49160 | tf_op jit(solution)/shard_map/ppermute | solution.py:23
  5.5 5.5 %collective-permute-start.1 = (f32[16,256]{1,0:T(8,128)S(1)}, f32[16,256]{1,0:T(8,128)S(1)}, u32[]{:S(2)}, u32[]{:S(2)}) collective-permute-start(f32[16,256]{1,0:T(8,128)S(1)} %shard_map.104.opening.refs_7_), channel_id=1, source_target_pairs={{0,12},{4,8},{8,4},{12,0},{1,13},{5,9},{9,5},{13,1},{2,14},{6,10},... | collective-permute-start | bytes 49160 | tf_op jit(solution)/shard_map/ppermute | solution.py:23
  6.8 4.2 %collective-permute-start = (f32[16,256]{1,0:T(8,128)S(1)}, f32[16,256]{1,0:T(8,128)S(1)}, u32[]{:S(2)}, u32[]{:S(2)}) collective-permute-start(f32[16,256]{1,0:T(8,128)S(1)} %shard_map.104.opening.refs_7_), channel_id=1, source_target_pairs={{0,4},{4,0},{8,12},{12,8},{1,5},{5,1},{9,13},{13,9},{2,6},{6,2},{1... | collective-permute-start | bytes 49160 | tf_op jit(solution)/shard_map/ppermute | solution.py:23
  7.1 4.0 %copy-start.2 = (s32[64]{0:T(128)S(1)}, s32[64]{0:T(128)}, u32[]{:S(2)}) copy-start(s32[64]{0:T(128)} %param.12) | copy-start | bytes 772
  14.3 3.4 %collective-permute-start.5 = (f32[16,256]{1,0:T(8,128)S(1)}, f32[16,256]{1,0:T(8,128)S(1)}, u32[]{:S(2)}, u32[]{:S(2)}) collective-permute-start(f32[16,256]{1,0:T(8,128)S(1)} %get-tuple-element.33.part.refs_8_), channel_id=1, source_target_pairs={{0,3},{1,2},{2,1},{3,0},{4,7},{5,6},{6,5},{7,4},{8,11},{9,10},{10,... | collective-permute-start | bytes 49160 | tf_op jit(solution)/shard_map/ppermute | solution.py:23
  14.4 3.8 %collective-permute-start.4 = (f32[16,256]{1,0:T(8,128)S(1)}, f32[16,256]{1,0:T(8,128)S(1)}, u32[]{:S(2)}, u32[]{:S(2)}) collective-permute-start(f32[16,256]{1,0:T(8,128)S(1)} %get-tuple-element.33.part.refs_8_), channel_id=1, source_target_pairs={{0,2},{1,3},{2,0},{3,1},{4,6},{5,7},{6,4},{7,5},{8,10},{9,11},{10,... | collective-permute-start | bytes 49160 | tf_op jit(solution)/shard_map/ppermute | solution.py:23
  16.0 2.3 %collective-permute-start.3 = (f32[16,256]{1,0:T(8,128)S(1)}, f32[16,256]{1,0:T(8,128)S(1)}, u32[]{:S(2)}, u32[]{:S(2)}) collective-permute-start(f32[16,256]{1,0:T(8,128)S(1)} %get-tuple-element.33.part.refs_8_), channel_id=1, source_target_pairs={{0,1},{1,0},{2,3},{3,2},{4,5},{5,4},{6,7},{7,6},{8,9},{9,8},{10,11... | collective-permute-start | bytes 49160 | tf_op jit(solution)/shard_map/ppermute | solution.py:23
  16.2 2.0 %copy-start = (f32[16,256]{1,0:T(8,128)S(1)}, f32[16,256]{1,0:T(8,128)}, u32[]{:S(2)}) copy-start(f32[16,256]{1,0:T(8,128)} %refs_5_.5) | copy-start | bytes 49156
  16.2 2.0 %copy-start.1 = (f32[16,256]{1,0:T(8,128)S(1)}, f32[16,256]{1,0:T(8,128)}, u32[]{:S(2)}) copy-start(f32[16,256]{1,0:T(8,128)} %refs_5_.3) | copy-start | bytes 49156
  19.6 4.7 %collective-permute-start.8 = (f32[16,256]{1,0:T(8,128)S(1)}, f32[16,256]{1,0:T(8,128)S(1)}, u32[]{:S(2)}, u32[]{:S(2)}) collective-permute-start(f32[16,256]{1,0:T(8,128)S(1)} %shard_map.108.refs_7_), channel_id=1, source_target_pairs={{0,8},{4,12},{8,0},{12,4},{1,9},{5,13},{9,1},{13,5},{2,10},{6,14},... | collective-permute-start | bytes 49160 | tf_op jit(solution)/shard_map/ppermute | solution.py:23
  22.1 5.5 %collective-permute-start.7 = (f32[16,256]{1,0:T(8,128)S(1)}, f32[16,256]{1,0:T(8,128)S(1)}, u32[]{:S(2)}, u32[]{:S(2)}) collective-permute-start(f32[16,256]{1,0:T(8,128)S(1)} %shard_map.108.refs_7_), channel_id=1, source_target_pairs={{0,12},{4,8},{8,4},{12,0},{1,13},{5,9},{9,5},{13,1},{2,14},{6,10},... | collective-permute-start | bytes 49160 | tf_op jit(solution)/shard_map/ppermute | solution.py:23
  23.4 4.2 %collective-permute-start.6 = (f32[16,256]{1,0:T(8,128)S(1)}, f32[16,256]{1,0:T(8,128)S(1)}, u32[]{:S(2)}, u32[]{:S(2)}) collective-permute-start(f32[16,256]{1,0:T(8,128)S(1)} %shard_map.108.refs_7_), channel_id=1, source_target_pairs={{0,4},{4,0},{8,12},{12,8},{1,5},{5,1},{9,13},{13,9},{2,6},{6,2},{1... | collective-permute-start | bytes 49160 | tf_op jit(solution)/shard_map/ppermute | solution.py:23
  29.0 3.5 %collective-permute-start.11 = (f32[24,256]{1,0:T(8,128)S(1)}, f32[24,256]{1,0:T(8,128)S(1)}, u32[]{:S(2)}, u32[]{:S(2)}) collective-permute-start(f32[24,256]{1,0:T(8,128)S(1)} %get-tuple-element.38.refs_6_), channel_id=1, source_target_pairs={{0,3},{1,2},{2,1},{3,0},{4,7},{5,6},{6,5},{7,4},{8,11},{9,10},{10,... | collective-permute-start | bytes 73736 | tf_op jit(solution)/shard_map/ppermute | solution.py:23
  29.0 3.9 %collective-permute-start.10 = (f32[24,256]{1,0:T(8,128)S(1)}, f32[24,256]{1,0:T(8,128)S(1)}, u32[]{:S(2)}, u32[]{:S(2)}) collective-permute-start(f32[24,256]{1,0:T(8,128)S(1)} %get-tuple-element.38.refs_6_), channel_id=1, source_target_pairs={{0,2},{1,3},{2,0},{3,1},{4,6},{5,7},{6,4},{7,5},{8,10},{9,11},{10,... | collective-permute-start | bytes 73736 | tf_op jit(solution)/shard_map/ppermute | solution.py:23
  30.6 2.4 %collective-permute-start.9 = (f32[24,256]{1,0:T(8,128)S(1)}, f32[24,256]{1,0:T(8,128)S(1)}, u32[]{:S(2)}, u32[]{:S(2)}) collective-permute-start(f32[24,256]{1,0:T(8,128)S(1)} %get-tuple-element.38.refs_6_), channel_id=1, source_target_pairs={{0,1},{1,0},{2,3},{3,2},{4,5},{5,4},{6,7},{7,6},{8,9},{9,8},{10,11... | collective-permute-start | bytes 73736 | tf_op jit(solution)/shard_map/ppermute | solution.py:23
  34.4 4.8 %collective-permute-start.14 = (f32[24,256]{1,0:T(8,128)S(1)}, f32[24,256]{1,0:T(8,128)S(1)}, u32[]{:S(2)}, u32[]{:S(2)}) collective-permute-start(f32[24,256]{1,0:T(8,128)S(1)} %get-tuple-element.40.refs_8_), channel_id=1, source_target_pairs={{0,8},{4,12},{8,0},{12,4},{1,9},{5,13},{9,1},{13,5},{2,10},{6,14},... | collective-permute-start | bytes 73736 | tf_op jit(solution)/shard_map/ppermute | solution.py:23
  35.1 5.7 %collective-permute-start.13 = (f32[24,256]{1,0:T(8,128)S(1)}, f32[24,256]{1,0:T(8,128)S(1)}, u32[]{:S(2)}, u32[]{:S(2)}) collective-permute-start(f32[24,256]{1,0:T(8,128)S(1)} %get-tuple-element.40.refs_8_), channel_id=1, source_target_pairs={{0,12},{4,8},{8,4},{12,0},{1,13},{5,9},{9,5},{13,1},{2,14},{6,10},... | collective-permute-start | bytes 73736 | tf_op jit(solution)/shard_map/ppermute | solution.py:23
  36.5 4.3 %collective-permute-start.12 = (f32[24,256]{1,0:T(8,128)S(1)}, f32[24,256]{1,0:T(8,128)S(1)}, u32[]{:S(2)}, u32[]{:S(2)}) collective-permute-start(f32[24,256]{1,0:T(8,128)S(1)} %get-tuple-element.40.refs_8_), channel_id=1, source_target_pairs={{0,4},{4,0},{8,12},{12,8},{1,5},{5,1},{9,13},{13,9},{2,6},{6,2},{1... | collective-permute-start | bytes 73736 | tf_op jit(solution)/shard_map/ppermute | solution.py:23
  42.3 3.5 %collective-permute-start.17 = (f32[24,256]{1,0:T(8,128)S(1)}, f32[24,256]{1,0:T(8,128)S(1)}, u32[]{:S(2)}, u32[]{:S(2)}) collective-permute-start(f32[24,256]{1,0:T(8,128)S(1)} %get-tuple-element.44.refs_8_), channel_id=1, source_target_pairs={{0,3},{1,2},{2,1},{3,0},{4,7},{5,6},{6,5},{7,4},{8,11},{9,10},{10,... | collective-permute-start | bytes 73736 | tf_op jit(solution)/shard_map/ppermute | solution.py:23
  42.3 3.9 %collective-permute-start.16 = (f32[24,256]{1,0:T(8,128)S(1)}, f32[24,256]{1,0:T(8,128)S(1)}, u32[]{:S(2)}, u32[]{:S(2)}) collective-permute-start(f32[24,256]{1,0:T(8,128)S(1)} %get-tuple-element.44.refs_8_), channel_id=1, source_target_pairs={{0,2},{1,3},{2,0},{3,1},{4,6},{5,7},{6,4},{7,5},{8,10},{9,11},{10,... | collective-permute-start | bytes 73736 | tf_op jit(solution)/shard_map/ppermute | solution.py:23
  43.8 2.4 %collective-permute-start.15 = (f32[24,256]{1,0:T(8,128)S(1)}, f32[24,256]{1,0:T(8,128)S(1)}, u32[]{:S(2)}, u32[]{:S(2)}) collective-permute-start(f32[24,256]{1,0:T(8,128)S(1)} %get-tuple-element.44.refs_8_), channel_id=1, source_target_pairs={{0,1},{1,0},{2,3},{3,2},{4,5},{5,4},{6,7},{7,6},{8,9},{9,8},{10,11... | collective-permute-start | bytes 73736 | tf_op jit(solution)/shard_map/ppermute | solution.py:23
  47.8 4.6 %collective-permute-start.18 = (f32[8,256]{1,0:T(8,128)S(1)}, f32[8,256]{1,0:T(8,128)S(1)}, u32[]{:S(2)}, u32[]{:S(2)}) collective-permute-start(f32[8,256]{1,0:T(8,128)S(1)} %get-tuple-element.47), channel_id=1, source_target_pairs={{0,8},{4,12},{8,0},{12,4},{1,9},{5,13},{9,1},{13,5},{2,10},{6,14},... | collective-permute-start | bytes 24584 | tf_op jit(solution)/shard_map/ppermute | solution.py:23
  49.3 5.5 %collective-permute-start.19 = (f32[8,256]{1,0:T(8,128)S(1)}, f32[8,256]{1,0:T(8,128)S(1)}, u32[]{:S(2)}, u32[]{:S(2)}) collective-permute-start(f32[8,256]{1,0:T(8,128)S(1)} %get-tuple-element.48), channel_id=1, source_target_pairs={{0,12},{4,8},{8,4},{12,0},{1,13},{5,9},{9,5},{13,1},{2,14},{6,10},... | collective-permute-start | bytes 24584 | tf_op jit(solution)/shard_map/ppermute | solution.py:23
  51.1 3.7 %collective-permute-start.20 = (f32[8,256]{1,0:T(8,128)S(1)}, f32[8,256]{1,0:T(8,128)S(1)}, u32[]{:S(2)}, u32[]{:S(2)}) collective-permute-start(f32[8,256]{1,0:T(8,128)S(1)} %get-tuple-element.49), channel_id=1, source_target_pairs={{0,4},{4,0},{8,12},{12,8},{1,5},{5,1},{9,13},{13,9},{2,6},{6,2},{1... | collective-permute-start | bytes 24584 | tf_op jit(solution)/shard_map/ppermute | solution.py:23

commit v4 on v3

--- a/solution.py
+++ b/solution.py
@@ -122,7 +122,7 @@
 
 
 def loading_kernel(far_codes, opening, far_scale, far_row, *refs):
-    low, early, rows_pick, rows_pair, wide_scale, scale, row, done, small = refs
+    low, rows_pick, rows_pair, wide_scale, scale, row, done, small = refs
     near = [
         pltpu.make_async_copy(far_scale, scale, small.at[0]),
         pltpu.make_async_copy(far_row, row, small.at[1]),
@@ -142,18 +142,15 @@
         precision=HIGH,
         preferred_element_type=F32,
     )
-    for chunk, copy in enumerate(copies):
+    for copy in copies:
         copy.wait()
-        for k in range(chunk * CHUNK, min((chunk + 1) * CHUNK, early.shape[0])):
-            early[k] = low[k].T
-
-
-def turning_kernel(low, high, part, late):
-    first = low.shape[0] + high.shape[0] - late.shape[0]
+
+
+def turning_kernel(first, low, high, part, turned):
     tile_of = kept_tiles(low, high)
-    for k in range(late.shape[0]):
+    for k in range(turned.shape[0]):
         tile, _ = tile_of(first + k)
-        late[k] = tile.T
+        turned[k] = tile.T
 
 
 def opening_kernel(start, weight, named, out, sources, weights, names, done):
@@ -176,10 +173,10 @@
 
 
 def first_kernel(blocks, slots, order, *refs):
-    far_codes, low, early, scale, rows_pair, column, place = refs[:7]
+    far_codes, low, scale, rows_pair, column, place = refs[:6]
     count = len(order)
-    parts = by_shift(order, refs[7 : 7 + count])
-    out, high, source_pick, source_pair, start, weight, done = refs[7 + count :]
+    parts = by_shift(order, refs[6 : 6 + count])
+    out, high, source_pick, source_pair, start, weight, done = refs[6 + count :]
     loaded = low.shape[0]
     copies = chunk_copies(far_codes, loaded, high, done)
     width = out.shape[1]
@@ -201,8 +198,6 @@
 
 
     def tile_of(k):
-        if k < early.shape[0]:
-            return early[k], False
         if k < loaded:
             return low[k], True
         if (k - loaded) % CHUNK == 0:
@@ -214,7 +209,7 @@
 
 
 def start_data_kernel(count, *refs):
-    low, high, rows_pick, source_pair, scale, observed, data_weight, late = refs[:8]
+    low, high, rows_pick, source_pair, scale, observed, data_weight, turned = refs[:8]
     parts = refs[8 : 8 + count]
     out = refs[8 + count]
     total = total_rows(parts)
@@ -361,7 +356,7 @@
     count = lax.axis_size("tiles")
     sharing = lax.axis_size(("split", "depth"))
     cells = count * blocks
-    late_tiles = tiles // 2
+    half = tiles // 2
     loaded = tiles * 5 // 8
     codes = pltpu.with_memory_space_constraint(tile_codes, pltpu.HBM)
     place = lax.axis_index("tiles").astype(jnp.int32).reshape(1)
@@ -390,11 +385,10 @@
         ],
     )
     begin = across([opening] * count)
-    low, early, rows_pick, rows_pair, scale = call(
+    low, rows_pick, rows_pair, scale = call(
         loading_kernel,
         [
             ((loaded, width, width), BF16),
-            ((tiles - late_tiles, width, width), BF16),
             ((tiles, data_rows), BF16),
             ((data_rows, 2 * tiles), BF16),
             ((tiles, width), F32),
@@ -422,7 +416,6 @@
         ],
         codes,
         low,
-        early,
         scale,
         rows_pair,
         tile_column.reshape(1, -1),
@@ -431,7 +424,18 @@
         scratch=[pltpu.SemaphoreType.DMA(((tiles - loaded) // CHUNK,))],
     )
     parts = within(part)
-    (late,) = call(turning_kernel, [((late_tiles, width, width), BF16)], low, high, part)
+
+    def turned_half(first, part):
+        (turned,) = call(
+            functools.partial(turning_kernel, first),
+            [((half, width, width), BF16)],
+            low,
+            high,
+            part,
+        )
+        return turned
+
+    early = turned_half(0, part)
     (part,) = call(
         functools.partial(start_data_kernel, sharing),
         [((cells, width), F32)],
@@ -442,9 +446,11 @@
         scale,
         observed,
         data_weight,
-        late,
+        early,
         *parts,
     )
+    parts = across([part] * count)
+    late = turned_half(half, part)
     part, first = call(
         functools.partial(start_residual_kernel, blocks, order),
         [((data_rows + EXTRA, width), F32), ((cells, width), F32)],
@@ -455,7 +461,7 @@
         scale,
         start,
         weight,
-        *across([part] * count),
+        *parts,
     )
     part, predicted, sums = call(
         functools.partial(image_data_kernel, sharing),

time: 55.8 us -> 55.3 us (level)
  waiting for transfers between devices: 15.9 us -> 15.1 us
  Pallas kernels: 16.8 us -> 17.5 us
    ppermute x21, waiting for transfers between devices: 15.9 us -> 15.1 us  [exchange(): parts[shift] = lax.ppermute(values[shift], axes, perm)]
    pallas_call x10 -> x11, Pallas kernels: 16.8 us -> 17.5 us  [call(): pl.pallas_call(body, out_shape=[jax.ShapeDtypeStruct(shape, dtype) for sh...]
  transfers between devices with their start and end apart: 21 -> 21, of which waited for: 14 -> 15; matrix products, arithmetic and copies ran while one was open for 0% -> 0% of each run, Pallas kernels for 8% -> 9%
where the time goes in v4:
time: 55.3 us; the launch traced here: 55.1 us
  starting transfers between devices  21.9 us (40%)
  Pallas kernels  17.5 us (32%)
  waiting for transfers between devices  15.1 us (27%)
  between operations  0.72 us (1%)
    ppermute x21, starting transfers between devices, exchange(): parts[shift] = lax.ppermute(values[shift], axes, perm)  21.9 us
    pallas_call x11, Pallas kernels, call(): pl.pallas_call(body, out_shape=[jax.ShapeDtypeStruct(shape, dtype) for sh...  17.5 us
    ppermute x21, waiting for transfers between devices, exchange(): parts[shift] = lax.ppermute(values[shift], axes, perm)  15.1 us
  transfers between devices with their start and end apart: 21, of which 15 were waited for; matrix products, arithmetic and copies ran while one was open for 0% of the time, Pallas kernels for 9%

profile of v4, /device:TPU:0, one launch (start us, length us, event | category | flops | bytes accessed | tf_op | source)
XLA Modules:
  0.0 55.1 jit_solution(9697394930891726784)
XLA Ops:
  0.6 0.7 %shard_map.104.opening.refs_6_ = f32[16,256]{1,0:T(8,128)S(1)} custom-call(f32[4,256]{1,0:T(4,128)} %start.1, f32[4,256]{1,0:T(4,128)} %weight.1, s32[2,4]{1,0:T(2,128)} %bitcast.8), custom_call_target="tpu_custom_call" | custom-call | tf_op jit(solution)/shard_map/pallas_call | solution.py:331
  1.4 4.1 %collective-permute-start.2 = (f32[16,256]{1,0:T(8,128)S(1)}, f32[16,256]{1,0:T(8,128)S(1)}, u32[]{:S(2)}, u32[]{:S(2)}) collective-permute-start(f32[16,256]{1,0:T(8,128)S(1)} %shard_map.104.opening.refs_6_), channel_id=1, source_target_pairs={{0,8},{4,12},{8,0},{12,4},{1,9},{5,13},{9,1},{13,5},{2,10},{6,14},... | collective-permute-start | bytes 49160 | tf_op jit(solution)/shard_map/ppermute | solution.py:23
  5.5 1.3 %collective-permute-start.1 = (f32[16,256]{1,0:T(8,128)S(1)}, f32[16,256]{1,0:T(8,128)S(1)}, u32[]{:S(2)}, u32[]{:S(2)}) collective-permute-start(f32[16,256]{1,0:T(8,128)S(1)} %shard_map.104.opening.refs_6_), channel_id=1, source_target_pairs={{0,12},{4,8},{8,4},{12,0},{1,13},{5,9},{9,5},{13,1},{2,14},{6,10},... | collective-permute-start | bytes 49160 | tf_op jit(solution)/shard_map/ppermute | solution.py:23
  6.8 0.2 collective-permute-start
  7.1 0.0 copy-start.2
  7.1 2.6 %shard_map.105 = (bf16[40,256,256]{2,1,0:T(8,128)(2,1)S(1)}, bf16[64,16]{1,0:T(8,128)(2,1)S(1)}, bf16[16,128]{1,0:T(8,128)(2,1)S(1)}, f32[64,256]{1,0:T(8,128)S(1)}) custom-call(bf16[64,256,256]{2,1,0:T(8,128)(2,1)} %refs_0_.1, f32[16,256]{1,0:T(8,128)S(1)} %shard_map.104.opening.refs_6_, f32[1,64]{1,0:T(1,128)} %bitcast.9, s32[1,64]{1,0:T(1,128)} %bitcast.10), custom_call_target="tpu_custom_call" | custom-call | tf_op jit(solution)/shard_map/pallas_call | solution.py:331
  9.7 0.0 collective-permute-done.2.refs_9_
  9.7 1.3 %collective-permute-done.1.refs_8_ = f32[16,256]{1,0:T(8,128)S(1)} collective-permute-done((f32[16,256]{1,0:T(8,128)S(1)}, f32[16,256]{1,0:T(8,128)S(1)}, u32[]{:S(2)}, u32[]{:S(2)}) %collective-permute-start.1) | collective-permute-done | bytes 16416 | tf_op jit(solution)/shard_map/ppermute | solution.py:23
  11.0 0.0 collective-permute-done.refs_7_
  11.0 0.0 copy-done.2
  11.0 3.7 %shard_map.106 = (f32[16,256]{1,0:T(8,128)S(1)}, bf16[24,256,256]{2,1,0:T(8,128)(2,1)S(1)}, bf16[64,16]{1,0:T(8,128)(2,1)S(1)}, bf16[16,128]{1,0:T(8,128)(2,1)S(...) custom-call(bf16[64,256,256]{2,1,0:T(8,128)(2,1)} %refs_0_.1, ...), custom_call_target="tpu_custom_call" | custom-call | tf_op jit(solution)/shard_map/pallas_call | solution.py:331
  14.7 0.1 collective-permute-start.5
  14.8 1.6 %collective-permute-start.4 = (f32[16,256]{1,0:T(8,128)S(1)}, f32[16,256]{1,0:T(8,128)S(1)}, u32[]{:S(2)}, u32[]{:S(2)}) collective-permute-start(f32[16,256]{1,0:T(8,128)S(1)} %get-tuple-element.31.part.refs_8_), channel_id=1, source_target_pairs={{0,2},{1,3},{2,0},{3,1},{4,6},{5,7},{6,4},{7,5},{8,10},{9,11},{10,... | collective-permute-start | bytes 49160 | tf_op jit(solution)/shard_map/ppermute | solution.py:23
  16.4 0.3 collective-permute-start.3
  16.7 0.0 copy-start
  16.7 0.0 copy-start.1
  16.7 1.1 %shard_map.107.refs_7_.refs_0_ = bf16[32,256,256]{2,1,0:T(8,128)(2,1)S(1)} custom-call(bf16[40,256,256]{2,1,0:T(8,128)(2,1)S(1)} %get-tuple-element.25.refs_1_.low.refs_0_, bf16[24,256,256]{2,1,0:T(8,128)(2,1)S(1)} %get-tuple-element.30.high.refs_1_, f32[16,256]{1,0:T(8,128)S(1)} %get-tuple-element.31.part.refs_8_), custom_call_target="tpu_custom_call" | custom-call | tf_op jit(solution)/shard_map/pallas_call | solution.py:331
  17.8 0.3 collective-permute-done.5.refs_11_
  18.1 0.5 collective-permute-done.4.refs_10_
  18.6 0.0 collective-permute-done.3.refs_9_
  18.6 0.0 copy-done
  18.6 0.0 copy-done.1
  18.6 1.4 %shard_map.108.part.refs_7_ = f32[16,256]{1,0:T(8,128)S(1)} custom-call(bf16[40,256,256]{2,1,0:T(8,128)(2,1)S(1)} %get-tuple-element.25.refs_1_.low.refs_0_, bf16[24,256,256]{2,1,0:T(8,128)(2,1)S(1)} %get-tuple-element.30.high.refs_1_, bf16[64,16]{1,0:T(8,128)(2,1)S(1)} %get-tuple-element.32.refs_2_, bf16[16,128]{1,0:T(8,128)(2,1)S(1)} %get-tuple-element.33.refs_3_, ...), custom_call_target="tpu_custom_call" | custom-call | tf_op jit(solution)/shard_map/pallas_call | solution.py:331
  20.1 1.5 %collective-permute-start.8 = (f32[16,256]{1,0:T(8,128)S(1)}, f32[16,256]{1,0:T(8,128)S(1)}, u32[]{:S(2)}, u32[]{:S(2)}) collective-permute-start(f32[16,256]{1,0:T(8,128)S(1)} %shard_map.108.part.refs_7_), channel_id=1, source_target_pairs={{0,8},{4,12},{8,0},{12,4},{1,9},{5,13},{9,1},{13,5},{2,10},{6,14},... | collective-permute-start | bytes 49160 | tf_op jit(solution)/shard_map/ppermute | solution.py:23
  21.6 1.4 %collective-permute-start.7 = (f32[16,256]{1,0:T(8,128)S(1)}, f32[16,256]{1,0:T(8,128)S(1)}, u32[]{:S(2)}, u32[]{:S(2)}) collective-permute-start(f32[16,256]{1,0:T(8,128)S(1)} %shard_map.108.part.refs_7_), channel_id=1, source_target_pairs={{0,12},{4,8},{8,4},{12,0},{1,13},{5,9},{9,5},{13,1},{2,14},{6,10},... | collective-permute-start | bytes 49160 | tf_op jit(solution)/shard_map/ppermute | solution.py:23
  23.0 0.6 %collective-permute-start.6 = (f32[16,256]{1,0:T(8,128)S(1)}, f32[16,256]{1,0:T(8,128)S(1)}, u32[]{:S(2)}, u32[]{:S(2)}) collective-permute-start(f32[16,256]{1,0:T(8,128)S(1)} %shard_map.108.part.refs_7_), channel_id=1, source_target_pairs={{0,4},{4,0},{8,12},{12,8},{1,5},{5,1},{9,13},{13,9},{2,6},{6,2},{1... | collective-permute-start | bytes 49160 | tf_op jit(solution)/shard_map/ppermute | solution.py:23
  23.6 1.1 %shard_map.109.refs_1_ = bf16[32,256,256]{2,1,0:T(8,128)(2,1)S(1)} custom-call(bf16[40,256,256]{2,1,0:T(8,128)(2,1)S(1)} %get-tuple-element.25.refs_1_.low.refs_0_, bf16[24,256,256]{2,1,0:T(8,128)(2,1)S(1)} %get-tuple-element.30.high.refs_1_, f32[16,256]{1,0:T(8,128)S(1)} %shard_map.108.part.refs_7_), custom_call_target="tpu_custom_call" | custom-call | tf_op jit(solution)/shard_map/pallas_call | solution.py:331
  24.7 0.2 collective-permute-done.8.refs_10_
  24.9 2.2 %collective-permute-done.7.refs_9_ = f32[16,256]{1,0:T(8,128)S(1)} collective-permute-done((f32[16,256]{1,0:T(8,128)S(1)}, f32[16,256]{1,0:T(8,128)S(1)}, u32[]{:S(2)}, u32[]{:S(2)}) %collective-permute-start.7) | collective-permute-done | bytes 16416 | tf_op jit(solution)/shard_map/ppermute | solution.py:23
  27.1 0.0 collective-permute-done.6.refs_8_
  27.1 1.4 %shard_map.110 = (f32[24,256]{1,0:T(8,128)S(1)}, f32[16,256]{1,0:T(8,128)S(1)}) custom-call(bf16[32,256,256]{2,1,0:T(8,128)(2,1)S(1)} %shard_map.107.refs_7_.refs_0_, bf16[32,256,256]{2,1,0:T(8,128)(2,1)S(1)} %shard_map.109.refs_1_, bf16[64,16]{1,0:T(8,128)(2,1)S(1)} %get-tuple-element.34.refs_2_, bf16[16,128]{1,0:T(8,128)(2,1)S(1)} %get-tuple-element.27.refs_3_, ...), custom_call_target="tpu_custom_call" | custom-call | tf_op jit(solution)/shard_map/pallas_call | solution.py:331
  28.6 0.0 collective-permute-start.11
  28.6 1.5 %collective-permute-start.10 = (f32[24,256]{1,0:T(8,128)S(1)}, f32[24,256]{1,0:T(8,128)S(1)}, u32[]{:S(2)}, u32[]{:S(2)}) collective-permute-start(f32[24,256]{1,0:T(8,128)S(1)} %get-tuple-element.36.refs_6_), channel_id=1, source_target_pairs={{0,2},{1,3},{2,0},{3,1},{4,6},{5,7},{6,4},{7,5},{8,10},{9,11},{10,... | collective-permute-start | bytes 73736 | tf_op jit(solution)/shard_map/ppermute | solution.py:23
  30.1 0.3 collective-permute-start.9
  30.4 1.6 %collective-permute-done.11.refs_9_ = f32[24,256]{1,0:T(8,128)S(1)} collective-permute-done((f32[24,256]{1,0:T(8,128)S(1)}, f32[24,256]{1,0:T(8,128)S(1)}, u32[]{:S(2)}, u32[]{:S(2)}) %collective-permute-start.11) | collective-permute-done | bytes 24608 | tf_op jit(solution)/shard_map/ppermute | solution.py:23
  32.1 0.4 collective-permute-done.10.refs_8_
  32.5 0.0 collective-permute-done.9.refs_7_
  32.5 1.4 %shard_map.111 = (f32[24,256]{1,0:T(8,128)S(1)}, f32[16,256]{1,0:T(8,128)S(1)}, f32[8,256]{1,0:T(8,128)S(1)}) custom-call(bf16[40,256,256]{2,1,0:T(8,128)(2,1)S(1)} %get-tuple-element.25.refs_1_.low.refs_0_, bf16[24,256,256]{2,1,0:T(8,128)(2,1)S(1)} %get-tuple-element.30.high.refs_1_, bf16[64,16]{1,0:T(8,128)(2,1)S(1)} %get-tuple-element.32.refs_2_, ...), custom_call_target="tpu_custom_call" | custom-call | tf_op jit(solution)/shard_map/pallas_call | solution.py:331
  33.9 0.8 %collective-permute-start.14 = (f32[24,256]{1,0:T(8,128)S(1)}, f32[24,256]{1,0:T(8,128)S(1)}, u32[]{:S(2)}, u32[]{:S(2)}) collective-permute-start(f32[24,256]{1,0:T(8,128)S(1)} %get-tuple-element.38.refs_8_), channel_id=1, source_target_pairs={{0,8},{4,12},{8,0},{12,4},{1,9},{5,13},{9,1},{13,5},{2,10},{6,14},... | collective-permute-start | bytes 73736 | tf_op jit(solution)/shard_map/ppermute | solution.py:23
  34.7 1.8 %collective-permute-start.13 = (f32[24,256]{1,0:T(8,128)S(1)}, f32[24,256]{1,0:T(8,128)S(1)}, u32[]{:S(2)}, u32[]{:S(2)}) collective-permute-start(f32[24,256]{1,0:T(8,128)S(1)} %get-tuple-element.38.refs_8_), channel_id=1, source_target_pairs={{0,12},{4,8},{8,4},{12,0},{1,13},{5,9},{9,5},{13,1},{2,14},{6,10},... | collective-permute-start | bytes 73736 | tf_op jit(solution)/shard_map/ppermute | solution.py:23
  36.5 0.9 %collective-permute-start.12 = (f32[24,256]{1,0:T(8,128)S(1)}, f32[24,256]{1,0:T(8,128)S(1)}, u32[]{:S(2)}, u32[]{:S(2)}) collective-permute-start(f32[24,256]{1,0:T(8,128)S(1)} %get-tuple-element.38.refs_8_), channel_id=1, source_target_pairs={{0,4},{4,0},{8,12},{12,8},{1,5},{5,1},{9,13},{13,9},{2,6},{6,2},{1... | collective-permute-start | bytes 73736 | tf_op jit(solution)/shard_map/ppermute | solution.py:23
  37.4 1.3 %collective-permute-done.14.refs_11_ = f32[24,256]{1,0:T(8,128)S(1)} collective-permute-done((f32[24,256]{1,0:T(8,128)S(1)}, f32[24,256]{1,0:T(8,128)S(1)}, u32[]{:S(2)}, u32[]{:S(2)}) %collective-permute-start.14) | collective-permute-done | bytes 24608 | tf_op jit(solution)/shard_map/ppermute | solution.py:23
  38.7 1.8 %collective-permute-done.13.refs_10_ = f32[24,256]{1,0:T(8,128)S(1)} collective-permute-done((f32[24,256]{1,0:T(8,128)S(1)}, f32[24,256]{1,0:T(8,128)S(1)}, u32[]{:S(2)}, u32[]{:S(2)}) %collective-permute-start.13) | collective-permute-done | bytes 24608 | tf_op jit(solution)/shard_map/ppermute | solution.py:23
  40.4 0.1 collective-permute-done.12.refs_9_
  40.5 1.5 %shard_map.112 = (f32[24,256]{1,0:T(8,128)S(1)}, f32[16,256]{1,0:T(8,128)S(1)}, f32[8,128]{1,0:T(8,128)S(1)}) custom-call(bf16[32,256,256]{2,1,0:T(8,128)(2,1)S(1)} %shard_map.107.refs_7_.refs_0_, bf16[32,256,256]{2,1,0:T(8,128)(2,1)S(1)} %shard_map.109.refs_1_, bf16[64,16]{1,0:T(8,128)(2,1)S(1)} %get-tuple-element.34.refs_2_, ...), custom_call_target="tpu_custom_call" | custom-call | tf_op jit(solution)/shard_map/pallas_call | solution.py:331
  42.1 0.0 collective-permute-start.17
  42.1 1.5 %collective-permute-start.16 = (f32[24,256]{1,0:T(8,128)S(1)}, f32[24,256]{1,0:T(8,128)S(1)}, u32[]{:S(2)}, u32[]{:S(2)}) collective-permute-start(f32[24,256]{1,0:T(8,128)S(1)} %get-tuple-element.42.refs_8_), channel_id=1, source_target_pairs={{0,2},{1,3},{2,0},{3,1},{4,6},{5,7},{6,4},{7,5},{8,10},{9,11},{10,... | collective-permute-start | bytes 73736 | tf_op jit(solution)/shard_map/ppermute | solution.py:23
  43.6 0.4 collective-permute-start.15
  44.0 1.6 %collective-permute-done.17.refs_11_ = f32[24,256]{1,0:T(8,128)S(1)} collective-permute-done((f32[24,256]{1,0:T(8,128)S(1)}, f32[24,256]{1,0:T(8,128)S(1)}, u32[]{:S(2)}, u32[]{:S(2)}) %collective-permute-start.17) | collective-permute-done | bytes 24608 | tf_op jit(solution)/shard_map/ppermute | solution.py:23
  45.6 0.4 collective-permute-done.16.refs_10_
  46.0 0.0 collective-permute-done.15.refs_9_
  46.0 1.6 %shard_map.113 = (f32[8,256]{1,0:T(8,128)S(1)}, f32[8,256]{1,0:T(8,128)S(1)}, f32[8,256]{1,0:T(8,128)S(1)}, f32[8,256]{1,0:T(8,128)S(1)}, f32[8,256]{1,0:T(8,128)S(1)}) custom-call(bf16[40,256,256]{2,1,0:T(8,128)(2,1)S(1)} %get-tuple-element.25.refs_1_.low.refs_0_, bf16[24,256,256]{2,1,0:T(8,128)(2,1)S(1)} %get-tuple-element.30.high.refs_1_, ...), custom_call_target="tpu_custom_call" | custom-call | tf_op jit(solution)/shard_map/pallas_call | solution.py:331
  47.5 1.3 %collective-permute-start.18 = (f32[8,256]{1,0:T(8,128)S(1)}, f32[8,256]{1,0:T(8,128)S(1)}, u32[]{:S(2)}, u32[]{:S(2)}) collective-permute-start(f32[8,256]{1,0:T(8,128)S(1)} %get-tuple-element.45), channel_id=1, source_target_pairs={{0,8},{4,12},{8,0},{12,4},{1,9},{5,13},{9,1},{13,5},{2,10},{6,14},... | collective-permute-start | bytes 24584 | tf_op jit(solution)/shard_map/ppermute | solution.py:23
  48.8 1.8 %collective-permute-start.19 = (f32[8,256]{1,0:T(8,128)S(1)}, f32[8,256]{1,0:T(8,128)S(1)}, u32[]{:S(2)}, u32[]{:S(2)}) collective-permute-start(f32[8,256]{1,0:T(8,128)S(1)} %get-tuple-element.46), channel_id=1, source_target_pairs={{0,12},{4,8},{8,4},{12,0},{1,13},{5,9},{9,5},{13,1},{2,14},{6,10},... | collective-permute-start | bytes 24584 | tf_op jit(solution)/shard_map/ppermute | solution.py:23
  50.6 0.5 collective-permute-start.20
  51.0 1.2 %collective-permute-done.18.refs_7_ = f32[8,256]{1,0:T(8,128)S(1)} collective-permute-done((f32[8,256]{1,0:T(8,128)S(1)}, f32[8,256]{1,0:T(8,128)S(1)}, u32[]{:S(2)}, u32[]{:S(2)}) %collective-permute-start.18) | collective-permute-done | bytes 8224 | tf_op jit(solution)/shard_map/ppermute | solution.py:23
  52.2 2.0 %collective-permute-done.19.refs_8_ = f32[8,256]{1,0:T(8,128)S(1)} collective-permute-done((f32[8,256]{1,0:T(8,128)S(1)}, f32[8,256]{1,0:T(8,128)S(1)}, u32[]{:S(2)}, u32[]{:S(2)}) %collective-permute-start.19) | collective-permute-done | bytes 8224 | tf_op jit(solution)/shard_map/ppermute | solution.py:23
  54.2 0.1 collective-permute-done.20.refs_9_
  54.3 0.8 %shard_map.114 = (f32[4,256]{1,0:T(4,128)}, f32[4,256]{1,0:T(4,128)}) custom-call(f32[16,256]{1,0:T(8,128)S(1)} %get-tuple-element.28.refs_6_.refs_5_.refs_0_, f32[16,256]{1,0:T(8,128)S(1)} %get-tuple-element.29.refs_5_.refs_1_, f32[16,256]{1,0:T(8,128)S(1)} %get-tuple-element.35.refs_6_.refs_2_, f32[16,256]{1,0:T(8,128)S(1)} %get-tuple-element.39.refs_3_, ...), custom_call_target="tpu_custom_call" | custom-call | tf_op jit(solution)/shard_map/pallas_call | solution.py:331
Async XLA Ops:
  1.4 8.3 %collective-permute-start.2 = (f32[16,256]{1,0:T(8,128)S(1)}, f32[16,256]{1,0:T(8,128)S(1)}, u32[]{:S(2)}, u32[]{:S(2)}) collective-permute-start(f32[16,256]{1,0:T(8,128)S(1)} %shard_map.104.opening.refs_6_), channel_id=1, source_target_pairs={{0,8},{4,12},{8,0},{12,4},{1,9},{5,13},{9,1},{13,5},{2,10},{6,14},... | collective-permute-start | bytes 49160 | tf_op jit(solution)/shard_map/ppermute | solution.py:23
  5.5 5.5 %collective-permute-start.1 = (f32[16,256]{1,0:T(8,128)S(1)}, f32[16,256]{1,0:T(8,128)S(1)}, u32[]{:S(2)}, u32[]{:S(2)}) collective-permute-start(f32[16,256]{1,0:T(8,128)S(1)} %shard_map.104.opening.refs_6_), channel_id=1, source_target_pairs={{0,12},{4,8},{8,4},{12,0},{1,13},{5,9},{9,5},{13,1},{2,14},{6,10},... | collective-permute-start | bytes 49160 | tf_op jit(solution)/shard_map/ppermute | solution.py:23
  6.8 4.2 %collective-permute-start = (f32[16,256]{1,0:T(8,128)S(1)}, f32[16,256]{1,0:T(8,128)S(1)}, u32[]{:S(2)}, u32[]{:S(2)}) collective-permute-start(f32[16,256]{1,0:T(8,128)S(1)} %shard_map.104.opening.refs_6_), channel_id=1, source_target_pairs={{0,4},{4,0},{8,12},{12,8},{1,5},{5,1},{9,13},{13,9},{2,6},{6,2},{1... | collective-permute-start | bytes 49160 | tf_op jit(solution)/shard_map/ppermute | solution.py:23
  7.1 4.0 %copy-start.2 = (s32[64]{0:T(128)S(1)}, s32[64]{0:T(128)}, u32[]{:S(2)}) copy-start(s32[64]{0:T(128)} %param.12) | copy-start | bytes 772
  14.7 3.4 %collective-permute-start.5 = (f32[16,256]{1,0:T(8,128)S(1)}, f32[16,256]{1,0:T(8,128)S(1)}, u32[]{:S(2)}, u32[]{:S(2)}) collective-permute-start(f32[16,256]{1,0:T(8,128)S(1)} %get-tuple-element.31.part.refs_8_), channel_id=1, source_target_pairs={{0,3},{1,2},{2,1},{3,0},{4,7},{5,6},{6,5},{7,4},{8,11},{9,10},{10,... | collective-permute-start | bytes 49160 | tf_op jit(solution)/shard_map/ppermute | solution.py:23
  14.8 3.8 %collective-permute-start.4 = (f32[16,256]{1,0:T(8,128)S(1)}, f32[16,256]{1,0:T(8,128)S(1)}, u32[]{:S(2)}, u32[]{:S(2)}) collective-permute-start(f32[16,256]{1,0:T(8,128)S(1)} %get-tuple-element.31.part.refs_8_), channel_id=1, source_target_pairs={{0,2},{1,3},{2,0},{3,1},{4,6},{5,7},{6,4},{7,5},{8,10},{9,11},{10,... | collective-permute-start | bytes 49160 | tf_op jit(solution)/shard_map/ppermute | solution.py:23
  16.4 2.3 %collective-permute-start.3 = (f32[16,256]{1,0:T(8,128)S(1)}, f32[16,256]{1,0:T(8,128)S(1)}, u32[]{:S(2)}, u32[]{:S(2)}) collective-permute-start(f32[16,256]{1,0:T(8,128)S(1)} %get-tuple-element.31.part.refs_8_), channel_id=1, source_target_pairs={{0,1},{1,0},{2,3},{3,2},{4,5},{5,4},{6,7},{7,6},{8,9},{9,8},{10,11... | collective-permute-start | bytes 49160 | tf_op jit(solution)/shard_map/ppermute | solution.py:23
  16.7 2.0 %copy-start = (f32[16,256]{1,0:T(8,128)S(1)}, f32[16,256]{1,0:T(8,128)}, u32[]{:S(2)}) copy-start(f32[16,256]{1,0:T(8,128)} %refs_5_.5) | copy-start | bytes 49156
  16.7 2.0 %copy-start.1 = (f32[16,256]{1,0:T(8,128)S(1)}, f32[16,256]{1,0:T(8,128)}, u32[]{:S(2)}) copy-start(f32[16,256]{1,0:T(8,128)} %refs_5_.3) | copy-start | bytes 49156
  20.1 4.8 %collective-permute-start.8 = (f32[16,256]{1,0:T(8,128)S(1)}, f32[16,256]{1,0:T(8,128)S(1)}, u32[]{:S(2)}, u32[]{:S(2)}) collective-permute-start(f32[16,256]{1,0:T(8,128)S(1)} %shard_map.108.part.refs_7_), channel_id=1, source_target_pairs={{0,8},{4,12},{8,0},{12,4},{1,9},{5,13},{9,1},{13,5},{2,10},{6,14},... | collective-permute-start | bytes 49160 | tf_op jit(solution)/shard_map/ppermute | solution.py:23
  21.6 5.5 %collective-permute-start.7 = (f32[16,256]{1,0:T(8,128)S(1)}, f32[16,256]{1,0:T(8,128)S(1)}, u32[]{:S(2)}, u32[]{:S(2)}) collective-permute-start(f32[16,256]{1,0:T(8,128)S(1)} %shard_map.108.part.refs_7_), channel_id=1, source_target_pairs={{0,12},{4,8},{8,4},{12,0},{1,13},{5,9},{9,5},{13,1},{2,14},{6,10},... | collective-permute-start | bytes 49160 | tf_op jit(solution)/shard_map/ppermute | solution.py:23
  23.0 4.2 %collective-permute-start.6 = (f32[16,256]{1,0:T(8,128)S(1)}, f32[16,256]{1,0:T(8,128)S(1)}, u32[]{:S(2)}, u32[]{:S(2)}) collective-permute-start(f32[16,256]{1,0:T(8,128)S(1)} %shard_map.108.part.refs_7_), channel_id=1, source_target_pairs={{0,4},{4,0},{8,12},{12,8},{1,5},{5,1},{9,13},{13,9},{2,6},{6,2},{1... | collective-permute-start | bytes 49160 | tf_op jit(solution)/shard_map/ppermute | solution.py:23
  28.6 3.5 %collective-permute-start.11 = (f32[24,256]{1,0:T(8,128)S(1)}, f32[24,256]{1,0:T(8,128)S(1)}, u32[]{:S(2)}, u32[]{:S(2)}) collective-permute-start(f32[24,256]{1,0:T(8,128)S(1)} %get-tuple-element.36.refs_6_), channel_id=1, source_target_pairs={{0,3},{1,2},{2,1},{3,0},{4,7},{5,6},{6,5},{7,4},{8,11},{9,10},{10,... | collective-permute-start | bytes 73736 | tf_op jit(solution)/shard_map/ppermute | solution.py:23
  28.6 3.9 %collective-permute-start.10 = (f32[24,256]{1,0:T(8,128)S(1)}, f32[24,256]{1,0:T(8,128)S(1)}, u32[]{:S(2)}, u32[]{:S(2)}) collective-permute-start(f32[24,256]{1,0:T(8,128)S(1)} %get-tuple-element.36.refs_6_), channel_id=1, source_target_pairs={{0,2},{1,3},{2,0},{3,1},{4,6},{5,7},{6,4},{7,5},{8,10},{9,11},{10,... | collective-permute-start | bytes 73736 | tf_op jit(solution)/shard_map/ppermute | solution.py:23
  30.1 2.4 %collective-permute-start.9 = (f32[24,256]{1,0:T(8,128)S(1)}, f32[24,256]{1,0:T(8,128)S(1)}, u32[]{:S(2)}, u32[]{:S(2)}) collective-permute-start(f32[24,256]{1,0:T(8,128)S(1)} %get-tuple-element.36.refs_6_), channel_id=1, source_target_pairs={{0,1},{1,0},{2,3},{3,2},{4,5},{5,4},{6,7},{7,6},{8,9},{9,8},{10,11... | collective-permute-start | bytes 73736 | tf_op jit(solution)/shard_map/ppermute | solution.py:23
  33.9 4.8 %collective-permute-start.14 = (f32[24,256]{1,0:T(8,128)S(1)}, f32[24,256]{1,0:T(8,128)S(1)}, u32[]{:S(2)}, u32[]{:S(2)}) collective-permute-start(f32[24,256]{1,0:T(8,128)S(1)} %get-tuple-element.38.refs_8_), channel_id=1, source_target_pairs={{0,8},{4,12},{8,0},{12,4},{1,9},{5,13},{9,1},{13,5},{2,10},{6,14},... | collective-permute-start | bytes 73736 | tf_op jit(solution)/shard_map/ppermute | solution.py:23
  34.7 5.8 %collective-permute-start.13 = (f32[24,256]{1,0:T(8,128)S(1)}, f32[24,256]{1,0:T(8,128)S(1)}, u32[]{:S(2)}, u32[]{:S(2)}) collective-permute-start(f32[24,256]{1,0:T(8,128)S(1)} %get-tuple-element.38.refs_8_), channel_id=1, source_target_pairs={{0,12},{4,8},{8,4},{12,0},{1,13},{5,9},{9,5},{13,1},{2,14},{6,10},... | collective-permute-start | bytes 73736 | tf_op jit(solution)/shard_map/ppermute | solution.py:23
  36.5 4.1 %collective-permute-start.12 = (f32[24,256]{1,0:T(8,128)S(1)}, f32[24,256]{1,0:T(8,128)S(1)}, u32[]{:S(2)}, u32[]{:S(2)}) collective-permute-start(f32[24,256]{1,0:T(8,128)S(1)} %get-tuple-element.38.refs_8_), channel_id=1, source_target_pairs={{0,4},{4,0},{8,12},{12,8},{1,5},{5,1},{9,13},{13,9},{2,6},{6,2},{1... | collective-permute-start | bytes 73736 | tf_op jit(solution)/shard_map/ppermute | solution.py:23
  42.1 3.5 %collective-permute-start.17 = (f32[24,256]{1,0:T(8,128)S(1)}, f32[24,256]{1,0:T(8,128)S(1)}, u32[]{:S(2)}, u32[]{:S(2)}) collective-permute-start(f32[24,256]{1,0:T(8,128)S(1)} %get-tuple-element.42.refs_8_), channel_id=1, source_target_pairs={{0,3},{1,2},{2,1},{3,0},{4,7},{5,6},{6,5},{7,4},{8,11},{9,10},{10,... | collective-permute-start | bytes 73736 | tf_op jit(solution)/shard_map/ppermute | solution.py:23
  42.1 3.9 %collective-permute-start.16 = (f32[24,256]{1,0:T(8,128)S(1)}, f32[24,256]{1,0:T(8,128)S(1)}, u32[]{:S(2)}, u32[]{:S(2)}) collective-permute-start(f32[24,256]{1,0:T(8,128)S(1)} %get-tuple-element.42.refs_8_), channel_id=1, source_target_pairs={{0,2},{1,3},{2,0},{3,1},{4,6},{5,7},{6,4},{7,5},{8,10},{9,11},{10,... | collective-permute-start | bytes 73736 | tf_op jit(solution)/shard_map/ppermute | solution.py:23
  43.6 2.4 %collective-permute-start.15 = (f32[24,256]{1,0:T(8,128)S(1)}, f32[24,256]{1,0:T(8,128)S(1)}, u32[]{:S(2)}, u32[]{:S(2)}) collective-permute-start(f32[24,256]{1,0:T(8,128)S(1)} %get-tuple-element.42.refs_8_), channel_id=1, source_target_pairs={{0,1},{1,0},{2,3},{3,2},{4,5},{5,4},{6,7},{7,6},{8,9},{9,8},{10,11... | collective-permute-start | bytes 73736 | tf_op jit(solution)/shard_map/ppermute | solution.py:23
  47.5 4.7 %collective-permute-start.18 = (f32[8,256]{1,0:T(8,128)S(1)}, f32[8,256]{1,0:T(8,128)S(1)}, u32[]{:S(2)}, u32[]{:S(2)}) collective-permute-start(f32[8,256]{1,0:T(8,128)S(1)} %get-tuple-element.45), channel_id=1, source_target_pairs={{0,8},{4,12},{8,0},{12,4},{1,9},{5,13},{9,1},{13,5},{2,10},{6,14},... | collective-permute-start | bytes 24584 | tf_op jit(solution)/shard_map/ppermute | solution.py:23
  48.8 5.5 %collective-permute-start.19 = (f32[8,256]{1,0:T(8,128)S(1)}, f32[8,256]{1,0:T(8,128)S(1)}, u32[]{:S(2)}, u32[]{:S(2)}) collective-permute-start(f32[8,256]{1,0:T(8,128)S(1)} %get-tuple-element.46), channel_id=1, source_target_pairs={{0,12},{4,8},{8,4},{12,0},{1,13},{5,9},{9,5},{13,1},{2,14},{6,10},... | collective-permute-start | bytes 24584 | tf_op jit(solution)/shard_map/ppermute | solution.py:23
  50.6 3.7 %collective-permute-start.20 = (f32[8,256]{1,0:T(8,128)S(1)}, f32[8,256]{1,0:T(8,128)S(1)}, u32[]{:S(2)}, u32[]{:S(2)}) collective-permute-start(f32[8,256]{1,0:T(8,128)S(1)} %get-tuple-element.47), channel_id=1, source_target_pairs={{0,4},{4,0},{8,12},{12,8},{1,5},{5,1},{9,13},{13,9},{2,6},{6,2},{1... | collective-permute-start | bytes 24584 | tf_op jit(solution)/shard_map/ppermute | solution.py:23

commit v5 on v4

--- a/solution.py
+++ b/solution.py
@@ -357,7 +357,7 @@
     sharing = lax.axis_size(("split", "depth"))
     cells = count * blocks
     half = tiles // 2
-    loaded = tiles * 5 // 8
+    loaded = tiles * 3 // 4
     codes = pltpu.with_memory_space_constraint(tile_codes, pltpu.HBM)
     place = lax.axis_index("tiles").astype(jnp.int32).reshape(1)
 

time: 55.3 us -> 54.8 us (level)
  transfers between devices with their start and end apart: 21 -> 21, of which waited for: 15 -> 13; matrix products, arithmetic and copies ran while one was open for 0% -> 0% of each run, Pallas kernels for 9% -> 9%
where the time goes in v5:
time: 54.8 us; the launch traced here: 54.6 us
  starting transfers between devices  21.9 us (40%)
  Pallas kernels  17 us (31%)
  waiting for transfers between devices  15.1 us (28%)
  between operations  0.72 us (1%)
    ppermute x21, starting transfers between devices, exchange(): parts[shift] = lax.ppermute(values[shift], axes, perm)  21.9 us
    pallas_call x11, Pallas kernels, call(): pl.pallas_call(body, out_shape=[jax.ShapeDtypeStruct(shape, dtype) for sh...  17 us
    ppermute x21, waiting for transfers between devices, exchange(): parts[shift] = lax.ppermute(values[shift], axes, perm)  15.1 us
  transfers between devices with their start and end apart: 21, of which 13 were waited for; matrix products, arithmetic and copies ran while one was open for 0% of the time, Pallas kernels for 9%

profile of v5, /device:TPU:0, one launch (start us, length us, event | category | flops | bytes accessed | tf_op | source)
XLA Modules:
  0.0 54.6 jit_solution(1953250545480881469)
XLA Ops:
  0.6 0.7 %shard_map.104.opening.refs_6_ = f32[16,256]{1,0:T(8,128)S(1)} custom-call(f32[4,256]{1,0:T(4,128)} %start.1, f32[4,256]{1,0:T(4,128)} %weight.1, s32[2,4]{1,0:T(2,128)} %bitcast.8), custom_call_target="tpu_custom_call" | custom-call | tf_op jit(solution)/shard_map/pallas_call | solution.py:331
  1.4 4.1 %collective-permute-start.2 = (f32[16,256]{1,0:T(8,128)S(1)}, f32[16,256]{1,0:T(8,128)S(1)}, u32[]{:S(2)}, u32[]{:S(2)}) collective-permute-start(f32[16,256]{1,0:T(8,128)S(1)} %shard_map.104.opening.refs_6_), channel_id=1, source_target_pairs={{0,8},{4,12},{8,0},{12,4},{1,9},{5,13},{9,1},{13,5},{2,10},{6,14},... | collective-permute-start | bytes 49160 | tf_op jit(solution)/shard_map/ppermute | solution.py:23
  5.5 1.3 %collective-permute-start.1 = (f32[16,256]{1,0:T(8,128)S(1)}, f32[16,256]{1,0:T(8,128)S(1)}, u32[]{:S(2)}, u32[]{:S(2)}) collective-permute-start(f32[16,256]{1,0:T(8,128)S(1)} %shard_map.104.opening.refs_6_), channel_id=1, source_target_pairs={{0,12},{4,8},{8,4},{12,0},{1,13},{5,9},{9,5},{13,1},{2,14},{6,10},... | collective-permute-start | bytes 49160 | tf_op jit(solution)/shard_map/ppermute | solution.py:23
  6.8 0.2 collective-permute-start
  7.1 0.0 copy-start.2
  7.1 2.9 %shard_map.105 = (bf16[48,256,256]{2,1,0:T(8,128)(2,1)S(1)}, bf16[64,16]{1,0:T(8,128)(2,1)S(1)}, bf16[16,128]{1,0:T(8,128)(2,1)S(1)}, f32[64,256]{1,0:T(8,128)S(1)}) custom-call(bf16[64,256,256]{2,1,0:T(8,128)(2,1)} %refs_0_.1, f32[16,256]{1,0:T(8,128)S(1)} %shard_map.104.opening.refs_6_, f32[1,64]{1,0:T(1,128)} %bitcast.9, s32[1,64]{1,0:T(1,128)} %bitcast.10), custom_call_target="tpu_custom_call" | custom-call | tf_op jit(solution)/shard_map/pallas_call | solution.py:331
  10.0 0.0 collective-permute-done.2.refs_9_
  10.0 1.0 %collective-permute-done.1.refs_8_ = f32[16,256]{1,0:T(8,128)S(1)} collective-permute-done((f32[16,256]{1,0:T(8,128)S(1)}, f32[16,256]{1,0:T(8,128)S(1)}, u32[]{:S(2)}, u32[]{:S(2)}) %collective-permute-start.1) | collective-permute-done | bytes 16416 | tf_op jit(solution)/shard_map/ppermute | solution.py:23
  11.0 0.0 collective-permute-done.refs_7_
  11.0 0.0 copy-done.2
  11.0 2.9 %shard_map.106 = (f32[16,256]{1,0:T(8,128)S(1)}, bf16[16,256,256]{2,1,0:T(8,128)(2,1)S(1)}, bf16[64,16]{1,0:T(8,128)(2,1)S(1)}, bf16[16,128]{1,0:T(8,128)(2,1)S(...) custom-call(bf16[64,256,256]{2,1,0:T(8,128)(2,1)} %refs_0_.1, ...), custom_call_target="tpu_custom_call" | custom-call | tf_op jit(solution)/shard_map/pallas_call | solution.py:331
  13.9 0.1 collective-permute-start.5
  14.0 1.6 %collective-permute-start.4 = (f32[16,256]{1,0:T(8,128)S(1)}, f32[16,256]{1,0:T(8,128)S(1)}, u32[]{:S(2)}, u32[]{:S(2)}) collective-permute-start(f32[16,256]{1,0:T(8,128)S(1)} %get-tuple-element.31.part.refs_8_), channel_id=1, source_target_pairs={{0,2},{1,3},{2,0},{3,1},{4,6},{5,7},{6,4},{7,5},{8,10},{9,11},{10,... | collective-permute-start | bytes 49160 | tf_op jit(solution)/shard_map/ppermute | solution.py:23
  15.6 0.3 collective-permute-start.3
  15.9 0.0 copy-start
  15.9 0.0 copy-start.1
  15.9 1.1 %shard_map.107.refs_7_.refs_0_ = bf16[32,256,256]{2,1,0:T(8,128)(2,1)S(1)} custom-call(bf16[48,256,256]{2,1,0:T(8,128)(2,1)S(1)} %get-tuple-element.25.refs_1_.low.refs_0_, bf16[16,256,256]{2,1,0:T(8,128)(2,1)S(1)} %get-tuple-element.30.high.refs_1_, f32[16,256]{1,0:T(8,128)S(1)} %get-tuple-element.31.part.refs_8_), custom_call_target="tpu_custom_call" | custom-call | tf_op jit(solution)/shard_map/pallas_call | solution.py:331
  17.0 0.3 collective-permute-done.5.refs_11_
  17.3 0.5 collective-permute-done.4.refs_10_
  17.8 0.0 collective-permute-done.3.refs_9_
  17.8 0.0 copy-done
  17.8 0.0 copy-done.1
  17.8 1.4 %shard_map.108.part.refs_7_ = f32[16,256]{1,0:T(8,128)S(1)} custom-call(bf16[48,256,256]{2,1,0:T(8,128)(2,1)S(1)} %get-tuple-element.25.refs_1_.low.refs_0_, bf16[16,256,256]{2,1,0:T(8,128)(2,1)S(1)} %get-tuple-element.30.high.refs_1_, bf16[64,16]{1,0:T(8,128)(2,1)S(1)} %get-tuple-element.32.refs_2_, bf16[16,128]{1,0:T(8,128)(2,1)S(1)} %get-tuple-element.33.refs_3_, ...), custom_call_target="tpu_custom_call" | custom-call | tf_op jit(solution)/shard_map/pallas_call | solution.py:331
  19.2 1.9 %collective-permute-start.8 = (f32[16,256]{1,0:T(8,128)S(1)}, f32[16,256]{1,0:T(8,128)S(1)}, u32[]{:S(2)}, u32[]{:S(2)}) collective-permute-start(f32[16,256]{1,0:T(8,128)S(1)} %shard_map.108.part.refs_7_), channel_id=1, source_target_pairs={{0,8},{4,12},{8,0},{12,4},{1,9},{5,13},{9,1},{13,5},{2,10},{6,14},... | collective-permute-start | bytes 49160 | tf_op jit(solution)/shard_map/ppermute | solution.py:23
  21.1 1.4 %collective-permute-start.7 = (f32[16,256]{1,0:T(8,128)S(1)}, f32[16,256]{1,0:T(8,128)S(1)}, u32[]{:S(2)}, u32[]{:S(2)}) collective-permute-start(f32[16,256]{1,0:T(8,128)S(1)} %shard_map.108.part.refs_7_), channel_id=1, source_target_pairs={{0,12},{4,8},{8,4},{12,0},{1,13},{5,9},{9,5},{13,1},{2,14},{6,10},... | collective-permute-start | bytes 49160 | tf_op jit(solution)/shard_map/ppermute | solution.py:23
  22.5 0.3 collective-permute-start.6
  22.8 1.1 %shard_map.109.refs_1_ = bf16[32,256,256]{2,1,0:T(8,128)(2,1)S(1)} custom-call(bf16[48,256,256]{2,1,0:T(8,128)(2,1)S(1)} %get-tuple-element.25.refs_1_.low.refs_0_, bf16[16,256,256]{2,1,0:T(8,128)(2,1)S(1)} %get-tuple-element.30.high.refs_1_, f32[16,256]{1,0:T(8,128)S(1)} %shard_map.108.part.refs_7_), custom_call_target="tpu_custom_call" | custom-call | tf_op jit(solution)/shard_map/pallas_call | solution.py:331
  23.9 0.0 collective-permute-done.8.refs_10_
  23.9 2.7 %collective-permute-done.7.refs_9_ = f32[16,256]{1,0:T(8,128)S(1)} collective-permute-done((f32[16,256]{1,0:T(8,128)S(1)}, f32[16,256]{1,0:T(8,128)S(1)}, u32[]{:S(2)}, u32[]{:S(2)}) %collective-permute-start.7) | collective-permute-done | bytes 16416 | tf_op jit(solution)/shard_map/ppermute | solution.py:23
  26.6 0.0 collective-permute-done.6.refs_8_
  26.6 1.4 %shard_map.110 = (f32[24,256]{1,0:T(8,128)S(1)}, f32[16,256]{1,0:T(8,128)S(1)}) custom-call(bf16[32,256,256]{2,1,0:T(8,128)(2,1)S(1)} %shard_map.107.refs_7_.refs_0_, bf16[32,256,256]{2,1,0:T(8,128)(2,1)S(1)} %shard_map.109.refs_1_, bf16[64,16]{1,0:T(8,128)(2,1)S(1)} %get-tuple-element.34.refs_2_, bf16[16,128]{1,0:T(8,128)(2,1)S(1)} %get-tuple-element.27.refs_3_, ...), custom_call_target="tpu_custom_call" | custom-call | tf_op jit(solution)/shard_map/pallas_call | solution.py:331
  28.1 0.0 collective-permute-start.11
  28.1 1.5 %collective-permute-start.10 = (f32[24,256]{1,0:T(8,128)S(1)}, f32[24,256]{1,0:T(8,128)S(1)}, u32[]{:S(2)}, u32[]{:S(2)}) collective-permute-start(f32[24,256]{1,0:T(8,128)S(1)} %get-tuple-element.36.refs_6_), channel_id=1, source_target_pairs={{0,2},{1,3},{2,0},{3,1},{4,6},{5,7},{6,4},{7,5},{8,10},{9,11},{10,... | collective-permute-start | bytes 73736 | tf_op jit(solution)/shard_map/ppermute | solution.py:23
  29.6 0.3 collective-permute-start.9
  29.9 1.6 %collective-permute-done.11.refs_9_ = f32[24,256]{1,0:T(8,128)S(1)} collective-permute-done((f32[24,256]{1,0:T(8,128)S(1)}, f32[24,256]{1,0:T(8,128)S(1)}, u32[]{:S(2)}, u32[]{:S(2)}) %collective-permute-start.11) | collective-permute-done | bytes 24608 | tf_op jit(solution)/shard_map/ppermute | solution.py:23
  31.6 0.4 collective-permute-done.10.refs_8_
  32.0 0.0 collective-permute-done.9.refs_7_
  32.0 1.4 %shard_map.111 = (f32[24,256]{1,0:T(8,128)S(1)}, f32[16,256]{1,0:T(8,128)S(1)}, f32[8,256]{1,0:T(8,128)S(1)}) custom-call(bf16[48,256,256]{2,1,0:T(8,128)(2,1)S(1)} %get-tuple-element.25.refs_1_.low.refs_0_, bf16[16,256,256]{2,1,0:T(8,128)(2,1)S(1)} %get-tuple-element.30.high.refs_1_, bf16[64,16]{1,0:T(8,128)(2,1)S(1)} %get-tuple-element.32.refs_2_, ...), custom_call_target="tpu_custom_call" | custom-call | tf_op jit(solution)/shard_map/pallas_call | solution.py:331
  33.4 0.8 %collective-permute-start.14 = (f32[24,256]{1,0:T(8,128)S(1)}, f32[24,256]{1,0:T(8,128)S(1)}, u32[]{:S(2)}, u32[]{:S(2)}) collective-permute-start(f32[24,256]{1,0:T(8,128)S(1)} %get-tuple-element.38.refs_8_), channel_id=1, source_target_pairs={{0,8},{4,12},{8,0},{12,4},{1,9},{5,13},{9,1},{13,5},{2,10},{6,14},... | collective-permute-start | bytes 73736 | tf_op jit(solution)/shard_map/ppermute | solution.py:23
  34.1 1.5 %collective-permute-start.13 = (f32[24,256]{1,0:T(8,128)S(1)}, f32[24,256]{1,0:T(8,128)S(1)}, u32[]{:S(2)}, u32[]{:S(2)}) collective-permute-start(f32[24,256]{1,0:T(8,128)S(1)} %get-tuple-element.38.refs_8_), channel_id=1, source_target_pairs={{0,12},{4,8},{8,4},{12,0},{1,13},{5,9},{9,5},{13,1},{2,14},{6,10},... | collective-permute-start | bytes 73736 | tf_op jit(solution)/shard_map/ppermute | solution.py:23
  35.6 1.3 %collective-permute-start.12 = (f32[24,256]{1,0:T(8,128)S(1)}, f32[24,256]{1,0:T(8,128)S(1)}, u32[]{:S(2)}, u32[]{:S(2)}) collective-permute-start(f32[24,256]{1,0:T(8,128)S(1)} %get-tuple-element.38.refs_8_), channel_id=1, source_target_pairs={{0,4},{4,0},{8,12},{12,8},{1,5},{5,1},{9,13},{13,9},{2,6},{6,2},{1... | collective-permute-start | bytes 73736 | tf_op jit(solution)/shard_map/ppermute | solution.py:23
  36.9 1.3 %collective-permute-done.14.refs_11_ = f32[24,256]{1,0:T(8,128)S(1)} collective-permute-done((f32[24,256]{1,0:T(8,128)S(1)}, f32[24,256]{1,0:T(8,128)S(1)}, u32[]{:S(2)}, u32[]{:S(2)}) %collective-permute-start.14) | collective-permute-done | bytes 24608 | tf_op jit(solution)/shard_map/ppermute | solution.py:23
  38.2 1.7 %collective-permute-done.13.refs_10_ = f32[24,256]{1,0:T(8,128)S(1)} collective-permute-done((f32[24,256]{1,0:T(8,128)S(1)}, f32[24,256]{1,0:T(8,128)S(1)}, u32[]{:S(2)}, u32[]{:S(2)}) %collective-permute-start.13) | collective-permute-done | bytes 24608 | tf_op jit(solution)/shard_map/ppermute | solution.py:23
  39.8 0.0 collective-permute-done.12.refs_9_
  39.8 1.5 %shard_map.112 = (f32[24,256]{1,0:T(8,128)S(1)}, f32[16,256]{1,0:T(8,128)S(1)}, f32[8,128]{1,0:T(8,128)S(1)}) custom-call(bf16[32,256,256]{2,1,0:T(8,128)(2,1)S(1)} %shard_map.107.refs_7_.refs_0_, bf16[32,256,256]{2,1,0:T(8,128)(2,1)S(1)} %shard_map.109.refs_1_, bf16[64,16]{1,0:T(8,128)(2,1)S(1)} %get-tuple-element.34.refs_2_, ...), custom_call_target="tpu_custom_call" | custom-call | tf_op jit(solution)/shard_map/pallas_call | solution.py:331
  41.4 0.0 collective-permute-start.17
  41.4 1.5 %collective-permute-start.16 = (f32[24,256]{1,0:T(8,128)S(1)}, f32[24,256]{1,0:T(8,128)S(1)}, u32[]{:S(2)}, u32[]{:S(2)}) collective-permute-start(f32[24,256]{1,0:T(8,128)S(1)} %get-tuple-element.42.refs_8_), channel_id=1, source_target_pairs={{0,2},{1,3},{2,0},{3,1},{4,6},{5,7},{6,4},{7,5},{8,10},{9,11},{10,... | collective-permute-start | bytes 73736 | tf_op jit(solution)/shard_map/ppermute | solution.py:23
  42.8 0.4 collective-permute-start.15
  43.2 1.6 %collective-permute-done.17.refs_11_ = f32[24,256]{1,0:T(8,128)S(1)} collective-permute-done((f32[24,256]{1,0:T(8,128)S(1)}, f32[24,256]{1,0:T(8,128)S(1)}, u32[]{:S(2)}, u32[]{:S(2)}) %collective-permute-start.17) | collective-permute-done | bytes 24608 | tf_op jit(solution)/shard_map/ppermute | solution.py:23
  44.8 0.4 collective-permute-done.16.refs_10_
  45.2 0.0 collective-permute-done.15.refs_9_
  45.2 1.6 %shard_map.113 = (f32[8,256]{1,0:T(8,128)S(1)}, f32[8,256]{1,0:T(8,128)S(1)}, f32[8,256]{1,0:T(8,128)S(1)}, f32[8,256]{1,0:T(8,128)S(1)}, f32[8,256]{1,0:T(8,128)S(1)}) custom-call(bf16[48,256,256]{2,1,0:T(8,128)(2,1)S(1)} %get-tuple-element.25.refs_1_.low.refs_0_, bf16[16,256,256]{2,1,0:T(8,128)(2,1)S(1)} %get-tuple-element.30.high.refs_1_, ...), custom_call_target="tpu_custom_call" | custom-call | tf_op jit(solution)/shard_map/pallas_call | solution.py:331
  46.8 1.5 %collective-permute-start.18 = (f32[8,256]{1,0:T(8,128)S(1)}, f32[8,256]{1,0:T(8,128)S(1)}, u32[]{:S(2)}, u32[]{:S(2)}) collective-permute-start(f32[8,256]{1,0:T(8,128)S(1)} %get-tuple-element.45), channel_id=1, source_target_pairs={{0,8},{4,12},{8,0},{12,4},{1,9},{5,13},{9,1},{13,5},{2,10},{6,14},... | collective-permute-start | bytes 24584 | tf_op jit(solution)/shard_map/ppermute | solution.py:23
  48.3 1.8 %collective-permute-start.19 = (f32[8,256]{1,0:T(8,128)S(1)}, f32[8,256]{1,0:T(8,128)S(1)}, u32[]{:S(2)}, u32[]{:S(2)}) collective-permute-start(f32[8,256]{1,0:T(8,128)S(1)} %get-tuple-element.46), channel_id=1, source_target_pairs={{0,12},{4,8},{8,4},{12,0},{1,13},{5,9},{9,5},{13,1},{2,14},{6,10},... | collective-permute-start | bytes 24584 | tf_op jit(solution)/shard_map/ppermute | solution.py:23
  50.1 0.2 collective-permute-start.20
  50.3 1.1 %collective-permute-done.18.refs_7_ = f32[8,256]{1,0:T(8,128)S(1)} collective-permute-done((f32[8,256]{1,0:T(8,128)S(1)}, f32[8,256]{1,0:T(8,128)S(1)}, u32[]{:S(2)}, u32[]{:S(2)}) %collective-permute-start.18) | collective-permute-done | bytes 8224 | tf_op jit(solution)/shard_map/ppermute | solution.py:23
  51.4 2.4 %collective-permute-done.19.refs_8_ = f32[8,256]{1,0:T(8,128)S(1)} collective-permute-done((f32[8,256]{1,0:T(8,128)S(1)}, f32[8,256]{1,0:T(8,128)S(1)}, u32[]{:S(2)}, u32[]{:S(2)}) %collective-permute-start.19) | collective-permute-done | bytes 8224 | tf_op jit(solution)/shard_map/ppermute | solution.py:23
  53.7 0.1 collective-permute-done.20.refs_9_
  53.8 0.8 %shard_map.114 = (f32[4,256]{1,0:T(4,128)}, f32[4,256]{1,0:T(4,128)}) custom-call(f32[16,256]{1,0:T(8,128)S(1)} %get-tuple-element.28.refs_6_.refs_5_.refs_0_, f32[16,256]{1,0:T(8,128)S(1)} %get-tuple-element.29.refs_5_.refs_1_, f32[16,256]{1,0:T(8,128)S(1)} %get-tuple-element.35.refs_6_.refs_2_, f32[16,256]{1,0:T(8,128)S(1)} %get-tuple-element.39.refs_3_, ...), custom_call_target="tpu_custom_call" | custom-call | tf_op jit(solution)/shard_map/pallas_call | solution.py:331
Async XLA Ops:
  1.4 8.6 %collective-permute-start.2 = (f32[16,256]{1,0:T(8,128)S(1)}, f32[16,256]{1,0:T(8,128)S(1)}, u32[]{:S(2)}, u32[]{:S(2)}) collective-permute-start(f32[16,256]{1,0:T(8,128)S(1)} %shard_map.104.opening.refs_6_), channel_id=1, source_target_pairs={{0,8},{4,12},{8,0},{12,4},{1,9},{5,13},{9,1},{13,5},{2,10},{6,14},... | collective-permute-start | bytes 49160 | tf_op jit(solution)/shard_map/ppermute | solution.py:23
  5.5 5.5 %collective-permute-start.1 = (f32[16,256]{1,0:T(8,128)S(1)}, f32[16,256]{1,0:T(8,128)S(1)}, u32[]{:S(2)}, u32[]{:S(2)}) collective-permute-start(f32[16,256]{1,0:T(8,128)S(1)} %shard_map.104.opening.refs_6_), channel_id=1, source_target_pairs={{0,12},{4,8},{8,4},{12,0},{1,13},{5,9},{9,5},{13,1},{2,14},{6,10},... | collective-permute-start | bytes 49160 | tf_op jit(solution)/shard_map/ppermute | solution.py:23
  6.8 4.2 %collective-permute-start = (f32[16,256]{1,0:T(8,128)S(1)}, f32[16,256]{1,0:T(8,128)S(1)}, u32[]{:S(2)}, u32[]{:S(2)}) collective-permute-start(f32[16,256]{1,0:T(8,128)S(1)} %shard_map.104.opening.refs_6_), channel_id=1, source_target_pairs={{0,4},{4,0},{8,12},{12,8},{1,5},{5,1},{9,13},{13,9},{2,6},{6,2},{1... | collective-permute-start | bytes 49160 | tf_op jit(solution)/shard_map/ppermute | solution.py:23
  7.1 4.0 %copy-start.2 = (s32[64]{0:T(128)S(1)}, s32[64]{0:T(128)}, u32[]{:S(2)}) copy-start(s32[64]{0:T(128)} %param.12) | copy-start | bytes 772
  13.9 3.4 %collective-permute-start.5 = (f32[16,256]{1,0:T(8,128)S(1)}, f32[16,256]{1,0:T(8,128)S(1)}, u32[]{:S(2)}, u32[]{:S(2)}) collective-permute-start(f32[16,256]{1,0:T(8,128)S(1)} %get-tuple-element.31.part.refs_8_), channel_id=1, source_target_pairs={{0,3},{1,2},{2,1},{3,0},{4,7},{5,6},{6,5},{7,4},{8,11},{9,10},{10,... | collective-permute-start | bytes 49160 | tf_op jit(solution)/shard_map/ppermute | solution.py:23
  14.0 3.8 %collective-permute-start.4 = (f32[16,256]{1,0:T(8,128)S(1)}, f32[16,256]{1,0:T(8,128)S(1)}, u32[]{:S(2)}, u32[]{:S(2)}) collective-permute-start(f32[16,256]{1,0:T(8,128)S(1)} %get-tuple-element.31.part.refs_8_), channel_id=1, source_target_pairs={{0,2},{1,3},{2,0},{3,1},{4,6},{5,7},{6,4},{7,5},{8,10},{9,11},{10,... | collective-permute-start | bytes 49160 | tf_op jit(solution)/shard_map/ppermute | solution.py:23
  15.6 2.3 %collective-permute-start.3 = (f32[16,256]{1,0:T(8,128)S(1)}, f32[16,256]{1,0:T(8,128)S(1)}, u32[]{:S(2)}, u32[]{:S(2)}) collective-permute-start(f32[16,256]{1,0:T(8,128)S(1)} %get-tuple-element.31.part.refs_8_), channel_id=1, source_target_pairs={{0,1},{1,0},{2,3},{3,2},{4,5},{5,4},{6,7},{7,6},{8,9},{9,8},{10,11... | collective-permute-start | bytes 49160 | tf_op jit(solution)/shard_map/ppermute | solution.py:23
  15.9 2.0 %copy-start = (f32[16,256]{1,0:T(8,128)S(1)}, f32[16,256]{1,0:T(8,128)}, u32[]{:S(2)}) copy-start(f32[16,256]{1,0:T(8,128)} %refs_5_.5) | copy-start | bytes 49156
  15.9 2.0 %copy-start.1 = (f32[16,256]{1,0:T(8,128)S(1)}, f32[16,256]{1,0:T(8,128)}, u32[]{:S(2)}) copy-start(f32[16,256]{1,0:T(8,128)} %refs_5_.3) | copy-start | bytes 49156
  19.2 4.7 %collective-permute-start.8 = (f32[16,256]{1,0:T(8,128)S(1)}, f32[16,256]{1,0:T(8,128)S(1)}, u32[]{:S(2)}, u32[]{:S(2)}) collective-permute-start(f32[16,256]{1,0:T(8,128)S(1)} %shard_map.108.part.refs_7_), channel_id=1, source_target_pairs={{0,8},{4,12},{8,0},{12,4},{1,9},{5,13},{9,1},{13,5},{2,10},{6,14},... | collective-permute-start | bytes 49160 | tf_op jit(solution)/shard_map/ppermute | solution.py:23
  21.1 5.5 %collective-permute-start.7 = (f32[16,256]{1,0:T(8,128)S(1)}, f32[16,256]{1,0:T(8,128)S(1)}, u32[]{:S(2)}, u32[]{:S(2)}) collective-permute-start(f32[16,256]{1,0:T(8,128)S(1)} %shard_map.108.part.refs_7_), channel_id=1, source_target_pairs={{0,12},{4,8},{8,4},{12,0},{1,13},{5,9},{9,5},{13,1},{2,14},{6,10},... | collective-permute-start | bytes 49160 | tf_op jit(solution)/shard_map/ppermute | solution.py:23
  22.5 4.2 %collective-permute-start.6 = (f32[16,256]{1,0:T(8,128)S(1)}, f32[16,256]{1,0:T(8,128)S(1)}, u32[]{:S(2)}, u32[]{:S(2)}) collective-permute-start(f32[16,256]{1,0:T(8,128)S(1)} %shard_map.108.part.refs_7_), channel_id=1, source_target_pairs={{0,4},{4,0},{8,12},{12,8},{1,5},{5,1},{9,13},{13,9},{2,6},{6,2},{1... | collective-permute-start | bytes 49160 | tf_op jit(solution)/shard_map/ppermute | solution.py:23
  28.1 3.5 %collective-permute-start.11 = (f32[24,256]{1,0:T(8,128)S(1)}, f32[24,256]{1,0:T(8,128)S(1)}, u32[]{:S(2)}, u32[]{:S(2)}) collective-permute-start(f32[24,256]{1,0:T(8,128)S(1)} %get-tuple-element.36.refs_6_), channel_id=1, source_target_pairs={{0,3},{1,2},{2,1},{3,0},{4,7},{5,6},{6,5},{7,4},{8,11},{9,10},{10,... | collective-permute-start | bytes 73736 | tf_op jit(solution)/shard_map/ppermute | solution.py:23
  28.1 3.9 %collective-permute-start.10 = (f32[24,256]{1,0:T(8,128)S(1)}, f32[24,256]{1,0:T(8,128)S(1)}, u32[]{:S(2)}, u32[]{:S(2)}) collective-permute-start(f32[24,256]{1,0:T(8,128)S(1)} %get-tuple-element.36.refs_6_), channel_id=1, source_target_pairs={{0,2},{1,3},{2,0},{3,1},{4,6},{5,7},{6,4},{7,5},{8,10},{9,11},{10,... | collective-permute-start | bytes 73736 | tf_op jit(solution)/shard_map/ppermute | solution.py:23
  29.6 2.4 %collective-permute-start.9 = (f32[24,256]{1,0:T(8,128)S(1)}, f32[24,256]{1,0:T(8,128)S(1)}, u32[]{:S(2)}, u32[]{:S(2)}) collective-permute-start(f32[24,256]{1,0:T(8,128)S(1)} %get-tuple-element.36.refs_6_), channel_id=1, source_target_pairs={{0,1},{1,0},{2,3},{3,2},{4,5},{5,4},{6,7},{7,6},{8,9},{9,8},{10,11... | collective-permute-start | bytes 73736 | tf_op jit(solution)/shard_map/ppermute | solution.py:23
  33.4 4.8 %collective-permute-start.14 = (f32[24,256]{1,0:T(8,128)S(1)}, f32[24,256]{1,0:T(8,128)S(1)}, u32[]{:S(2)}, u32[]{:S(2)}) collective-permute-start(f32[24,256]{1,0:T(8,128)S(1)} %get-tuple-element.38.refs_8_), channel_id=1, source_target_pairs={{0,8},{4,12},{8,0},{12,4},{1,9},{5,13},{9,1},{13,5},{2,10},{6,14},... | collective-permute-start | bytes 73736 | tf_op jit(solution)/shard_map/ppermute | solution.py:23
  34.1 5.7 %collective-permute-start.13 = (f32[24,256]{1,0:T(8,128)S(1)}, f32[24,256]{1,0:T(8,128)S(1)}, u32[]{:S(2)}, u32[]{:S(2)}) collective-permute-start(f32[24,256]{1,0:T(8,128)S(1)} %get-tuple-element.38.refs_8_), channel_id=1, source_target_pairs={{0,12},{4,8},{8,4},{12,0},{1,13},{5,9},{9,5},{13,1},{2,14},{6,10},... | collective-permute-start | bytes 73736 | tf_op jit(solution)/shard_map/ppermute | solution.py:23
  35.6 4.2 %collective-permute-start.12 = (f32[24,256]{1,0:T(8,128)S(1)}, f32[24,256]{1,0:T(8,128)S(1)}, u32[]{:S(2)}, u32[]{:S(2)}) collective-permute-start(f32[24,256]{1,0:T(8,128)S(1)} %get-tuple-element.38.refs_8_), channel_id=1, source_target_pairs={{0,4},{4,0},{8,12},{12,8},{1,5},{5,1},{9,13},{13,9},{2,6},{6,2},{1... | collective-permute-start | bytes 73736 | tf_op jit(solution)/shard_map/ppermute | solution.py:23
  41.4 3.5 %collective-permute-start.17 = (f32[24,256]{1,0:T(8,128)S(1)}, f32[24,256]{1,0:T(8,128)S(1)}, u32[]{:S(2)}, u32[]{:S(2)}) collective-permute-start(f32[24,256]{1,0:T(8,128)S(1)} %get-tuple-element.42.refs_8_), channel_id=1, source_target_pairs={{0,3},{1,2},{2,1},{3,0},{4,7},{5,6},{6,5},{7,4},{8,11},{9,10},{10,... | collective-permute-start | bytes 73736 | tf_op jit(solution)/shard_map/ppermute | solution.py:23
  41.4 3.9 %collective-permute-start.16 = (f32[24,256]{1,0:T(8,128)S(1)}, f32[24,256]{1,0:T(8,128)S(1)}, u32[]{:S(2)}, u32[]{:S(2)}) collective-permute-start(f32[24,256]{1,0:T(8,128)S(1)} %get-tuple-element.42.refs_8_), channel_id=1, source_target_pairs={{0,2},{1,3},{2,0},{3,1},{4,6},{5,7},{6,4},{7,5},{8,10},{9,11},{10,... | collective-permute-start | bytes 73736 | tf_op jit(solution)/shard_map/ppermute | solution.py:23
  42.8 2.4 %collective-permute-start.15 = (f32[24,256]{1,0:T(8,128)S(1)}, f32[24,256]{1,0:T(8,128)S(1)}, u32[]{:S(2)}, u32[]{:S(2)}) collective-permute-start(f32[24,256]{1,0:T(8,128)S(1)} %get-tuple-element.42.refs_8_), channel_id=1, source_target_pairs={{0,1},{1,0},{2,3},{3,2},{4,5},{5,4},{6,7},{7,6},{8,9},{9,8},{10,11... | collective-permute-start | bytes 73736 | tf_op jit(solution)/shard_map/ppermute | solution.py:23
  46.8 4.6 %collective-permute-start.18 = (f32[8,256]{1,0:T(8,128)S(1)}, f32[8,256]{1,0:T(8,128)S(1)}, u32[]{:S(2)}, u32[]{:S(2)}) collective-permute-start(f32[8,256]{1,0:T(8,128)S(1)} %get-tuple-element.45), channel_id=1, source_target_pairs={{0,8},{4,12},{8,0},{12,4},{1,9},{5,13},{9,1},{13,5},{2,10},{6,14},... | collective-permute-start | bytes 24584 | tf_op jit(solution)/shard_map/ppermute | solution.py:23
  48.3 5.5 %collective-permute-start.19 = (f32[8,256]{1,0:T(8,128)S(1)}, f32[8,256]{1,0:T(8,128)S(1)}, u32[]{:S(2)}, u32[]{:S(2)}) collective-permute-start(f32[8,256]{1,0:T(8,128)S(1)} %get-tuple-element.46), channel_id=1, source_target_pairs={{0,12},{4,8},{8,4},{12,0},{1,13},{5,9},{9,5},{13,1},{2,14},{6,10},... | collective-permute-start | bytes 24584 | tf_op jit(solution)/shard_map/ppermute | solution.py:23
  50.1 3.7 %collective-permute-start.20 = (f32[8,256]{1,0:T(8,128)S(1)}, f32[8,256]{1,0:T(8,128)S(1)}, u32[]{:S(2)}, u32[]{:S(2)}) collective-permute-start(f32[8,256]{1,0:T(8,128)S(1)} %get-tuple-element.47), channel_id=1, source_target_pairs={{0,4},{4,0},{8,12},{12,8},{1,5},{5,1},{9,13},{13,9},{2,6},{6,2},{1... | collective-permute-start | bytes 24584 | tf_op jit(solution)/shard_map/ppermute | solution.py:23

commit v6 on v5

--- a/solution.py
+++ b/solution.py
@@ -11,7 +11,7 @@
 EXTRA = 8
 LIMIT = 16 * 1024 * 1024
 GROUP = 16
-CHUNK = 8
+CHUNK = 16
 F32 = jnp.float32
 BF16 = jnp.bfloat16
 

time: 54.8 us -> 54.8 us (level)
  transfers between devices with their start and end apart: 21 -> 21, of which waited for: 13 -> 13; matrix products, arithmetic and copies ran while one was open for 0% -> 0% of each run, Pallas kernels for 9% -> 10%
where the time goes in v6:
time: 54.8 us; the launch traced here: 54.5 us
  starting transfers between devices  21.9 us (40%)
  Pallas kernels  16.9 us (31%)
  waiting for transfers between devices  15.1 us (28%)
  between operations  0.72 us (1%)
    ppermute x21, starting transfers between devices, exchange(): parts[shift] = lax.ppermute(values[shift], axes, perm)  21.9 us
    pallas_call x11, Pallas kernels, call(): pl.pallas_call(body, out_shape=[jax.ShapeDtypeStruct(shape, dtype) for sh...  16.9 us
    ppermute x21, waiting for transfers between devices, exchange(): parts[shift] = lax.ppermute(values[shift], axes, perm)  15.1 us
  transfers between devices with their start and end apart: 21, of which 13 were waited for; matrix products, arithmetic and copies ran while one was open for 0% of the time, Pallas kernels for 10%

profile of v6, /device:TPU:0, one launch (start us, length us, event | category | flops | bytes accessed | tf_op | source)
XLA Modules:
  0.0 54.5 jit_solution(4298323479178683244)
XLA Ops:
  0.6 0.7 %shard_map.104.opening.refs_6_ = f32[16,256]{1,0:T(8,128)S(1)} custom-call(f32[4,256]{1,0:T(4,128)} %start.1, f32[4,256]{1,0:T(4,128)} %weight.1, s32[2,4]{1,0:T(2,128)} %bitcast.8), custom_call_target="tpu_custom_call" | custom-call | tf_op jit(solution)/shard_map/pallas_call | solution.py:331
  1.4 4.1 %collective-permute-start.2 = (f32[16,256]{1,0:T(8,128)S(1)}, f32[16,256]{1,0:T(8,128)S(1)}, u32[]{:S(2)}, u32[]{:S(2)}) collective-permute-start(f32[16,256]{1,0:T(8,128)S(1)} %shard_map.104.opening.refs_6_), channel_id=1, source_target_pairs={{0,8},{4,12},{8,0},{12,4},{1,9},{5,13},{9,1},{13,5},{2,10},{6,14},... | collective-permute-start | bytes 49160 | tf_op jit(solution)/shard_map/ppermute | solution.py:23
  5.5 1.3 %collective-permute-start.1 = (f32[16,256]{1,0:T(8,128)S(1)}, f32[16,256]{1,0:T(8,128)S(1)}, u32[]{:S(2)}, u32[]{:S(2)}) collective-permute-start(f32[16,256]{1,0:T(8,128)S(1)} %shard_map.104.opening.refs_6_), channel_id=1, source_target_pairs={{0,12},{4,8},{8,4},{12,0},{1,13},{5,9},{9,5},{13,1},{2,14},{6,10},... | collective-permute-start | bytes 49160 | tf_op jit(solution)/shard_map/ppermute | solution.py:23
  6.8 0.2 collective-permute-start
  7.1 0.0 copy-start.2
  7.1 2.9 %shard_map.105 = (bf16[48,256,256]{2,1,0:T(8,128)(2,1)S(1)}, bf16[64,16]{1,0:T(8,128)(2,1)S(1)}, bf16[16,128]{1,0:T(8,128)(2,1)S(1)}, f32[64,256]{1,0:T(8,128)S(1)}) custom-call(bf16[64,256,256]{2,1,0:T(8,128)(2,1)} %refs_0_.1, f32[16,256]{1,0:T(8,128)S(1)} %shard_map.104.opening.refs_6_, f32[1,64]{1,0:T(1,128)} %bitcast.9, s32[1,64]{1,0:T(1,128)} %bitcast.10), custom_call_target="tpu_custom_call" | custom-call | tf_op jit(solution)/shard_map/pallas_call | solution.py:331
  10.0 0.0 collective-permute-done.2.refs_9_
  10.0 1.0 %collective-permute-done.1.refs_8_ = f32[16,256]{1,0:T(8,128)S(1)} collective-permute-done((f32[16,256]{1,0:T(8,128)S(1)}, f32[16,256]{1,0:T(8,128)S(1)}, u32[]{:S(2)}, u32[]{:S(2)}) %collective-permute-start.1) | collective-permute-done | bytes 16416 | tf_op jit(solution)/shard_map/ppermute | solution.py:23
  11.0 0.0 collective-permute-done.refs_7_
  11.0 0.0 copy-done.2
  11.0 2.8 %shard_map.106 = (f32[16,256]{1,0:T(8,128)S(1)}, bf16[16,256,256]{2,1,0:T(8,128)(2,1)S(1)}, bf16[64,16]{1,0:T(8,128)(2,1)S(1)}, bf16[16,128]{1,0:T(8,128)(2,1)S(...) custom-call(bf16[64,256,256]{2,1,0:T(8,128)(2,1)} %refs_0_.1, ...), custom_call_target="tpu_custom_call" | custom-call | tf_op jit(solution)/shard_map/pallas_call | solution.py:331
  13.8 0.1 collective-permute-start.5
  13.9 1.6 %collective-permute-start.4 = (f32[16,256]{1,0:T(8,128)S(1)}, f32[16,256]{1,0:T(8,128)S(1)}, u32[]{:S(2)}, u32[]{:S(2)}) collective-permute-start(f32[16,256]{1,0:T(8,128)S(1)} %get-tuple-element.31.part.refs_8_), channel_id=1, source_target_pairs={{0,2},{1,3},{2,0},{3,1},{4,6},{5,7},{6,4},{7,5},{8,10},{9,11},{10,... | collective-permute-start | bytes 49160 | tf_op jit(solution)/shard_map/ppermute | solution.py:23
  15.4 0.3 collective-permute-start.3
  15.7 0.0 copy-start
  15.7 0.0 copy-start.1
  15.7 1.1 %shard_map.107.refs_7_.refs_0_ = bf16[32,256,256]{2,1,0:T(8,128)(2,1)S(1)} custom-call(bf16[48,256,256]{2,1,0:T(8,128)(2,1)S(1)} %get-tuple-element.25.refs_1_.low.refs_0_, bf16[16,256,256]{2,1,0:T(8,128)(2,1)S(1)} %get-tuple-element.30.high.refs_1_, f32[16,256]{1,0:T(8,128)S(1)} %get-tuple-element.31.part.refs_8_), custom_call_target="tpu_custom_call" | custom-call | tf_op jit(solution)/shard_map/pallas_call | solution.py:331
  16.9 0.3 collective-permute-done.5.refs_11_
  17.2 0.5 collective-permute-done.4.refs_10_
  17.7 0.0 collective-permute-done.3.refs_9_
  17.7 0.0 copy-done
  17.7 0.0 copy-done.1
  17.7 1.4 %shard_map.108.part.refs_7_ = f32[16,256]{1,0:T(8,128)S(1)} custom-call(bf16[48,256,256]{2,1,0:T(8,128)(2,1)S(1)} %get-tuple-element.25.refs_1_.low.refs_0_, bf16[16,256,256]{2,1,0:T(8,128)(2,1)S(1)} %get-tuple-element.30.high.refs_1_, bf16[64,16]{1,0:T(8,128)(2,1)S(1)} %get-tuple-element.32.refs_2_, bf16[16,128]{1,0:T(8,128)(2,1)S(1)} %get-tuple-element.33.refs_3_, ...), custom_call_target="tpu_custom_call" | custom-call | tf_op jit(solution)/shard_map/pallas_call | solution.py:331
  19.1 1.9 %collective-permute-start.8 = (f32[16,256]{1,0:T(8,128)S(1)}, f32[16,256]{1,0:T(8,128)S(1)}, u32[]{:S(2)}, u32[]{:S(2)}) collective-permute-start(f32[16,256]{1,0:T(8,128)S(1)} %shard_map.108.part.refs_7_), channel_id=1, source_target_pairs={{0,8},{4,12},{8,0},{12,4},{1,9},{5,13},{9,1},{13,5},{2,10},{6,14},... | collective-permute-start | bytes 49160 | tf_op jit(solution)/shard_map/ppermute | solution.py:23
  21.0 1.4 %collective-permute-start.7 = (f32[16,256]{1,0:T(8,128)S(1)}, f32[16,256]{1,0:T(8,128)S(1)}, u32[]{:S(2)}, u32[]{:S(2)}) collective-permute-start(f32[16,256]{1,0:T(8,128)S(1)} %shard_map.108.part.refs_7_), channel_id=1, source_target_pairs={{0,12},{4,8},{8,4},{12,0},{1,13},{5,9},{9,5},{13,1},{2,14},{6,10},... | collective-permute-start | bytes 49160 | tf_op jit(solution)/shard_map/ppermute | solution.py:23
  22.4 0.3 collective-permute-start.6
  22.6 1.1 %shard_map.109.refs_1_ = bf16[32,256,256]{2,1,0:T(8,128)(2,1)S(1)} custom-call(bf16[48,256,256]{2,1,0:T(8,128)(2,1)S(1)} %get-tuple-element.25.refs_1_.low.refs_0_, bf16[16,256,256]{2,1,0:T(8,128)(2,1)S(1)} %get-tuple-element.30.high.refs_1_, f32[16,256]{1,0:T(8,128)S(1)} %shard_map.108.part.refs_7_), custom_call_target="tpu_custom_call" | custom-call | tf_op jit(solution)/shard_map/pallas_call | solution.py:331
  23.8 0.0 collective-permute-done.8.refs_10_
  23.8 2.8 %collective-permute-done.7.refs_9_ = f32[16,256]{1,0:T(8,128)S(1)} collective-permute-done((f32[16,256]{1,0:T(8,128)S(1)}, f32[16,256]{1,0:T(8,128)S(1)}, u32[]{:S(2)}, u32[]{:S(2)}) %collective-permute-start.7) | collective-permute-done | bytes 16416 | tf_op jit(solution)/shard_map/ppermute | solution.py:23
  26.5 0.0 collective-permute-done.6.refs_8_
  26.5 1.4 %shard_map.110 = (f32[24,256]{1,0:T(8,128)S(1)}, f32[16,256]{1,0:T(8,128)S(1)}) custom-call(bf16[32,256,256]{2,1,0:T(8,128)(2,1)S(1)} %shard_map.107.refs_7_.refs_0_, bf16[32,256,256]{2,1,0:T(8,128)(2,1)S(1)} %shard_map.109.refs_1_, bf16[64,16]{1,0:T(8,128)(2,1)S(1)} %get-tuple-element.34.refs_2_, bf16[16,128]{1,0:T(8,128)(2,1)S(1)} %get-tuple-element.27.refs_3_, ...), custom_call_target="tpu_custom_call" | custom-call | tf_op jit(solution)/shard_map/pallas_call | solution.py:331
  28.0 0.0 collective-permute-start.11
  28.0 1.5 %collective-permute-start.10 = (f32[24,256]{1,0:T(8,128)S(1)}, f32[24,256]{1,0:T(8,128)S(1)}, u32[]{:S(2)}, u32[]{:S(2)}) collective-permute-start(f32[24,256]{1,0:T(8,128)S(1)} %get-tuple-element.36.refs_6_), channel_id=1, source_target_pairs={{0,2},{1,3},{2,0},{3,1},{4,6},{5,7},{6,4},{7,5},{8,10},{9,11},{10,... | collective-permute-start | bytes 73736 | tf_op jit(solution)/shard_map/ppermute | solution.py:23
  29.5 0.3 collective-permute-start.9
  29.8 1.6 %collective-permute-done.11.refs_9_ = f32[24,256]{1,0:T(8,128)S(1)} collective-permute-done((f32[24,256]{1,0:T(8,128)S(1)}, f32[24,256]{1,0:T(8,128)S(1)}, u32[]{:S(2)}, u32[]{:S(2)}) %collective-permute-start.11) | collective-permute-done | bytes 24608 | tf_op jit(solution)/shard_map/ppermute | solution.py:23
  31.5 0.4 collective-permute-done.10.refs_8_
  31.9 0.0 collective-permute-done.9.refs_7_
  31.9 1.4 %shard_map.111 = (f32[24,256]{1,0:T(8,128)S(1)}, f32[16,256]{1,0:T(8,128)S(1)}, f32[8,256]{1,0:T(8,128)S(1)}) custom-call(bf16[48,256,256]{2,1,0:T(8,128)(2,1)S(1)} %get-tuple-element.25.refs_1_.low.refs_0_, bf16[16,256,256]{2,1,0:T(8,128)(2,1)S(1)} %get-tuple-element.30.high.refs_1_, bf16[64,16]{1,0:T(8,128)(2,1)S(1)} %get-tuple-element.32.refs_2_, ...), custom_call_target="tpu_custom_call" | custom-call | tf_op jit(solution)/shard_map/pallas_call | solution.py:331
  33.3 0.8 %collective-permute-start.14 = (f32[24,256]{1,0:T(8,128)S(1)}, f32[24,256]{1,0:T(8,128)S(1)}, u32[]{:S(2)}, u32[]{:S(2)}) collective-permute-start(f32[24,256]{1,0:T(8,128)S(1)} %get-tuple-element.38.refs_8_), channel_id=1, source_target_pairs={{0,8},{4,12},{8,0},{12,4},{1,9},{5,13},{9,1},{13,5},{2,10},{6,14},... | collective-permute-start | bytes 73736 | tf_op jit(solution)/shard_map/ppermute | solution.py:23
  34.0 1.5 %collective-permute-start.13 = (f32[24,256]{1,0:T(8,128)S(1)}, f32[24,256]{1,0:T(8,128)S(1)}, u32[]{:S(2)}, u32[]{:S(2)}) collective-permute-start(f32[24,256]{1,0:T(8,128)S(1)} %get-tuple-element.38.refs_8_), channel_id=1, source_target_pairs={{0,12},{4,8},{8,4},{12,0},{1,13},{5,9},{9,5},{13,1},{2,14},{6,10},... | collective-permute-start | bytes 73736 | tf_op jit(solution)/shard_map/ppermute | solution.py:23
  35.5 1.3 %collective-permute-start.12 = (f32[24,256]{1,0:T(8,128)S(1)}, f32[24,256]{1,0:T(8,128)S(1)}, u32[]{:S(2)}, u32[]{:S(2)}) collective-permute-start(f32[24,256]{1,0:T(8,128)S(1)} %get-tuple-element.38.refs_8_), channel_id=1, source_target_pairs={{0,4},{4,0},{8,12},{12,8},{1,5},{5,1},{9,13},{13,9},{2,6},{6,2},{1... | collective-permute-start | bytes 73736 | tf_op jit(solution)/shard_map/ppermute | solution.py:23
  36.8 1.3 %collective-permute-done.14.refs_11_ = f32[24,256]{1,0:T(8,128)S(1)} collective-permute-done((f32[24,256]{1,0:T(8,128)S(1)}, f32[24,256]{1,0:T(8,128)S(1)}, u32[]{:S(2)}, u32[]{:S(2)}) %collective-permute-start.14) | collective-permute-done | bytes 24608 | tf_op jit(solution)/shard_map/ppermute | solution.py:23
  38.1 1.7 %collective-permute-done.13.refs_10_ = f32[24,256]{1,0:T(8,128)S(1)} collective-permute-done((f32[24,256]{1,0:T(8,128)S(1)}, f32[24,256]{1,0:T(8,128)S(1)}, u32[]{:S(2)}, u32[]{:S(2)}) %collective-permute-start.13) | collective-permute-done | bytes 24608 | tf_op jit(solution)/shard_map/ppermute | solution.py:23
  39.7 0.0 collective-permute-done.12.refs_9_
  39.7 1.5 %shard_map.112 = (f32[24,256]{1,0:T(8,128)S(1)}, f32[16,256]{1,0:T(8,128)S(1)}, f32[8,128]{1,0:T(8,128)S(1)}) custom-call(bf16[32,256,256]{2,1,0:T(8,128)(2,1)S(1)} %shard_map.107.refs_7_.refs_0_, bf16[32,256,256]{2,1,0:T(8,128)(2,1)S(1)} %shard_map.109.refs_1_, bf16[64,16]{1,0:T(8,128)(2,1)S(1)} %get-tuple-element.34.refs_2_, ...), custom_call_target="tpu_custom_call" | custom-call | tf_op jit(solution)/shard_map/pallas_call | solution.py:331
  41.3 0.0 collective-permute-start.17
  41.3 1.5 %collective-permute-start.16 = (f32[24,256]{1,0:T(8,128)S(1)}, f32[24,256]{1,0:T(8,128)S(1)}, u32[]{:S(2)}, u32[]{:S(2)}) collective-permute-start(f32[24,256]{1,0:T(8,128)S(1)} %get-tuple-element.42.refs_8_), channel_id=1, source_target_pairs={{0,2},{1,3},{2,0},{3,1},{4,6},{5,7},{6,4},{7,5},{8,10},{9,11},{10,... | collective-permute-start | bytes 73736 | tf_op jit(solution)/shard_map/ppermute | solution.py:23
  42.7 0.4 collective-permute-start.15
  43.1 1.6 %collective-permute-done.17.refs_11_ = f32[24,256]{1,0:T(8,128)S(1)} collective-permute-done((f32[24,256]{1,0:T(8,128)S(1)}, f32[24,256]{1,0:T(8,128)S(1)}, u32[]{:S(2)}, u32[]{:S(2)}) %collective-permute-start.17) | collective-permute-done | bytes 24608 | tf_op jit(solution)/shard_map/ppermute | solution.py:23
  44.7 0.4 collective-permute-done.16.refs_10_
  45.1 0.0 collective-permute-done.15.refs_9_
  45.2 1.6 %shard_map.113 = (f32[8,256]{1,0:T(8,128)S(1)}, f32[8,256]{1,0:T(8,128)S(1)}, f32[8,256]{1,0:T(8,128)S(1)}, f32[8,256]{1,0:T(8,128)S(1)}, f32[8,256]{1,0:T(8,128)S(1)}) custom-call(bf16[48,256,256]{2,1,0:T(8,128)(2,1)S(1)} %get-tuple-element.25.refs_1_.low.refs_0_, bf16[16,256,256]{2,1,0:T(8,128)(2,1)S(1)} %get-tuple-element.30.high.refs_1_, ...), custom_call_target="tpu_custom_call" | custom-call | tf_op jit(solution)/shard_map/pallas_call | solution.py:331
  46.7 1.5 %collective-permute-start.18 = (f32[8,256]{1,0:T(8,128)S(1)}, f32[8,256]{1,0:T(8,128)S(1)}, u32[]{:S(2)}, u32[]{:S(2)}) collective-permute-start(f32[8,256]{1,0:T(8,128)S(1)} %get-tuple-element.45), channel_id=1, source_target_pairs={{0,8},{4,12},{8,0},{12,4},{1,9},{5,13},{9,1},{13,5},{2,10},{6,14},... | collective-permute-start | bytes 24584 | tf_op jit(solution)/shard_map/ppermute | solution.py:23
  48.2 1.8 %collective-permute-start.19 = (f32[8,256]{1,0:T(8,128)S(1)}, f32[8,256]{1,0:T(8,128)S(1)}, u32[]{:S(2)}, u32[]{:S(2)}) collective-permute-start(f32[8,256]{1,0:T(8,128)S(1)} %get-tuple-element.46), channel_id=1, source_target_pairs={{0,12},{4,8},{8,4},{12,0},{1,13},{5,9},{9,5},{13,1},{2,14},{6,10},... | collective-permute-start | bytes 24584 | tf_op jit(solution)/shard_map/ppermute | solution.py:23
  50.0 0.2 collective-permute-start.20
  50.2 1.1 %collective-permute-done.18.refs_7_ = f32[8,256]{1,0:T(8,128)S(1)} collective-permute-done((f32[8,256]{1,0:T(8,128)S(1)}, f32[8,256]{1,0:T(8,128)S(1)}, u32[]{:S(2)}, u32[]{:S(2)}) %collective-permute-start.18) | collective-permute-done | bytes 8224 | tf_op jit(solution)/shard_map/ppermute | solution.py:23
  51.3 2.4 %collective-permute-done.19.refs_8_ = f32[8,256]{1,0:T(8,128)S(1)} collective-permute-done((f32[8,256]{1,0:T(8,128)S(1)}, f32[8,256]{1,0:T(8,128)S(1)}, u32[]{:S(2)}, u32[]{:S(2)}) %collective-permute-start.19) | collective-permute-done | bytes 8224 | tf_op jit(solution)/shard_map/ppermute | solution.py:23
  53.7 0.1 collective-permute-done.20.refs_9_
  53.7 0.8 %shard_map.114 = (f32[4,256]{1,0:T(4,128)}, f32[4,256]{1,0:T(4,128)}) custom-call(f32[16,256]{1,0:T(8,128)S(1)} %get-tuple-element.28.refs_6_.refs_5_.refs_0_, f32[16,256]{1,0:T(8,128)S(1)} %get-tuple-element.29.refs_5_.refs_1_, f32[16,256]{1,0:T(8,128)S(1)} %get-tuple-element.35.refs_6_.refs_2_, f32[16,256]{1,0:T(8,128)S(1)} %get-tuple-element.39.refs_3_, ...), custom_call_target="tpu_custom_call" | custom-call | tf_op jit(solution)/shard_map/pallas_call | solution.py:331
Async XLA Ops:
  1.4 8.6 %collective-permute-start.2 = (f32[16,256]{1,0:T(8,128)S(1)}, f32[16,256]{1,0:T(8,128)S(1)}, u32[]{:S(2)}, u32[]{:S(2)}) collective-permute-start(f32[16,256]{1,0:T(8,128)S(1)} %shard_map.104.opening.refs_6_), channel_id=1, source_target_pairs={{0,8},{4,12},{8,0},{12,4},{1,9},{5,13},{9,1},{13,5},{2,10},{6,14},... | collective-permute-start | bytes 49160 | tf_op jit(solution)/shard_map/ppermute | solution.py:23
  5.5 5.5 %collective-permute-start.1 = (f32[16,256]{1,0:T(8,128)S(1)}, f32[16,256]{1,0:T(8,128)S(1)}, u32[]{:S(2)}, u32[]{:S(2)}) collective-permute-start(f32[16,256]{1,0:T(8,128)S(1)} %shard_map.104.opening.refs_6_), channel_id=1, source_target_pairs={{0,12},{4,8},{8,4},{12,0},{1,13},{5,9},{9,5},{13,1},{2,14},{6,10},... | collective-permute-start | bytes 49160 | tf_op jit(solution)/shard_map/ppermute | solution.py:23
  6.8 4.2 %collective-permute-start = (f32[16,256]{1,0:T(8,128)S(1)}, f32[16,256]{1,0:T(8,128)S(1)}, u32[]{:S(2)}, u32[]{:S(2)}) collective-permute-start(f32[16,256]{1,0:T(8,128)S(1)} %shard_map.104.opening.refs_6_), channel_id=1, source_target_pairs={{0,4},{4,0},{8,12},{12,8},{1,5},{5,1},{9,13},{13,9},{2,6},{6,2},{1... | collective-permute-start | bytes 49160 | tf_op jit(solution)/shard_map/ppermute | solution.py:23
  7.1 4.0 %copy-start.2 = (s32[64]{0:T(128)S(1)}, s32[64]{0:T(128)}, u32[]{:S(2)}) copy-start(s32[64]{0:T(128)} %param.12) | copy-start | bytes 772
  13.8 3.4 %collective-permute-start.5 = (f32[16,256]{1,0:T(8,128)S(1)}, f32[16,256]{1,0:T(8,128)S(1)}, u32[]{:S(2)}, u32[]{:S(2)}) collective-permute-start(f32[16,256]{1,0:T(8,128)S(1)} %get-tuple-element.31.part.refs_8_), channel_id=1, source_target_pairs={{0,3},{1,2},{2,1},{3,0},{4,7},{5,6},{6,5},{7,4},{8,11},{9,10},{10,... | collective-permute-start | bytes 49160 | tf_op jit(solution)/shard_map/ppermute | solution.py:23
  13.9 3.8 %collective-permute-start.4 = (f32[16,256]{1,0:T(8,128)S(1)}, f32[16,256]{1,0:T(8,128)S(1)}, u32[]{:S(2)}, u32[]{:S(2)}) collective-permute-start(f32[16,256]{1,0:T(8,128)S(1)} %get-tuple-element.31.part.refs_8_), channel_id=1, source_target_pairs={{0,2},{1,3},{2,0},{3,1},{4,6},{5,7},{6,4},{7,5},{8,10},{9,11},{10,... | collective-permute-start | bytes 49160 | tf_op jit(solution)/shard_map/ppermute | solution.py:23
  15.4 2.3 %collective-permute-start.3 = (f32[16,256]{1,0:T(8,128)S(1)}, f32[16,256]{1,0:T(8,128)S(1)}, u32[]{:S(2)}, u32[]{:S(2)}) collective-permute-start(f32[16,256]{1,0:T(8,128)S(1)} %get-tuple-element.31.part.refs_8_), channel_id=1, source_target_pairs={{0,1},{1,0},{2,3},{3,2},{4,5},{5,4},{6,7},{7,6},{8,9},{9,8},{10,11... | collective-permute-start | bytes 49160 | tf_op jit(solution)/shard_map/ppermute | solution.py:23
  15.7 2.0 %copy-start = (f32[16,256]{1,0:T(8,128)S(1)}, f32[16,256]{1,0:T(8,128)}, u32[]{:S(2)}) copy-start(f32[16,256]{1,0:T(8,128)} %refs_5_.5) | copy-start | bytes 49156
  15.7 2.0 %copy-start.1 = (f32[16,256]{1,0:T(8,128)S(1)}, f32[16,256]{1,0:T(8,128)}, u32[]{:S(2)}) copy-start(f32[16,256]{1,0:T(8,128)} %refs_5_.3) | copy-start | bytes 49156
  19.1 4.7 %collective-permute-start.8 = (f32[16,256]{1,0:T(8,128)S(1)}, f32[16,256]{1,0:T(8,128)S(1)}, u32[]{:S(2)}, u32[]{:S(2)}) collective-permute-start(f32[16,256]{1,0:T(8,128)S(1)} %shard_map.108.part.refs_7_), channel_id=1, source_target_pairs={{0,8},{4,12},{8,0},{12,4},{1,9},{5,13},{9,1},{13,5},{2,10},{6,14},... | collective-permute-start | bytes 49160 | tf_op jit(solution)/shard_map/ppermute | solution.py:23
  21.0 5.5 %collective-permute-start.7 = (f32[16,256]{1,0:T(8,128)S(1)}, f32[16,256]{1,0:T(8,128)S(1)}, u32[]{:S(2)}, u32[]{:S(2)}) collective-permute-start(f32[16,256]{1,0:T(8,128)S(1)} %shard_map.108.part.refs_7_), channel_id=1, source_target_pairs={{0,12},{4,8},{8,4},{12,0},{1,13},{5,9},{9,5},{13,1},{2,14},{6,10},... | collective-permute-start | bytes 49160 | tf_op jit(solution)/shard_map/ppermute | solution.py:23
  22.4 4.2 %collective-permute-start.6 = (f32[16,256]{1,0:T(8,128)S(1)}, f32[16,256]{1,0:T(8,128)S(1)}, u32[]{:S(2)}, u32[]{:S(2)}) collective-permute-start(f32[16,256]{1,0:T(8,128)S(1)} %shard_map.108.part.refs_7_), channel_id=1, source_target_pairs={{0,4},{4,0},{8,12},{12,8},{1,5},{5,1},{9,13},{13,9},{2,6},{6,2},{1... | collective-permute-start | bytes 49160 | tf_op jit(solution)/shard_map/ppermute | solution.py:23
  28.0 3.5 %collective-permute-start.11 = (f32[24,256]{1,0:T(8,128)S(1)}, f32[24,256]{1,0:T(8,128)S(1)}, u32[]{:S(2)}, u32[]{:S(2)}) collective-permute-start(f32[24,256]{1,0:T(8,128)S(1)} %get-tuple-element.36.refs_6_), channel_id=1, source_target_pairs={{0,3},{1,2},{2,1},{3,0},{4,7},{5,6},{6,5},{7,4},{8,11},{9,10},{10,... | collective-permute-start | bytes 73736 | tf_op jit(solution)/shard_map/ppermute | solution.py:23
  28.0 3.9 %collective-permute-start.10 = (f32[24,256]{1,0:T(8,128)S(1)}, f32[24,256]{1,0:T(8,128)S(1)}, u32[]{:S(2)}, u32[]{:S(2)}) collective-permute-start(f32[24,256]{1,0:T(8,128)S(1)} %get-tuple-element.36.refs_6_), channel_id=1, source_target_pairs={{0,2},{1,3},{2,0},{3,1},{4,6},{5,7},{6,4},{7,5},{8,10},{9,11},{10,... | collective-permute-start | bytes 73736 | tf_op jit(solution)/shard_map/ppermute | solution.py:23
  29.5 2.4 %collective-permute-start.9 = (f32[24,256]{1,0:T(8,128)S(1)}, f32[24,256]{1,0:T(8,128)S(1)}, u32[]{:S(2)}, u32[]{:S(2)}) collective-permute-start(f32[24,256]{1,0:T(8,128)S(1)} %get-tuple-element.36.refs_6_), channel_id=1, source_target_pairs={{0,1},{1,0},{2,3},{3,2},{4,5},{5,4},{6,7},{7,6},{8,9},{9,8},{10,11... | collective-permute-start | bytes 73736 | tf_op jit(solution)/shard_map/ppermute | solution.py:23
  33.3 4.8 %collective-permute-start.14 = (f32[24,256]{1,0:T(8,128)S(1)}, f32[24,256]{1,0:T(8,128)S(1)}, u32[]{:S(2)}, u32[]{:S(2)}) collective-permute-start(f32[24,256]{1,0:T(8,128)S(1)} %get-tuple-element.38.refs_8_), channel_id=1, source_target_pairs={{0,8},{4,12},{8,0},{12,4},{1,9},{5,13},{9,1},{13,5},{2,10},{6,14},... | collective-permute-start | bytes 73736 | tf_op jit(solution)/shard_map/ppermute | solution.py:23
  34.0 5.7 %collective-permute-start.13 = (f32[24,256]{1,0:T(8,128)S(1)}, f32[24,256]{1,0:T(8,128)S(1)}, u32[]{:S(2)}, u32[]{:S(2)}) collective-permute-start(f32[24,256]{1,0:T(8,128)S(1)} %get-tuple-element.38.refs_8_), channel_id=1, source_target_pairs={{0,12},{4,8},{8,4},{12,0},{1,13},{5,9},{9,5},{13,1},{2,14},{6,10},... | collective-permute-start | bytes 73736 | tf_op jit(solution)/shard_map/ppermute | solution.py:23
  35.5 4.2 %collective-permute-start.12 = (f32[24,256]{1,0:T(8,128)S(1)}, f32[24,256]{1,0:T(8,128)S(1)}, u32[]{:S(2)}, u32[]{:S(2)}) collective-permute-start(f32[24,256]{1,0:T(8,128)S(1)} %get-tuple-element.38.refs_8_), channel_id=1, source_target_pairs={{0,4},{4,0},{8,12},{12,8},{1,5},{5,1},{9,13},{13,9},{2,6},{6,2},{1... | collective-permute-start | bytes 73736 | tf_op jit(solution)/shard_map/ppermute | solution.py:23
  41.3 3.5 %collective-permute-start.17 = (f32[24,256]{1,0:T(8,128)S(1)}, f32[24,256]{1,0:T(8,128)S(1)}, u32[]{:S(2)}, u32[]{:S(2)}) collective-permute-start(f32[24,256]{1,0:T(8,128)S(1)} %get-tuple-element.42.refs_8_), channel_id=1, source_target_pairs={{0,3},{1,2},{2,1},{3,0},{4,7},{5,6},{6,5},{7,4},{8,11},{9,10},{10,... | collective-permute-start | bytes 73736 | tf_op jit(solution)/shard_map/ppermute | solution.py:23
  41.3 3.9 %collective-permute-start.16 = (f32[24,256]{1,0:T(8,128)S(1)}, f32[24,256]{1,0:T(8,128)S(1)}, u32[]{:S(2)}, u32[]{:S(2)}) collective-permute-start(f32[24,256]{1,0:T(8,128)S(1)} %get-tuple-element.42.refs_8_), channel_id=1, source_target_pairs={{0,2},{1,3},{2,0},{3,1},{4,6},{5,7},{6,4},{7,5},{8,10},{9,11},{10,... | collective-permute-start | bytes 73736 | tf_op jit(solution)/shard_map/ppermute | solution.py:23
  42.7 2.4 %collective-permute-start.15 = (f32[24,256]{1,0:T(8,128)S(1)}, f32[24,256]{1,0:T(8,128)S(1)}, u32[]{:S(2)}, u32[]{:S(2)}) collective-permute-start(f32[24,256]{1,0:T(8,128)S(1)} %get-tuple-element.42.refs_8_), channel_id=1, source_target_pairs={{0,1},{1,0},{2,3},{3,2},{4,5},{5,4},{6,7},{7,6},{8,9},{9,8},{10,11... | collective-permute-start | bytes 73736 | tf_op jit(solution)/shard_map/ppermute | solution.py:23
  46.7 4.6 %collective-permute-start.18 = (f32[8,256]{1,0:T(8,128)S(1)}, f32[8,256]{1,0:T(8,128)S(1)}, u32[]{:S(2)}, u32[]{:S(2)}) collective-permute-start(f32[8,256]{1,0:T(8,128)S(1)} %get-tuple-element.45), channel_id=1, source_target_pairs={{0,8},{4,12},{8,0},{12,4},{1,9},{5,13},{9,1},{13,5},{2,10},{6,14},... | collective-permute-start | bytes 24584 | tf_op jit(solution)/shard_map/ppermute | solution.py:23
  48.2 5.5 %collective-permute-start.19 = (f32[8,256]{1,0:T(8,128)S(1)}, f32[8,256]{1,0:T(8,128)S(1)}, u32[]{:S(2)}, u32[]{:S(2)}) collective-permute-start(f32[8,256]{1,0:T(8,128)S(1)} %get-tuple-element.46), channel_id=1, source_target_pairs={{0,12},{4,8},{8,4},{12,0},{1,13},{5,9},{9,5},{13,1},{2,14},{6,10},... | collective-permute-start | bytes 24584 | tf_op jit(solution)/shard_map/ppermute | solution.py:23
  50.0 3.7 %collective-permute-start.20 = (f32[8,256]{1,0:T(8,128)S(1)}, f32[8,256]{1,0:T(8,128)S(1)}, u32[]{:S(2)}, u32[]{:S(2)}) collective-permute-start(f32[8,256]{1,0:T(8,128)S(1)} %get-tuple-element.47), channel_id=1, source_target_pairs={{0,4},{4,0},{8,12},{12,8},{1,5},{5,1},{9,13},{13,9},{2,6},{6,2},{1... | collective-permute-start | bytes 24584 | tf_op jit(solution)/shard_map/ppermute | solution.py:23

commit v7 on v5

--- a/solution.py
+++ b/solution.py
@@ -363,7 +363,9 @@
 
     order = [0] + sorted(range(1, count), key=lambda shift: (shift != 1, -abs(2 * shift - count)))
 
-    def across(values):
+    far = list(range(count))
+
+    def across(values, order):
         parts = exchange(values, "tiles", count)
         return [parts[shift] for shift in order]
 
@@ -384,7 +386,7 @@
             pltpu.SemaphoreType.DMA((3,)),
         ],
     )
-    begin = across([opening] * count)
+    begin = across([opening] * count, order)
     low, rows_pick, rows_pair, scale = call(
         loading_kernel,
         [
@@ -449,10 +451,10 @@
         early,
         *parts,
     )
-    parts = across([part] * count)
+    parts = across([part] * count, far)
     late = turned_half(half, part)
     part, first = call(
-        functools.partial(start_residual_kernel, blocks, order),
+        functools.partial(start_residual_kernel, blocks, far),
         [((data_rows + EXTRA, width), F32), ((cells, width), F32)],
         early,
         late,
@@ -475,7 +477,7 @@
         *within(part),
     )
     part, second, step = call(
-        functools.partial(residual_kernel, blocks, order),
+        functools.partial(residual_kernel, blocks, far),
         [((data_rows + EXTRA, width), F32), ((cells, width), F32), ((8, 128), F32)],
         early,
         late,
@@ -485,7 +487,7 @@
         weight,
         first,
         sums,
-        *across([part] * count),
+        *across([part] * count, far),
     )
     *part, scalars = call(
         functools.partial(second_data_kernel, blocks, sharing),
@@ -509,7 +511,7 @@
         second,
         step,
         scalars,
-        *[part[0]] + across(part)[:0:-1],
+        *[part[0]] + across(part, order)[:0:-1],
     )
     return (model, residual)
 

time: 54.8 us -> 55 us (level)
  starting transfers between devices: 21.9 us -> 23.8 us
  waiting for transfers between devices: 15.1 us -> 13.3 us
    ppermute x21, starting transfers between devices: 21.9 us -> 23.8 us  [exchange(): parts[shift] = lax.ppermute(values[shift], axes, perm)]
    ppermute x21, waiting for transfers between devices: 15.1 us -> 13.3 us  [exchange(): parts[shift] = lax.ppermute(values[shift], axes, perm)]
  transfers between devices with their start and end apart: 21 -> 21, of which waited for: 13 -> 14; matrix products, arithmetic and copies ran while one was open for 0% -> 0% of each run, Pallas kernels for 9% -> 9%
where the time goes in v7:
time: 55 us; the launch traced here: 54.8 us
  starting transfers between devices  23.8 us (43%)
  Pallas kernels  17 us (31%)
  waiting for transfers between devices  13.3 us (24%)
  between operations  0.72 us (1%)
    ppermute x21, starting transfers between devices, exchange(): parts[shift] = lax.ppermute(values[shift], axes, perm)  23.8 us
    pallas_call x11, Pallas kernels, call(): pl.pallas_call(body, out_shape=[jax.ShapeDtypeStruct(shape, dtype) for sh...  17 us
    ppermute x21, waiting for transfers between devices, exchange(): parts[shift] = lax.ppermute(values[shift], axes, perm)  13.3 us
  transfers between devices with their start and end apart: 21, of which 14 were waited for; matrix products, arithmetic and copies ran while one was open for 0% of the time, Pallas kernels for 9%

profile of v7, /device:TPU:0, one launch (start us, length us, event | category | flops | bytes accessed | tf_op | source)
XLA Modules:
  0.0 54.8 jit_solution(7721315698906310785)
XLA Ops:
  0.6 0.7 %shard_map.104.opening.refs_6_ = f32[16,256]{1,0:T(8,128)S(1)} custom-call(f32[4,256]{1,0:T(4,128)} %start.1, f32[4,256]{1,0:T(4,128)} %weight.1, s32[2,4]{1,0:T(2,128)} %bitcast.8), custom_call_target="tpu_custom_call" | custom-call | tf_op jit(solution)/shard_map/pallas_call | solution.py:331
  1.4 4.1 %collective-permute-start.2 = (f32[16,256]{1,0:T(8,128)S(1)}, f32[16,256]{1,0:T(8,128)S(1)}, u32[]{:S(2)}, u32[]{:S(2)}) collective-permute-start(f32[16,256]{1,0:T(8,128)S(1)} %shard_map.104.opening.refs_6_), channel_id=1, source_target_pairs={{0,8},{4,12},{8,0},{12,4},{1,9},{5,13},{9,1},{13,5},{2,10},{6,14},... | collective-permute-start | bytes 49160 | tf_op jit(solution)/shard_map/ppermute | solution.py:23
  5.5 1.3 %collective-permute-start.1 = (f32[16,256]{1,0:T(8,128)S(1)}, f32[16,256]{1,0:T(8,128)S(1)}, u32[]{:S(2)}, u32[]{:S(2)}) collective-permute-start(f32[16,256]{1,0:T(8,128)S(1)} %shard_map.104.opening.refs_6_), channel_id=1, source_target_pairs={{0,12},{4,8},{8,4},{12,0},{1,13},{5,9},{9,5},{13,1},{2,14},{6,10},... | collective-permute-start | bytes 49160 | tf_op jit(solution)/shard_map/ppermute | solution.py:23
  6.8 0.2 collective-permute-start
  7.1 0.0 copy-start.2
  7.1 2.9 %shard_map.105 = (bf16[48,256,256]{2,1,0:T(8,128)(2,1)S(1)}, bf16[64,16]{1,0:T(8,128)(2,1)S(1)}, bf16[16,128]{1,0:T(8,128)(2,1)S(1)}, f32[64,256]{1,0:T(8,128)S(1)}) custom-call(bf16[64,256,256]{2,1,0:T(8,128)(2,1)} %refs_0_.1, f32[16,256]{1,0:T(8,128)S(1)} %shard_map.104.opening.refs_6_, f32[1,64]{1,0:T(1,128)} %bitcast.9, s32[1,64]{1,0:T(1,128)} %bitcast.10), custom_call_target="tpu_custom_call" | custom-call | tf_op jit(solution)/shard_map/pallas_call | solution.py:331
  10.0 0.0 collective-permute-done.2.refs_9_
  10.0 1.0 %collective-permute-done.1.refs_8_ = f32[16,256]{1,0:T(8,128)S(1)} collective-permute-done((f32[16,256]{1,0:T(8,128)S(1)}, f32[16,256]{1,0:T(8,128)S(1)}, u32[]{:S(2)}, u32[]{:S(2)}) %collective-permute-start.1) | collective-permute-done | bytes 16416 | tf_op jit(solution)/shard_map/ppermute | solution.py:23
  11.0 0.0 collective-permute-done.refs_7_
  11.0 0.0 copy-done.2
  11.0 2.9 %shard_map.106 = (f32[16,256]{1,0:T(8,128)S(1)}, bf16[16,256,256]{2,1,0:T(8,128)(2,1)S(1)}, bf16[64,16]{1,0:T(8,128)(2,1)S(1)}, bf16[16,128]{1,0:T(8,128)(2,1)S(...) custom-call(bf16[64,256,256]{2,1,0:T(8,128)(2,1)} %refs_0_.1, ...), custom_call_target="tpu_custom_call" | custom-call | tf_op jit(solution)/shard_map/pallas_call | solution.py:331
  13.9 0.1 collective-permute-start.5
  14.0 1.6 %collective-permute-start.4 = (f32[16,256]{1,0:T(8,128)S(1)}, f32[16,256]{1,0:T(8,128)S(1)}, u32[]{:S(2)}, u32[]{:S(2)}) collective-permute-start(f32[16,256]{1,0:T(8,128)S(1)} %get-tuple-element.31.part.refs_8_), channel_id=1, source_target_pairs={{0,2},{1,3},{2,0},{3,1},{4,6},{5,7},{6,4},{7,5},{8,10},{9,11},{10,... | collective-permute-start | bytes 49160 | tf_op jit(solution)/shard_map/ppermute | solution.py:23
  15.6 0.3 collective-permute-start.3
  15.9 0.0 copy-start
  15.9 0.0 copy-start.1
  15.9 1.1 %shard_map.107.refs_7_.refs_0_ = bf16[32,256,256]{2,1,0:T(8,128)(2,1)S(1)} custom-call(bf16[48,256,256]{2,1,0:T(8,128)(2,1)S(1)} %get-tuple-element.25.refs_1_.low.refs_0_, bf16[16,256,256]{2,1,0:T(8,128)(2,1)S(1)} %get-tuple-element.30.high.refs_1_, f32[16,256]{1,0:T(8,128)S(1)} %get-tuple-element.31.part.refs_8_), custom_call_target="tpu_custom_call" | custom-call | tf_op jit(solution)/shard_map/pallas_call | solution.py:331
  17.0 0.3 collective-permute-done.5.refs_11_
  17.3 0.5 collective-permute-done.4.refs_10_
  17.8 0.0 collective-permute-done.3.refs_9_
  17.8 0.0 copy-done
  17.8 0.0 copy-done.1
  17.8 1.4 %shard_map.108.part.refs_7_ = f32[16,256]{1,0:T(8,128)S(1)} custom-call(bf16[48,256,256]{2,1,0:T(8,128)(2,1)S(1)} %get-tuple-element.25.refs_1_.low.refs_0_, bf16[16,256,256]{2,1,0:T(8,128)(2,1)S(1)} %get-tuple-element.30.high.refs_1_, bf16[64,16]{1,0:T(8,128)(2,1)S(1)} %get-tuple-element.32.refs_2_, bf16[16,128]{1,0:T(8,128)(2,1)S(1)} %get-tuple-element.33.refs_3_, ...), custom_call_target="tpu_custom_call" | custom-call | tf_op jit(solution)/shard_map/pallas_call | solution.py:331
  19.2 2.0 %collective-permute-start.8 = (f32[16,256]{1,0:T(8,128)S(1)}, f32[16,256]{1,0:T(8,128)S(1)}, u32[]{:S(2)}, u32[]{:S(2)}) collective-permute-start(f32[16,256]{1,0:T(8,128)S(1)} %shard_map.108.part.refs_7_), channel_id=1, source_target_pairs={{0,12},{4,8},{8,4},{12,0},{1,13},{5,9},{9,5},{13,1},{2,14},{6,10},... | collective-permute-start | bytes 49160 | tf_op jit(solution)/shard_map/ppermute | solution.py:23
  21.3 0.3 collective-permute-start.7
  21.6 2.1 %collective-permute-start.6 = (f32[16,256]{1,0:T(8,128)S(1)}, f32[16,256]{1,0:T(8,128)S(1)}, u32[]{:S(2)}, u32[]{:S(2)}) collective-permute-start(f32[16,256]{1,0:T(8,128)S(1)} %shard_map.108.part.refs_7_), channel_id=1, source_target_pairs={{0,4},{4,0},{8,12},{12,8},{1,5},{5,1},{9,13},{13,9},{2,6},{6,2},{1... | collective-permute-start | bytes 49160 | tf_op jit(solution)/shard_map/ppermute | solution.py:23
  23.7 1.1 %shard_map.109.refs_1_ = bf16[32,256,256]{2,1,0:T(8,128)(2,1)S(1)} custom-call(bf16[48,256,256]{2,1,0:T(8,128)(2,1)S(1)} %get-tuple-element.25.refs_1_.low.refs_0_, bf16[16,256,256]{2,1,0:T(8,128)(2,1)S(1)} %get-tuple-element.30.high.refs_1_, f32[16,256]{1,0:T(8,128)S(1)} %shard_map.108.part.refs_7_), custom_call_target="tpu_custom_call" | custom-call | tf_op jit(solution)/shard_map/pallas_call | solution.py:331
  24.8 0.2 collective-permute-done.8.refs_10_
  25.0 1.0 %collective-permute-done.7.refs_9_ = f32[16,256]{1,0:T(8,128)S(1)} collective-permute-done((f32[16,256]{1,0:T(8,128)S(1)}, f32[16,256]{1,0:T(8,128)S(1)}, u32[]{:S(2)}, u32[]{:S(2)}) %collective-permute-start.7) | collective-permute-done | bytes 16416 | tf_op jit(solution)/shard_map/ppermute | solution.py:23
  25.9 0.0 collective-permute-done.6.refs_8_
  25.9 1.4 %shard_map.110 = (f32[24,256]{1,0:T(8,128)S(1)}, f32[16,256]{1,0:T(8,128)S(1)}) custom-call(bf16[32,256,256]{2,1,0:T(8,128)(2,1)S(1)} %shard_map.107.refs_7_.refs_0_, bf16[32,256,256]{2,1,0:T(8,128)(2,1)S(1)} %shard_map.109.refs_1_, bf16[64,16]{1,0:T(8,128)(2,1)S(1)} %get-tuple-element.34.refs_2_, bf16[16,128]{1,0:T(8,128)(2,1)S(1)} %get-tuple-element.27.refs_3_, ...), custom_call_target="tpu_custom_call" | custom-call | tf_op jit(solution)/shard_map/pallas_call | solution.py:331
  27.4 0.0 collective-permute-start.11
  27.4 1.5 %collective-permute-start.10 = (f32[24,256]{1,0:T(8,128)S(1)}, f32[24,256]{1,0:T(8,128)S(1)}, u32[]{:S(2)}, u32[]{:S(2)}) collective-permute-start(f32[24,256]{1,0:T(8,128)S(1)} %get-tuple-element.36.refs_6_), channel_id=1, source_target_pairs={{0,2},{1,3},{2,0},{3,1},{4,6},{5,7},{6,4},{7,5},{8,10},{9,11},{10,... | collective-permute-start | bytes 73736 | tf_op jit(solution)/shard_map/ppermute | solution.py:23
  28.9 0.3 collective-permute-start.9
  29.2 1.6 %collective-permute-done.11.refs_9_ = f32[24,256]{1,0:T(8,128)S(1)} collective-permute-done((f32[24,256]{1,0:T(8,128)S(1)}, f32[24,256]{1,0:T(8,128)S(1)}, u32[]{:S(2)}, u32[]{:S(2)}) %collective-permute-start.11) | collective-permute-done | bytes 24608 | tf_op jit(solution)/shard_map/ppermute | solution.py:23
  30.9 0.4 collective-permute-done.10.refs_8_
  31.2 0.0 collective-permute-done.9.refs_7_
  31.3 1.4 %shard_map.111 = (f32[24,256]{1,0:T(8,128)S(1)}, f32[16,256]{1,0:T(8,128)S(1)}, f32[8,256]{1,0:T(8,128)S(1)}) custom-call(bf16[48,256,256]{2,1,0:T(8,128)(2,1)S(1)} %get-tuple-element.25.refs_1_.low.refs_0_, bf16[16,256,256]{2,1,0:T(8,128)(2,1)S(1)} %get-tuple-element.30.high.refs_1_, bf16[64,16]{1,0:T(8,128)(2,1)S(1)} %get-tuple-element.32.refs_2_, ...), custom_call_target="tpu_custom_call" | custom-call | tf_op jit(solution)/shard_map/pallas_call | solution.py:331
  32.7 2.0 %collective-permute-start.14 = (f32[24,256]{1,0:T(8,128)S(1)}, f32[24,256]{1,0:T(8,128)S(1)}, u32[]{:S(2)}, u32[]{:S(2)}) collective-permute-start(f32[24,256]{1,0:T(8,128)S(1)} %get-tuple-element.38.refs_8_), channel_id=1, source_target_pairs={{0,12},{4,8},{8,4},{12,0},{1,13},{5,9},{9,5},{13,1},{2,14},{6,10},... | collective-permute-start | bytes 73736 | tf_op jit(solution)/shard_map/ppermute | solution.py:23
  34.7 1.0 %collective-permute-start.13 = (f32[24,256]{1,0:T(8,128)S(1)}, f32[24,256]{1,0:T(8,128)S(1)}, u32[]{:S(2)}, u32[]{:S(2)}) collective-permute-start(f32[24,256]{1,0:T(8,128)S(1)} %get-tuple-element.38.refs_8_), channel_id=1, source_target_pairs={{0,8},{4,12},{8,0},{12,4},{1,9},{5,13},{9,1},{13,5},{2,10},{6,14},... | collective-permute-start | bytes 73736 | tf_op jit(solution)/shard_map/ppermute | solution.py:23
  35.6 1.5 %collective-permute-start.12 = (f32[24,256]{1,0:T(8,128)S(1)}, f32[24,256]{1,0:T(8,128)S(1)}, u32[]{:S(2)}, u32[]{:S(2)}) collective-permute-start(f32[24,256]{1,0:T(8,128)S(1)} %get-tuple-element.38.refs_8_), channel_id=1, source_target_pairs={{0,4},{4,0},{8,12},{12,8},{1,5},{5,1},{9,13},{13,9},{2,6},{6,2},{1... | collective-permute-start | bytes 73736 | tf_op jit(solution)/shard_map/ppermute | solution.py:23
  37.1 1.3 %collective-permute-done.14.refs_11_ = f32[24,256]{1,0:T(8,128)S(1)} collective-permute-done((f32[24,256]{1,0:T(8,128)S(1)}, f32[24,256]{1,0:T(8,128)S(1)}, u32[]{:S(2)}, u32[]{:S(2)}) %collective-permute-start.14) | collective-permute-done | bytes 24608 | tf_op jit(solution)/shard_map/ppermute | solution.py:23
  38.4 1.2 %collective-permute-done.13.refs_10_ = f32[24,256]{1,0:T(8,128)S(1)} collective-permute-done((f32[24,256]{1,0:T(8,128)S(1)}, f32[24,256]{1,0:T(8,128)S(1)}, u32[]{:S(2)}, u32[]{:S(2)}) %collective-permute-start.13) | collective-permute-done | bytes 24608 | tf_op jit(solution)/shard_map/ppermute | solution.py:23
  39.7 0.0 collective-permute-done.12.refs_9_
  39.7 1.5 %shard_map.112 = (f32[24,256]{1,0:T(8,128)S(1)}, f32[16,256]{1,0:T(8,128)S(1)}, f32[8,128]{1,0:T(8,128)S(1)}) custom-call(bf16[32,256,256]{2,1,0:T(8,128)(2,1)S(1)} %shard_map.107.refs_7_.refs_0_, bf16[32,256,256]{2,1,0:T(8,128)(2,1)S(1)} %shard_map.109.refs_1_, bf16[64,16]{1,0:T(8,128)(2,1)S(1)} %get-tuple-element.34.refs_2_, ...), custom_call_target="tpu_custom_call" | custom-call | tf_op jit(solution)/shard_map/pallas_call | solution.py:331
  41.2 0.0 collective-permute-start.17
  41.2 1.5 %collective-permute-start.16 = (f32[24,256]{1,0:T(8,128)S(1)}, f32[24,256]{1,0:T(8,128)S(1)}, u32[]{:S(2)}, u32[]{:S(2)}) collective-permute-start(f32[24,256]{1,0:T(8,128)S(1)} %get-tuple-element.42.refs_8_), channel_id=1, source_target_pairs={{0,2},{1,3},{2,0},{3,1},{4,6},{5,7},{6,4},{7,5},{8,10},{9,11},{10,... | collective-permute-start | bytes 73736 | tf_op jit(solution)/shard_map/ppermute | solution.py:23
  42.7 0.4 collective-permute-start.15
  43.1 1.7 %collective-permute-done.17.refs_11_ = f32[24,256]{1,0:T(8,128)S(1)} collective-permute-done((f32[24,256]{1,0:T(8,128)S(1)}, f32[24,256]{1,0:T(8,128)S(1)}, u32[]{:S(2)}, u32[]{:S(2)}) %collective-permute-start.17) | collective-permute-done | bytes 24608 | tf_op jit(solution)/shard_map/ppermute | solution.py:23
  44.8 0.4 collective-permute-done.16.refs_10_
  45.1 0.0 collective-permute-done.15.refs_9_
  45.1 1.6 %shard_map.113 = (f32[8,256]{1,0:T(8,128)S(1)}, f32[8,256]{1,0:T(8,128)S(1)}, f32[8,256]{1,0:T(8,128)S(1)}, f32[8,256]{1,0:T(8,128)S(1)}, f32[8,256]{1,0:T(8,128)S(1)}) custom-call(bf16[48,256,256]{2,1,0:T(8,128)(2,1)S(1)} %get-tuple-element.25.refs_1_.low.refs_0_, bf16[16,256,256]{2,1,0:T(8,128)(2,1)S(1)} %get-tuple-element.30.high.refs_1_, ...), custom_call_target="tpu_custom_call" | custom-call | tf_op jit(solution)/shard_map/pallas_call | solution.py:331
  46.7 1.8 %collective-permute-start.18 = (f32[8,256]{1,0:T(8,128)S(1)}, f32[8,256]{1,0:T(8,128)S(1)}, u32[]{:S(2)}, u32[]{:S(2)}) collective-permute-start(f32[8,256]{1,0:T(8,128)S(1)} %get-tuple-element.45), channel_id=1, source_target_pairs={{0,8},{4,12},{8,0},{12,4},{1,9},{5,13},{9,1},{13,5},{2,10},{6,14},... | collective-permute-start | bytes 24584 | tf_op jit(solution)/shard_map/ppermute | solution.py:23
  48.4 1.9 %collective-permute-start.19 = (f32[8,256]{1,0:T(8,128)S(1)}, f32[8,256]{1,0:T(8,128)S(1)}, u32[]{:S(2)}, u32[]{:S(2)}) collective-permute-start(f32[8,256]{1,0:T(8,128)S(1)} %get-tuple-element.46), channel_id=1, source_target_pairs={{0,12},{4,8},{8,4},{12,0},{1,13},{5,9},{9,5},{13,1},{2,14},{6,10},... | collective-permute-start | bytes 24584 | tf_op jit(solution)/shard_map/ppermute | solution.py:23
  50.3 0.0 collective-permute-start.20
  50.3 1.0 %collective-permute-done.18.refs_7_ = f32[8,256]{1,0:T(8,128)S(1)} collective-permute-done((f32[8,256]{1,0:T(8,128)S(1)}, f32[8,256]{1,0:T(8,128)S(1)}, u32[]{:S(2)}, u32[]{:S(2)}) %collective-permute-start.18) | collective-permute-done | bytes 8224 | tf_op jit(solution)/shard_map/ppermute | solution.py:23
  51.3 2.6 %collective-permute-done.19.refs_8_ = f32[8,256]{1,0:T(8,128)S(1)} collective-permute-done((f32[8,256]{1,0:T(8,128)S(1)}, f32[8,256]{1,0:T(8,128)S(1)}, u32[]{:S(2)}, u32[]{:S(2)}) %collective-permute-start.19) | collective-permute-done | bytes 8224 | tf_op jit(solution)/shard_map/ppermute | solution.py:23
  53.9 0.1 collective-permute-done.20.refs_9_
  54.0 0.8 %shard_map.114 = (f32[4,256]{1,0:T(4,128)}, f32[4,256]{1,0:T(4,128)}) custom-call(f32[16,256]{1,0:T(8,128)S(1)} %get-tuple-element.28.refs_6_.refs_5_.refs_0_, f32[16,256]{1,0:T(8,128)S(1)} %get-tuple-element.29.refs_5_.refs_1_, f32[16,256]{1,0:T(8,128)S(1)} %get-tuple-element.35.refs_6_.refs_2_, f32[16,256]{1,0:T(8,128)S(1)} %get-tuple-element.39.refs_3_, ...), custom_call_target="tpu_custom_call" | custom-call | tf_op jit(solution)/shard_map/pallas_call | solution.py:331
Async XLA Ops:
  1.4 8.6 %collective-permute-start.2 = (f32[16,256]{1,0:T(8,128)S(1)}, f32[16,256]{1,0:T(8,128)S(1)}, u32[]{:S(2)}, u32[]{:S(2)}) collective-permute-start(f32[16,256]{1,0:T(8,128)S(1)} %shard_map.104.opening.refs_6_), channel_id=1, source_target_pairs={{0,8},{4,12},{8,0},{12,4},{1,9},{5,13},{9,1},{13,5},{2,10},{6,14},... | collective-permute-start | bytes 49160 | tf_op jit(solution)/shard_map/ppermute | solution.py:23
  5.5 5.5 %collective-permute-start.1 = (f32[16,256]{1,0:T(8,128)S(1)}, f32[16,256]{1,0:T(8,128)S(1)}, u32[]{:S(2)}, u32[]{:S(2)}) collective-permute-start(f32[16,256]{1,0:T(8,128)S(1)} %shard_map.104.opening.refs_6_), channel_id=1, source_target_pairs={{0,12},{4,8},{8,4},{12,0},{1,13},{5,9},{9,5},{13,1},{2,14},{6,10},... | collective-permute-start | bytes 49160 | tf_op jit(solution)/shard_map/ppermute | solution.py:23
  6.8 4.2 %collective-permute-start = (f32[16,256]{1,0:T(8,128)S(1)}, f32[16,256]{1,0:T(8,128)S(1)}, u32[]{:S(2)}, u32[]{:S(2)}) collective-permute-start(f32[16,256]{1,0:T(8,128)S(1)} %shard_map.104.opening.refs_6_), channel_id=1, source_target_pairs={{0,4},{4,0},{8,12},{12,8},{1,5},{5,1},{9,13},{13,9},{2,6},{6,2},{1... | collective-permute-start | bytes 49160 | tf_op jit(solution)/shard_map/ppermute | solution.py:23
  7.1 4.0 %copy-start.2 = (s32[64]{0:T(128)S(1)}, s32[64]{0:T(128)}, u32[]{:S(2)}) copy-start(s32[64]{0:T(128)} %param.12) | copy-start | bytes 772
  13.9 3.4 %collective-permute-start.5 = (f32[16,256]{1,0:T(8,128)S(1)}, f32[16,256]{1,0:T(8,128)S(1)}, u32[]{:S(2)}, u32[]{:S(2)}) collective-permute-start(f32[16,256]{1,0:T(8,128)S(1)} %get-tuple-element.31.part.refs_8_), channel_id=1, source_target_pairs={{0,3},{1,2},{2,1},{3,0},{4,7},{5,6},{6,5},{7,4},{8,11},{9,10},{10,... | collective-permute-start | bytes 49160 | tf_op jit(solution)/shard_map/ppermute | solution.py:23
  14.0 3.8 %collective-permute-start.4 = (f32[16,256]{1,0:T(8,128)S(1)}, f32[16,256]{1,0:T(8,128)S(1)}, u32[]{:S(2)}, u32[]{:S(2)}) collective-permute-start(f32[16,256]{1,0:T(8,128)S(1)} %get-tuple-element.31.part.refs_8_), channel_id=1, source_target_pairs={{0,2},{1,3},{2,0},{3,1},{4,6},{5,7},{6,4},{7,5},{8,10},{9,11},{10,... | collective-permute-start | bytes 49160 | tf_op jit(solution)/shard_map/ppermute | solution.py:23
  15.6 2.3 %collective-permute-start.3 = (f32[16,256]{1,0:T(8,128)S(1)}, f32[16,256]{1,0:T(8,128)S(1)}, u32[]{:S(2)}, u32[]{:S(2)}) collective-permute-start(f32[16,256]{1,0:T(8,128)S(1)} %get-tuple-element.31.part.refs_8_), channel_id=1, source_target_pairs={{0,1},{1,0},{2,3},{3,2},{4,5},{5,4},{6,7},{7,6},{8,9},{9,8},{10,11... | collective-permute-start | bytes 49160 | tf_op jit(solution)/shard_map/ppermute | solution.py:23
  15.9 2.0 %copy-start = (f32[16,256]{1,0:T(8,128)S(1)}, f32[16,256]{1,0:T(8,128)}, u32[]{:S(2)}) copy-start(f32[16,256]{1,0:T(8,128)} %refs_5_.5) | copy-start | bytes 49156
  15.9 2.0 %copy-start.1 = (f32[16,256]{1,0:T(8,128)S(1)}, f32[16,256]{1,0:T(8,128)}, u32[]{:S(2)}) copy-start(f32[16,256]{1,0:T(8,128)} %refs_5_.3) | copy-start | bytes 49156
  19.2 5.7 %collective-permute-start.8 = (f32[16,256]{1,0:T(8,128)S(1)}, f32[16,256]{1,0:T(8,128)S(1)}, u32[]{:S(2)}, u32[]{:S(2)}) collective-permute-start(f32[16,256]{1,0:T(8,128)S(1)} %shard_map.108.part.refs_7_), channel_id=1, source_target_pairs={{0,12},{4,8},{8,4},{12,0},{1,13},{5,9},{9,5},{13,1},{2,14},{6,10},... | collective-permute-start | bytes 49160 | tf_op jit(solution)/shard_map/ppermute | solution.py:23
  21.3 4.6 %collective-permute-start.7 = (f32[16,256]{1,0:T(8,128)S(1)}, f32[16,256]{1,0:T(8,128)S(1)}, u32[]{:S(2)}, u32[]{:S(2)}) collective-permute-start(f32[16,256]{1,0:T(8,128)S(1)} %shard_map.108.part.refs_7_), channel_id=1, source_target_pairs={{0,8},{4,12},{8,0},{12,4},{1,9},{5,13},{9,1},{13,5},{2,10},{6,14},... | collective-permute-start | bytes 49160 | tf_op jit(solution)/shard_map/ppermute | solution.py:23
  21.6 4.4 %collective-permute-start.6 = (f32[16,256]{1,0:T(8,128)S(1)}, f32[16,256]{1,0:T(8,128)S(1)}, u32[]{:S(2)}, u32[]{:S(2)}) collective-permute-start(f32[16,256]{1,0:T(8,128)S(1)} %shard_map.108.part.refs_7_), channel_id=1, source_target_pairs={{0,4},{4,0},{8,12},{12,8},{1,5},{5,1},{9,13},{13,9},{2,6},{6,2},{1... | collective-permute-start | bytes 49160 | tf_op jit(solution)/shard_map/ppermute | solution.py:23
  27.4 3.5 %collective-permute-start.11 = (f32[24,256]{1,0:T(8,128)S(1)}, f32[24,256]{1,0:T(8,128)S(1)}, u32[]{:S(2)}, u32[]{:S(2)}) collective-permute-start(f32[24,256]{1,0:T(8,128)S(1)} %get-tuple-element.36.refs_6_), channel_id=1, source_target_pairs={{0,3},{1,2},{2,1},{3,0},{4,7},{5,6},{6,5},{7,4},{8,11},{9,10},{10,... | collective-permute-start | bytes 73736 | tf_op jit(solution)/shard_map/ppermute | solution.py:23
  27.4 3.9 %collective-permute-start.10 = (f32[24,256]{1,0:T(8,128)S(1)}, f32[24,256]{1,0:T(8,128)S(1)}, u32[]{:S(2)}, u32[]{:S(2)}) collective-permute-start(f32[24,256]{1,0:T(8,128)S(1)} %get-tuple-element.36.refs_6_), channel_id=1, source_target_pairs={{0,2},{1,3},{2,0},{3,1},{4,6},{5,7},{6,4},{7,5},{8,10},{9,11},{10,... | collective-permute-start | bytes 73736 | tf_op jit(solution)/shard_map/ppermute | solution.py:23
  28.9 2.4 %collective-permute-start.9 = (f32[24,256]{1,0:T(8,128)S(1)}, f32[24,256]{1,0:T(8,128)S(1)}, u32[]{:S(2)}, u32[]{:S(2)}) collective-permute-start(f32[24,256]{1,0:T(8,128)S(1)} %get-tuple-element.36.refs_6_), channel_id=1, source_target_pairs={{0,1},{1,0},{2,3},{3,2},{4,5},{5,4},{6,7},{7,6},{8,9},{9,8},{10,11... | collective-permute-start | bytes 73736 | tf_op jit(solution)/shard_map/ppermute | solution.py:23
  32.7 5.8 %collective-permute-start.14 = (f32[24,256]{1,0:T(8,128)S(1)}, f32[24,256]{1,0:T(8,128)S(1)}, u32[]{:S(2)}, u32[]{:S(2)}) collective-permute-start(f32[24,256]{1,0:T(8,128)S(1)} %get-tuple-element.38.refs_8_), channel_id=1, source_target_pairs={{0,12},{4,8},{8,4},{12,0},{1,13},{5,9},{9,5},{13,1},{2,14},{6,10},... | collective-permute-start | bytes 73736 | tf_op jit(solution)/shard_map/ppermute | solution.py:23
  34.7 5.0 %collective-permute-start.13 = (f32[24,256]{1,0:T(8,128)S(1)}, f32[24,256]{1,0:T(8,128)S(1)}, u32[]{:S(2)}, u32[]{:S(2)}) collective-permute-start(f32[24,256]{1,0:T(8,128)S(1)} %get-tuple-element.38.refs_8_), channel_id=1, source_target_pairs={{0,8},{4,12},{8,0},{12,4},{1,9},{5,13},{9,1},{13,5},{2,10},{6,14},... | collective-permute-start | bytes 73736 | tf_op jit(solution)/shard_map/ppermute | solution.py:23
  35.6 4.0 %collective-permute-start.12 = (f32[24,256]{1,0:T(8,128)S(1)}, f32[24,256]{1,0:T(8,128)S(1)}, u32[]{:S(2)}, u32[]{:S(2)}) collective-permute-start(f32[24,256]{1,0:T(8,128)S(1)} %get-tuple-element.38.refs_8_), channel_id=1, source_target_pairs={{0,4},{4,0},{8,12},{12,8},{1,5},{5,1},{9,13},{13,9},{2,6},{6,2},{1... | collective-permute-start | bytes 73736 | tf_op jit(solution)/shard_map/ppermute | solution.py:23
  41.2 3.5 %collective-permute-start.17 = (f32[24,256]{1,0:T(8,128)S(1)}, f32[24,256]{1,0:T(8,128)S(1)}, u32[]{:S(2)}, u32[]{:S(2)}) collective-permute-start(f32[24,256]{1,0:T(8,128)S(1)} %get-tuple-element.42.refs_8_), channel_id=1, source_target_pairs={{0,3},{1,2},{2,1},{3,0},{4,7},{5,6},{6,5},{7,4},{8,11},{9,10},{10,... | collective-permute-start | bytes 73736 | tf_op jit(solution)/shard_map/ppermute | solution.py:23
  41.2 3.9 %collective-permute-start.16 = (f32[24,256]{1,0:T(8,128)S(1)}, f32[24,256]{1,0:T(8,128)S(1)}, u32[]{:S(2)}, u32[]{:S(2)}) collective-permute-start(f32[24,256]{1,0:T(8,128)S(1)} %get-tuple-element.42.refs_8_), channel_id=1, source_target_pairs={{0,2},{1,3},{2,0},{3,1},{4,6},{5,7},{6,4},{7,5},{8,10},{9,11},{10,... | collective-permute-start | bytes 73736 | tf_op jit(solution)/shard_map/ppermute | solution.py:23
  42.7 2.4 %collective-permute-start.15 = (f32[24,256]{1,0:T(8,128)S(1)}, f32[24,256]{1,0:T(8,128)S(1)}, u32[]{:S(2)}, u32[]{:S(2)}) collective-permute-start(f32[24,256]{1,0:T(8,128)S(1)} %get-tuple-element.42.refs_8_), channel_id=1, source_target_pairs={{0,1},{1,0},{2,3},{3,2},{4,5},{5,4},{6,7},{7,6},{8,9},{9,8},{10,11... | collective-permute-start | bytes 73736 | tf_op jit(solution)/shard_map/ppermute | solution.py:23
  46.7 4.6 %collective-permute-start.18 = (f32[8,256]{1,0:T(8,128)S(1)}, f32[8,256]{1,0:T(8,128)S(1)}, u32[]{:S(2)}, u32[]{:S(2)}) collective-permute-start(f32[8,256]{1,0:T(8,128)S(1)} %get-tuple-element.45), channel_id=1, source_target_pairs={{0,8},{4,12},{8,0},{12,4},{1,9},{5,13},{9,1},{13,5},{2,10},{6,14},... | collective-permute-start | bytes 24584 | tf_op jit(solution)/shard_map/ppermute | solution.py:23
  48.4 5.4 %collective-permute-start.19 = (f32[8,256]{1,0:T(8,128)S(1)}, f32[8,256]{1,0:T(8,128)S(1)}, u32[]{:S(2)}, u32[]{:S(2)}) collective-permute-start(f32[8,256]{1,0:T(8,128)S(1)} %get-tuple-element.46), channel_id=1, source_target_pairs={{0,12},{4,8},{8,4},{12,0},{1,13},{5,9},{9,5},{13,1},{2,14},{6,10},... | collective-permute-start | bytes 24584 | tf_op jit(solution)/shard_map/ppermute | solution.py:23
  50.3 3.7 %collective-permute-start.20 = (f32[8,256]{1,0:T(8,128)S(1)}, f32[8,256]{1,0:T(8,128)S(1)}, u32[]{:S(2)}, u32[]{:S(2)}) collective-permute-start(f32[8,256]{1,0:T(8,128)S(1)} %get-tuple-element.47), channel_id=1, source_target_pairs={{0,4},{4,0},{8,12},{12,8},{1,5},{5,1},{9,13},{13,9},{2,6},{6,2},{1... | collective-permute-start | bytes 24584 | tf_op jit(solution)/shard_map/ppermute | solution.py:23
